TPU v7x, 256 devices: a whole 4x4x8 slice. The times are simulated.
256 devices in a mesh: ctx: 32 (over x, z), mp: 8 (over y, core).
Axes of the slice: x: 4, y: 4, z: 8, core: 2. Of those that a mesh axis runs over, the one named last changes fastest.
Arguments:
- gate_rows: bfloat16 [4096, 8192], P(('ctx', 'mp')), may hold values from -6 to 6
- key_rows: bfloat16 [4096, 8192], P(('ctx', 'mp')), may hold values from -6 to 6
- value_rows: bfloat16 [4096, 8192], P(('ctx', 'mp')), may hold values from -6 to 6
- out_grad: bfloat16 [4096, 8192], P(('ctx', 'mp')), may hold values from -12 to 12
- conv_taps: float32 [3, 3, 8192], P(None, None, 'mp'), may hold values from -3 to 3
- filter_residues: float32 [512, 16], P('mp'), may hold values from -3 to 3
- filter_poles: float32 [512, 16], P('mp'), may hold values from 0.96 to 1, as said below
- skip_gain: float32 [8192], P('mp'), may hold values from -3 to 3
- seq_lengths: int32 [8], replicated, may hold values from 1 to 2048, 4096 in all
- piece_list: int32 [32], replicated, may hold values from 0 to 31, each once
Outputs:
- mixed_out: bfloat16 [4096, 8192], P(('ctx', 'mp'))
- gate_grad: bfloat16 [4096, 8192], P(('ctx', 'mp'))
- key_grad: bfloat16 [4096, 8192], P(('ctx', 'mp'))
- value_grad: bfloat16 [4096, 8192], P(('ctx', 'mp'))
- taps_grad: float32 [3, 3, 8192], P(None, None, 'mp')
- skip_grad: float32 [8192], P('mp')
Inputs may be any that keep to these rules, and one draw needn't show every extreme that they name: `seq_lengths`: the genomes' lengths sum to 4096; the longest is exactly 2048. `piece_list`: each piece number appears once. `filter_poles`: poles are below 1.
All inputs are finite; a program needn't handle non-finite values.
Results may differ from a plain program's by a relative error of at most 0.00245.
Values may be sent and summed in bfloat16 or wider, within the bound.
No kernel may reach another device: no remote copies, remote signals or barrier semaphores. Data moves between devices by JAX's collectives and lax.ppermute only.
A program may use at most 128 MiB of HBM per device.

v0:
```python
import math

import jax
import jax.numpy as jnp
from jax import lax
from jax.sharding import PartitionSpec as P

GROUP = 16
MODES = 16
PIECE = 128
PIECES_DEV = 1


HIGHEST = lax.Precision.HIGHEST


def segment_of(row_ids, bounds):
    return jnp.sum((bounds <= row_ids[..., None]).astype(jnp.int32), axis=-1)


def starts_upto(piece_ids, begins, piece_len):
    limit = (piece_ids + 1) * piece_len
    return jnp.sum((begins < limit[..., None]).astype(jnp.int32), axis=-1)


def neighbour_mask(segs, inside, offset, piece_len):
    other = lax.slice_in_dim(segs, 2 + offset, 2 + offset + piece_len, axis=1)
    within = lax.slice_in_dim(inside, 2 + offset, 2 + offset + piece_len, axis=1)
    own = lax.slice_in_dim(segs, 2, 2 + piece_len, axis=1)
    return (within & (other == own)).astype(jnp.float32)


def carry_weights(dest, source, begins, log_decay, piece_len, forward):
    if forward:
        gap = dest[:, None] - source[None, :] - 1
        newer = dest[:, None] + 0 * source[None, :]
        older = source[None, :]
    else:
        gap = source[None, :] - dest[:, None] - 1
        newer = source[None, :]
        older = dest[:, None] + 0 * source[None, :]
    between = starts_upto(newer - 1, begins, piece_len) - starts_upto(older, begins, piece_len)
    usable = (gap >= 0) & (between == 0)
    lags = (piece_len * jnp.maximum(gap, 0)).astype(jnp.float32)
    power = jnp.exp(lags[:, :, None, None] * log_decay[None, None])
    return jnp.where(usable[:, :, None, None], power, 0.0)


def carry_mix(dest, source, piece_states, begins, log_decay, piece_len):
    groups = log_decay.shape[0]
    modes = log_decay.shape[1]
    width = piece_states.shape[-1]
    split = piece_states.reshape(source.shape[0], 2, modes, groups, width // groups)
    ahead_w = carry_weights(dest, source, begins, log_decay, piece_len, True)
    behind_w = carry_weights(dest, source, begins, log_decay, piece_len, False)
    ahead = jnp.einsum("ijgn,jngc->ingc", ahead_w, split[:, 0], precision=HIGHEST)
    behind = jnp.einsum("ijgn,jngc->ingc", behind_w, split[:, 1], precision=HIGHEST)
    return jnp.stack([ahead, behind], axis=1).reshape(dest.shape[0], 2, modes, width)


def local(
    gate_rows,
    key_rows,
    value_rows,
    out_grad,
    conv_taps,
    filter_residues,
    filter_poles,
    skip_gain,
    seq_lengths,
    piece_list,
):
    gate_local, key_local, value_local, grad_local = (
        lax.all_to_all(gate_rows, "mp", split_axis=1, concat_axis=0, tiled=True),
        lax.all_to_all(key_rows, "mp", split_axis=1, concat_axis=0, tiled=True),
        lax.all_to_all(value_rows, "mp", split_axis=1, concat_axis=0, tiled=True),
        lax.all_to_all(out_grad, "mp", split_axis=1, concat_axis=0, tiled=True),
    )
    tok_dev, width = gate_local.shape
    groups = width // GROUP
    ctx_size = lax.axis_size("ctx")
    total_rows = tok_dev * ctx_size
    count = PIECES_DEV
    plen = PIECE
    npieces = count * ctx_size
    here = lax.axis_index("ctx")
    my_ids = lax.dynamic_slice_in_dim(piece_list, here * count, count)
    slots = jnp.arange(npieces, dtype=jnp.int32)

    def slot_of(wanted):
        return jnp.sum(jnp.where(piece_list[None, :] == wanted[:, None], slots[None, :], 0), axis=1)

    bounds = jnp.cumsum(seq_lengths)
    begins = jnp.concatenate([jnp.zeros((1,), jnp.int32), bounds[:-1]])
    offsets = jnp.arange(-2, plen + 2, dtype=jnp.int32)
    row_ids = my_ids[:, None] * plen + offsets[None, :]
    inside = (row_ids >= 0) & (row_ids < total_rows)
    segs = segment_of(row_ids, bounds)
    seg_main = segs[:, 2 : plen + 2]
    early = [neighbour_mask(segs, inside, -1, plen), neighbour_mask(segs, inside, -2, plen)]
    later = [neighbour_mask(segs, inside, 1, plen), neighbour_mask(segs, inside, 2, plen)]
    fresh = 1.0 - early[0]
    seen = jnp.cumsum(fresh, axis=1)
    lead = (seen == 0).astype(jnp.float32)
    tail = (seen[:, -1:] - seen == 0).astype(jnp.float32)
    stacked = jnp.stack([gate_local, key_local, value_local], axis=1).reshape(count, plen, 3, width)
    tails = stacked[:, plen - 2 :]
    all_tails = lax.all_gather(tails, "ctx", axis=0, tiled=True)
    prior = all_tails[slot_of(my_ids - 1)]
    extended = jnp.concatenate([prior, stacked], axis=1)
    feats = extended[:, 2:].astype(jnp.float32) * conv_taps[None, None, :, 0, :]
    for delay in (1, 2):
        shifted = extended[:, 2 - delay : 2 - delay + plen].astype(jnp.float32)
        feats = (
            feats
            + shifted * conv_taps[None, None, :, delay, :] * early[delay - 1][:, :, None, None]
        )
    front = feats[:, :, 0]
    keyed = feats[:, :, 1]
    valued = feats[:, :, 2]
    mixed = keyed * valued
    upstream = grad_local.reshape(count, plen, width).astype(jnp.float32)
    grad_filtered = upstream * front
    log_decay = jnp.log(filter_poles)
    weight = filter_residues * jnp.sqrt(1.0 - filter_poles * filter_poles)
    steps = jnp.arange(plen, dtype=jnp.float32)
    powers = jnp.exp(log_decay[:, :, None] * steps)
    falling = jnp.exp(log_decay[:, :, None] * (plen - 1.0 - steps))
    rising = jnp.exp(log_decay[:, :, None] * (steps + 1.0))
    shrinking = jnp.exp(log_decay[:, :, None] * (plen - steps))
    kernel = jnp.einsum("gn,gnd->gd", weight, powers, precision=HIGHEST)
    grid = jnp.arange(plen, dtype=jnp.int32)
    lag = grid[:, None] - grid[None, :]
    toeplitz = jnp.where(lag[None] >= 0, kernel[:, jnp.clip(lag, 0, plen - 1)], 0.0)

    def local_piece(inputs):
        seg_row, mixed_piece, grad_piece = inputs
        same = (seg_row[:, None] == seg_row[None, :]).astype(jnp.float32)
        matrix = toeplitz * same[None]
        mixed_cols = mixed_piece.T.reshape(groups, GROUP, plen)
        grad_cols = grad_piece.T.reshape(groups, GROUP, plen)
        ahead_part = (
            jnp.einsum("gcs,gts->gct", mixed_cols, matrix, precision=HIGHEST).reshape(width, plen).T
        )
        behind_part = (
            jnp.einsum("gct,gts->gcs", grad_cols, matrix, precision=HIGHEST).reshape(width, plen).T
        )
        return (ahead_part, behind_part)

    filter_local, grad_mixed_local = lax.map(local_piece, (seg_main, mixed, grad_filtered))
    mixed_groups = mixed.reshape(count, plen, groups, GROUP)
    grad_groups = grad_filtered.reshape(count, plen, groups, GROUP)
    ends = jnp.einsum("gns,ps,psgc->pngc", falling, tail, mixed_groups, precision=HIGHEST)
    heads = jnp.einsum("gnt,pt,ptgc->pngc", powers, lead, grad_groups, precision=HIGHEST)
    states = jnp.stack([ends, heads], axis=1).reshape(count, 2, MODES, width)
    every = lax.all_gather(states, "ctx", axis=0, tiled=True)
    entering = carry_mix(my_ids, piece_list, every, begins, log_decay, plen)
    split_enter = entering.reshape(count, 2, MODES, groups, GROUP)
    filter_carry = jnp.einsum(
        "gn,gnt,pt,pngc->ptgc", weight, rising, lead, split_enter[:, 0], precision=HIGHEST
    ).reshape(count, plen, width)
    grad_carry = jnp.einsum(
        "gn,gns,ps,pngc->psgc", weight, shrinking, tail, split_enter[:, 1], precision=HIGHEST
    ).reshape(count, plen, width)
    filtered = filter_local + filter_carry + skip_gain * mixed
    output = (front * filtered).astype(jnp.bfloat16)
    grad_front = upstream * filtered
    grad_mixed = grad_mixed_local + grad_carry + skip_gain * grad_filtered
    grad_feats = jnp.stack([grad_front, grad_mixed * valued, grad_mixed * keyed], axis=2)
    head_rows = grad_feats[:, :2]
    all_heads = lax.all_gather(head_rows, "ctx", axis=0, tiled=True)
    after = all_heads[slot_of(my_ids + 1)]
    grad_extended = jnp.concatenate([grad_feats, after], axis=1)
    input_grads = grad_feats * conv_taps[None, None, :, 0, :]
    for delay in (1, 2):
        input_grads = (
            input_grads
            + grad_extended[:, delay : delay + plen]
            * conv_taps[None, None, :, delay, :]
            * later[delay - 1][:, :, None, None]
        )
    tap_terms = [jnp.sum(grad_feats * extended[:, 2:].astype(jnp.float32), axis=(0, 1))]
    for delay in (1, 2):
        shifted = extended[:, 2 - delay : 2 - delay + plen].astype(jnp.float32)
        tap_terms.append(
            jnp.sum(grad_feats * shifted * early[delay - 1][:, :, None, None], axis=(0, 1))
        )
    tap_local = jnp.stack(tap_terms, axis=1)
    skip_local = jnp.sum(grad_filtered * mixed, axis=(0, 1))
    tap_total, skip_total = lax.psum((tap_local, skip_local), "ctx")
    norm = 1.0 / math.sqrt(total_rows)
    input_bf = input_grads.astype(jnp.bfloat16)
    out_rows, gate_back, key_back, value_back = (
        lax.all_to_all(
            output.reshape(tok_dev, width), "mp", split_axis=0, concat_axis=1, tiled=True
        ),
        lax.all_to_all(
            input_bf[:, :, 0].reshape(tok_dev, width), "mp", split_axis=0, concat_axis=1, tiled=True
        ),
        lax.all_to_all(
            input_bf[:, :, 1].reshape(tok_dev, width), "mp", split_axis=0, concat_axis=1, tiled=True
        ),
        lax.all_to_all(
            input_bf[:, :, 2].reshape(tok_dev, width), "mp", split_axis=0, concat_axis=1, tiled=True
        ),
    )
    return (out_rows, gate_back, key_back, value_back, tap_total * norm, skip_total * norm)


def solution(mesh):
    return jax.shard_map(
        local,
        mesh=mesh,
        in_specs=(
            P(("ctx", "mp"), None),
            P(("ctx", "mp"), None),
            P(("ctx", "mp"), None),
            P(("ctx", "mp"), None),
            P(None, None, "mp"),
            P("mp", None),
            P("mp", None),
            P("mp"),
            P(),
            P(),
        ),
        out_specs=(
            P(("ctx", "mp"), None),
            P(("ctx", "mp"), None),
            P(("ctx", "mp"), None),
            P(("ctx", "mp"), None),
            P(None, None, "mp"),
            P("mp"),
        ),
        check_vma=False,
    )
```

profile of v0, /device:TPU:8, one launch (start us, length us, event | category | flops | bytes accessed | tf_op | source)
XLA Modules:
  0.0 490.8 jit_solution(13207246188331177079)
XLA Ops:
  7.2 1.7 copy.217
  8.9 5.6 %all-to-all-start = ((bf16[16,8,1024]{2,0,1:T(8,128)(2,1)}), bf16[16,8,1024]{2,0,1:T(8,128)(2,1)S(1)}, u32[]{:S(2)}, u32[]{:S(2)}) async-start(bf16[16,8,1024]{2,0,1:T(8,128)(2,1)} %bitcast.201), calls=%async_computation | async-start | bytes 524288 | tf_op jit(solution)/shard_map/all_to_all | solution.py:74
  14.6 1.2 dynamic_slice.11
  19.1 2.5 multiply_convert_fusion.1
  22.2 1.7 copy.216
  24.8 4.8 all-to-all-start.1
  29.6 1.2 fusion.69
  31.6 4.1 all-to-all-done.1
  35.7 4.8 all-to-all-start.2
  43.9 2.7 all-to-all-done.2
  46.6 4.8 all-to-all-start.3
  51.5 52.0 %all_gather.9 = bf16[32,2,3,1024]{3,1,2,0:T(2,128)(2,1)S(1)} all-gather(bf16[1,2,3,1024]{3,1,2,0:T(2,128)(2,1)S(1)} %slice.149), channel_id=1, replica_groups=mesh['ctx'=32,'mp'=8] {'ctx'}, dimensions={0}, use_global_device_ids=true | all-gather | bytes 405504 | tf_op jit(solution)/shard_map/all_gather | solution.py:108
  105.2 2.0 copy.160
  107.3 2.8 reshape.900
  110.0 3.7 copy.161
  113.8 2.9 fusion.42
  116.6 1.2 copy.163
  117.9 1.5 fusion.30
  119.4 1.2 copy.158
  120.7 1.0 fusion.45
  125.4 1.2 compare_and_fusion.2
  126.7 1.7 select_bitcast_fusion.1
  128.4 1.9 copy.197
  130.3 2.8 copy.198
  134.4 54.5 %gather_fusion = f32[16384,64]{1,0:T(8,128)} fusion(f32[64,128]{0,1:T(8,128)S(1)} %copy.179, s32[16384]{0:T(1024)S(1)} %fusion.62), kind=kCustom, calls=%fused_computation | custom fusion | bytes 8454144 | tf_op jit(solution)/shard_map/gather | solution.py:134
  188.8 7.4 %copy.156 = f32[128,128,64]{1,0,2:T(8,128)} copy(f32[128,128,64]{2,1,0:T(8,128)} %bitcast.204) | data formatting | bytes 8388608 | tf_op jit(solution)/shard_map/gather | solution.py:134
  199.8 8.4 %fusion.6 = f32[64,16,128]{2,1,0:T(8,128)S(1)} fusion(f32[64,16,128]{2,1,0:T(8,128)} %bitcast.226, f32[128,128,64]{1,0,2:T(8,128)} %copy.156, f32[128,128]{1,0:T(8,128)S(1)} %get-tuple-element.137, pred[128,128]{1,0:T(8,128)(4,1)} %get-tuple-element.136), kind=kOutput, calls=%fused_computation.9 | convolution fusion | flops 203423744 | bytes 5324800 | tf_op jit(solution)/shard_map/while/body/eval_jaxpr/gcs,gts->gct/dot_general | solution.py:143
  208.2 1.0 copy.157
  209.2 10.6 %copy.164 = f32[32,2,16,1024]{0,3,2,1:T(8,128)} copy(f32[32,2,16,1024]{3,2,1,0:T(8,128)} %all-gather.2.cloned.1.call-done) | data formatting | bytes 8388608 | tf_op jit(solution)/shard_map/all_gather | solution.py:156
  219.8 9.4 %fusion.1 = (f32[16,64,16]{2,1,0:T(8,128)}, f32[16,64,16]{2,1,0:T(8,128)}) fusion(f32[32,2,16,64,16]{0,4,3,2,1:T(8,128)} %bitcast.203, f32[16,64,32]{2,1,0:T(8,128)S(1)} %copy-done.7, f32[16,64,32]{2,1,0:T(8,128)S(1)} %copy.197), kind=kLoop, calls=%fused_computation.3 | loop fusion | flops 2064384 | bytes 4587520
  229.2 1.3 copy.185
  230.5 1.4 convolution_multiply_fusion.1
  231.9 1.1 copy.167
  232.9 2.4 bitcast_multiply_fusion.2
  236.3 6.8 %fusion.4 = f32[64,16,128]{2,1,0:T(8,128)} fusion(f32[64,16,128]{2,1,0:T(8,128)} %bitcast.225, f32[128,128,64]{1,0,2:T(8,128)} %copy.156, f32[128,128]{1,0:T(8,128)S(1)} %get-tuple-element.137, pred[128,128]{1,0:T(8,128)(4,1)} %get-tuple-element.136), kind=kOutput, calls=%fused_computation.7 | convolution fusion | flops 203423744 | bytes 5324800 | tf_op jit(solution)/shard_map/while/body/eval_jaxpr/gct,gts->gcs/dot_general | solution.py:146
  243.1 2.0 copy.170
  245.2 2.1 copy.191
  247.3 2.6 convolution_multiply_fusion
  249.9 2.0 copy.171
  251.9 1.4 fusion.33
  254.5 1.1 fusion.19
  255.6 48.8 %all_gather.11 = f32[32,2,3,1024]{3,1,2,0:T(2,128)S(1)} all-gather(f32[1,2,3,1024]{3,1,2,0:T(2,128)S(1)} %slice.162), channel_id=1, replica_groups=mesh['ctx'=32,'mp'=8] {'ctx'}, dimensions={0}, use_global_device_ids=true | all-gather | bytes 811008 | tf_op jit(solution)/shard_map/all_gather | solution.py:171
  306.5 10.7 %all_to_all.137 = bf16[8,16,1024]{2,1,0:T(8,128)(2,1)S(1)} all-to-all(bf16[8,16,1024]{2,1,0:T(8,128)(2,1)S(1)} %bitcast.233), channel_id=1, replica_groups=mesh['ctx'=32,'mp'=8] {'mp'}, dimensions={0} | all-to-all | bytes 524288 | tf_op jit(solution)/shard_map/all_to_all | solution.py:197
  317.2 9.9 %all_to_all.138 = bf16[8,16,1024]{2,1,0:T(8,128)(2,1)S(1)} all-to-all(bf16[8,16,1024]{2,1,0:T(8,128)(2,1)S(1)} %bitcast.232), channel_id=1, replica_groups=mesh['ctx'=32,'mp'=8] {'mp'}, dimensions={0} | all-to-all | bytes 524288 | tf_op jit(solution)/shard_map/all_to_all | solution.py:200
  327.1 4.8 all-to-all-start.7
  331.9 140.4 %all-reduce = (f32[3,3,1024]{2,0,1:T(4,128)S(1)}, f32[1024]{0:T(1024)S(1)}) all-reduce(f32[3,3,1024]{2,0,1:T(4,128)S(1)} %pad_maximum_fusion.5, f32[1024]{0:T(1024)S(1)} %copy-done.20), channel_id=1, replica_groups=mesh['ctx'=32,'mp'=8] {'ctx'}, use_global_device_ids=true, to_apply=%region_12.13 | all-reduce | flops 10240 | bytes 81920 | tf_op jit(solution)/shard_map/psum | solution.py:190
  472.3 4.8 all-to-all-start.4
  480.5 2.7 all-to-all-done.4
  (143 shorter events, 21.3 us)
Async XLA Ops:
  7.2 17.6 %copy-start.23 = (f32[64,16]{0,1:T(8,128)S(1)}, f32[64,16]{0,1:T(8,128)}, u32[]{:S(2)}) copy-start(f32[64,16]{0,1:T(8,128)} %param.15) | copy-start | bytes 12292
  7.2 17.6 %copy-start.24 = (f32[64,16]{0,1:T(8,128)S(1)}, f32[64,16]{0,1:T(8,128)}, u32[]{:S(2)}) copy-start(f32[64,16]{0,1:T(8,128)} %param.16) | copy-start | bytes 12292
  7.2 23.7 %copy-start.9 = (bf16[16,8192]{1,0:T(8,128)(2,1)S(1)}, bf16[16,8192]{1,0:T(8,128)(2,1)}, u32[]{:S(2)}) copy-start(bf16[16,8192]{1,0:T(8,128)(2,1)} %param.12) | copy-start | bytes 786436
  7.2 24.4 %copy-start.18 = (f32[3,3,1024]{2,1,0:T(4,128)S(1)}, f32[3,3,1024]{2,1,0:T(4,128)}, u32[]{:S(2)}) copy-start(f32[3,3,1024]{2,1,0:T(4,128)} %param.14) | copy-start | bytes 110596
  8.9 33.6 %copy-start.10 = (bf16[16,8192]{1,0:T(8,128)(2,1)S(1)}, bf16[16,8192]{1,0:T(8,128)(2,1)}, u32[]{:S(2)}) copy-start(bf16[16,8192]{1,0:T(8,128)(2,1)} %param.13) | copy-start | bytes 786436
  8.9 15.9 %all-to-all-start = ((bf16[16,8,1024]{2,0,1:T(8,128)(2,1)}), bf16[16,8,1024]{2,0,1:T(8,128)(2,1)S(1)}, u32[]{:S(2)}, u32[]{:S(2)}) async-start(bf16[16,8,1024]{2,0,1:T(8,128)(2,1)} %bitcast.201), calls=%async_computation | async-start | bytes 524288 | tf_op jit(solution)/shard_map/all_to_all | solution.py:74
  18.3 28.3 %copy-start.40 = (s32[8,1]{0,1:T(1,128)}, s32[8,1]{0,1:T(1,128)S(1)}, u32[]{:S(2)}) copy-start(s32[8,1]{0,1:T(1,128)S(1)} %reduce-window.4) | copy-start | bytes 100
  18.4 28.2 %copy-start.21 = (s32[132]{0:T(256)}, s32[132]{0:T(256)S(1)}, u32[]{:S(2)}) copy-start(s32[132]{0:T(256)S(1)} %convert_reduce_fusion) | copy-start | bytes 1588
  24.8 108.3 %copy-start.17 = (f32[64,16]{0,1:T(8,128)}, f32[64,16]{0,1:T(8,128)S(1)}, u32[]{:S(2)}) copy-start(f32[64,16]{0,1:T(8,128)S(1)} %get-tuple-element.118) | copy-start | bytes 12292
  24.8 78.7 %copy-start.1 = (bf16[16,8,1024]{2,0,1:T(8,128)(2,1)}, bf16[16,8,1024]{2,0,1:T(8,128)(2,1)S(1)}, u32[]{:S(2)}) copy-start(bf16[16,8,1024]{2,0,1:T(8,128)(2,1)S(1)} %all-to-all-done) | copy-start | bytes 786436
  24.8 10.9 %all-to-all-start.1 = ((bf16[16,8,1024]{2,0,1:T(8,128)(2,1)}), bf16[16,8,1024]{2,0,1:T(8,128)(2,1)S(1)}, u32[]{:S(2)}, u32[]{:S(2)}) async-start(bf16[16,8,1024]{2,0,1:T(8,128)(2,1)} %bitcast.200), calls=%async_computation.1 | async-start | bytes 524288 | tf_op jit(solution)/shard_map/all_to_all | solution.py:75
  30.9 82.9 %copy-start.27 = (f32[128]{0:T(128)}, f32[128]{0:T(128)S(1)}, u32[]{:S(2)}) copy-start(f32[128]{0:T(128)S(1)} %get-tuple-element.132) | copy-start | bytes 1540
  35.7 67.8 %copy-start.3 = (bf16[16,8,1024]{2,0,1:T(8,128)(2,1)}, bf16[16,8,1024]{2,0,1:T(8,128)(2,1)S(1)}, u32[]{:S(2)}) copy-start(bf16[16,8,1024]{2,0,1:T(8,128)(2,1)S(1)} %all-to-all-done.1) | copy-start | bytes 786436
  35.7 10.9 %all-to-all-start.2 = ((bf16[16,8,1024]{2,0,1:T(8,128)(2,1)}), bf16[16,8,1024]{2,0,1:T(8,128)(2,1)S(1)}, u32[]{:S(2)}, u32[]{:S(2)}) async-start(bf16[16,8,1024]{2,0,1:T(8,128)(2,1)} %bitcast.199), calls=%async_computation.2 | async-start | bytes 524288 | tf_op jit(solution)/shard_map/all_to_all | solution.py:76
  42.5 61.1 %copy-start.28 = (f32[128]{0:T(128)S(1)}, f32[128]{0:T(128)}, u32[]{:S(2)}) copy-start(f32[128]{0:T(128)} %get-tuple-element.122) | copy-start | bytes 1540
  42.5 61.1 %copy-start.30 = (f32[1,128]{1,0:T(1,128)S(1)}, f32[1,128]{1,0:T(1,128)}, u32[]{:S(2)}) copy-start(f32[1,128]{1,0:T(1,128)} %get-tuple-element.105) | copy-start | bytes 1540
  43.9 60.4 %copy-start.11 = (f32[3,1024]{1,0:T(4,128)}, f32[3,1024]{1,0:T(4,128)S(1)}, u32[]{:S(2)}) copy-start(f32[3,1024]{1,0:T(4,128)S(1)} %get-tuple-element.133) | copy-start | bytes 36868
  43.9 60.4 %copy-start.13 = (f32[3,1024]{1,0:T(4,128)}, f32[3,1024]{1,0:T(4,128)S(1)}, u32[]{:S(2)}) copy-start(f32[3,1024]{1,0:T(4,128)S(1)} %get-tuple-element.134) | copy-start | bytes 36868
  46.6 57.7 %copy-start.5 = (bf16[16,8,1024]{2,0,1:T(8,128)(2,1)}, bf16[16,8,1024]{2,0,1:T(8,128)(2,1)S(1)}, u32[]{:S(2)}) copy-start(bf16[16,8,1024]{2,0,1:T(8,128)(2,1)S(1)} %all-to-all-done.2) | copy-start | bytes 786436
  46.6 60.6 %all-to-all-start.3 = ((bf16[16,8,1024]{2,0,1:T(8,128)(2,1)}), bf16[16,8,1024]{2,0,1:T(8,128)(2,1)S(1)}, u32[]{:S(2)}, u32[]{:S(2)}) async-start(bf16[16,8,1024]{2,0,1:T(8,128)(2,1)} %bitcast.198), calls=%async_computation.3 | async-start | bytes 524288 | tf_op jit(solution)/shard_map/all_to_all | solution.py:77
  51.4 157.8 %all-gather.2.cloned.1.call-start = ((), (), s32[]{:S(2)}) async-start(), calls=%async_computation.8 | async-start | bytes 4325376 | tf_op jit(solution)/shard_map/all_gather | solution.py:156
  103.5 0.8 copy-start.15
  107.2 10.6 %copy-start = (bf16[16,8,1024]{2,0,1:T(8,128)(2,1)}, bf16[16,8,1024]{2,0,1:T(8,128)(2,1)S(1)}, u32[]{:S(2)}) copy-start(bf16[16,8,1024]{2,0,1:T(8,128)(2,1)S(1)} %all-to-all-done.3) | copy-start | bytes 786436
  117.8 2.8 copy-start.25
  117.8 2.8 copy-start.38
  119.4 6.0 %copy-start.36 = (s32[32]{0:T(128)S(1)}, s32[32]{0:T(128)}, u32[]{:S(2)}) copy-start(s32[32]{0:T(128)} %get-tuple-element.126) | copy-start | bytes 388
  119.4 6.0 %copy-start.37 = (s32[32]{0:T(128)S(1)}, s32[32]{0:T(128)}, u32[]{:S(2)}) copy-start(s32[32]{0:T(128)} %get-tuple-element.130) | copy-start | bytes 388
  119.4 7.3 %copy-start.34 = (f32[32]{0:T(128)S(1)}, f32[32]{0:T(128)}, u32[]{:S(2)}) copy-start(f32[32]{0:T(128)} %get-tuple-element.125) | copy-start | bytes 388
  119.4 7.3 %copy-start.35 = (f32[32]{0:T(128)S(1)}, f32[32]{0:T(128)}, u32[]{:S(2)}) copy-start(f32[32]{0:T(128)} %get-tuple-element.127) | copy-start | bytes 388
  188.8 9.2 %copy-start.22 = (s32[132]{0:T(256)S(1)}, s32[132]{0:T(256)}, u32[]{:S(2)}) copy-start(s32[132]{0:T(256)} %copy-done.21) | copy-start | bytes 1588
  209.2 10.6 %copy-start.7 = (f32[16,64,32]{2,1,0:T(8,128)S(1)}, f32[16,64,32]{2,1,0:T(8,128)}, u32[]{:S(2)}) copy-start(f32[16,64,32]{2,1,0:T(8,128)} %copy.198) | copy-start | bytes 393220
  243.1 4.2 copy-start.26
  243.1 4.2 copy-start.39
  245.2 6.7 %copy-start.19 = (f32[1024]{0:T(1024)S(1)}, f32[1024]{0:T(1024)}, u32[]{:S(2)}) copy-start(f32[1024]{0:T(1024)} %param.17) | copy-start | bytes 12292
  251.9 1.5 copy-start.8
  253.3 1.0 copy-start.2
  253.3 1.0 copy-start.4
  253.4 1.1 copy-start.6
  253.4 1.1 copy-start.16
  253.4 1.1 copy-start.29
  253.4 1.1 copy-start.31
  304.3 0.7 copy-start.12
  304.4 0.7 copy-start.14
  304.4 0.7 copy-start.32
  304.4 0.7 copy-start.33
  305.7 26.2 %copy-start.20 = (f32[1024]{0:T(1024)S(1)}, f32[1024]{0:T(1024)}, u32[]{:S(2)}) copy-start(f32[1024]{0:T(1024)} %get-tuple-element.96) | copy-start | bytes 12292
  327.1 145.2 %all-to-all-start.7 = ((bf16[8,16,1024]{2,1,0:T(8,128)(2,1)}), bf16[8,16,1024]{2,1,0:T(8,128)(2,1)S(1)}, u32[]{:S(2)}, u32[]{:S(2)}) async-start(bf16[8,16,1024]{2,1,0:T(8,128)(2,1)} %bitcast.79), calls=%async_computation.7 | async-start | bytes 524288 | tf_op jit(solution)/shard_map/all_to_all | solution.py:203
  472.3 10.9 %all-to-all-start.4 = ((bf16[8,16,1024]{2,1,0:T(8,128)(2,1)}), bf16[8,16,1024]{2,1,0:T(8,128)(2,1)S(1)}, u32[]{:S(2)}, u32[]{:S(2)}) async-start(bf16[8,16,1024]{2,1,0:T(8,128)(2,1)} %bitcast.54), calls=%async_computation.4 | async-start | bytes 524288 | tf_op jit(solution)/shard_map/all_to_all | solution.py:194
Sparse Core Ops, SparseCore 0:
  122.7 79.2 all-gather.1
where the time goes:
time: 494 us; the launch traced here: 491 us
  blocking collectives  262 us (53%)
  local copies, waits for them, and re-layouts  114 us (23%)
  other arithmetic  31.8 us (6%)
  starting transfers between devices  29.6 us (6%)
  matrix products  22.9 us (5%)
  between operations  20.8 us (4%)
  waiting for transfers between devices  9.47 us (2%)
    psum x1, blocking collectives, local(): tap_total, skip_total = lax.psum((tap_local, skip_local), 'ctx')  140 us
    gather x2, local copies, waits for them, and re-layouts, local(): kernel[:, jnp.clip(lag, 0, plen - 1)]  61.9 us
    all_gather x1, blocking collectives, local(): all_tails = lax.all_gather(tails, 'ctx', axis=0, tiled=True)  52 us
    all_gather x1, blocking collectives, local(): all_heads = lax.all_gather(head_rows, 'ctx', axis=0, tiled=True)  48.8 us
    unnamed x3, other arithmetic  11.4 us
    all_to_all x1, blocking collectives, local(): lax.all_to_all(input_bf[:, :, 0].reshape(tok_dev, width), 'mp', split_axi...  10.7 us
    all_gather x1, local copies, waits for them, and re-layouts, local(): every = lax.all_gather(states, 'ctx', axis=0, tiled=True)  10.6 us
    all_to_all x1, blocking collectives, local(): lax.all_to_all(input_bf[:, :, 1].reshape(tok_dev, width), 'mp', split_axi...  9.94 us
  transfers between devices with their start and end apart: 7, of which 3 were waited for; matrix products, arithmetic and copies ran while one was open for 21% of the time, Pallas kernels for 0%

commit v1 on v0

v1 whole, which is shorter than its diff:
```python
import math

import jax
import jax.numpy as jnp
from jax import lax
from jax.experimental import pallas as pl
from jax.experimental.pallas import tpu as pltpu
from jax.sharding import PartitionSpec as P

BOTH = ("ctx", "mp")
PIECE = 128
NPIECES = 32
NSEQ = 8
MODES = 16
OWN = 32
TOKENS = 4096
BASE = NPIECES * 16
VROWS = BASE + NSEQ * 16
F32 = jnp.float32
BF16 = jnp.bfloat16


def lane_ids(shape):
    return lax.broadcasted_iota(jnp.int32, shape, 1)


def swap_blocks(tiles):
    lane = lane_ids(tiles[0].shape)
    low = lane < 64
    even = (lane & 32) == 0
    a, b, c, d = tiles
    n0 = jnp.where(low, a, pltpu.roll(c, 64, 1))
    n2 = jnp.where(low, pltpu.roll(a, 64, 1), c)
    n1 = jnp.where(low, b, pltpu.roll(d, 64, 1))
    n3 = jnp.where(low, pltpu.roll(b, 64, 1), d)
    m0 = jnp.where(even, n0, pltpu.roll(n1, 32, 1))
    m1 = jnp.where(even, pltpu.roll(n0, 96, 1), n1)
    m2 = jnp.where(even, n2, pltpu.roll(n3, 32, 1))
    m3 = jnp.where(even, pltpu.roll(n2, 96, 1), n3)
    return m0, m1, m2, m3


def pack_kernel(a_ref, b_ref, c_ref, d_ref, o_ref):
    for j in range(8):
        for q in range(8):
            cols = slice(j * 1024 + q * 128, j * 1024 + (q + 1) * 128)
            tiles = [ref[:, cols].astype(F32) for ref in (a_ref, b_ref, c_ref, d_ref)]
            for k, tile in enumerate(swap_blocks(tiles)):
                o_ref[(4 * q + k) * 8 + j] = tile.astype(BF16)


def unpack_kernel(x_ref, a_ref, b_ref, c_ref, d_ref):
    for j in range(8):
        for q in range(8):
            cols = slice(j * 1024 + q * 128, j * 1024 + (q + 1) * 128)
            tiles = [x_ref[(4 * q + k) * 8 + j].astype(F32) for k in range(4)]
            for ref, tile in zip((a_ref, b_ref, c_ref, d_ref), swap_blocks(tiles)):
                ref[:, cols] = tile.astype(BF16)


def split(values):
    high = values.astype(BF16)
    return high, (values - high.astype(F32)).astype(BF16)


def dot3(left, right):
    def dot(a, b):
        return jnp.dot(a, b, preferred_element_type=F32)

    return dot(left[0], right[0]) + (dot(left[1], right[0]) + dot(left[0], right[1]))


(M_ONE, M_TWO, L_ONE, L_TWO, FIRST, TAIL, NOTBEG, NEXTCONT, WHOLE) = range(9)


def main_kernel(
    lens_ref, list_ref, here_ref, x_ref, taps_ref, res_ref, pole_ref, gain_ref,
    y_ref, g_ref,
    inv_ref, mask_ref, prep_ref, tapb_ref, gainb_ref,
    tf_ref, tb_ref, we_ref, wh_ref, wr_ref, ws_ref,
    xt_ref, feat_ref, z_ref, gu_ref,
    lzf_ref, lzt_ref, lgt_ref, lgf_ref,
    u_ref, gz_ref, e_ref, h_ref, roll_ref, acc_ref,
):
    here = here_ref[0]
    begins = [jnp.int32(0)]
    for k in range(NSEQ):
        begins.append(begins[-1] + lens_ref[k])

    def invert(s, carry):
        inv_ref[list_ref[s]] = s
        return carry

    lax.fori_loop(0, NPIECES, invert, 0)

    shape = (NPIECES, PIECE)
    base = lax.broadcasted_iota(jnp.int32, shape, 0) * PIECE
    row = base + lane_ids(shape)

    def count(ids, upto=NSEQ):
        total = jnp.zeros(shape, jnp.int32)
        for k in range(upto):
            total = total + (begins[k] <= ids).astype(jnp.int32)
        return total

    def starts(ids):
        hit = ids == begins[0]
        for k in range(1, NSEQ + 1):
            hit = hit | (ids == begins[k])
        return hit

    own = count(row)
    at_first, at_last, before = count(base), count(base + PIECE - 1), count(base - 1)
    here_start, prior_start = starts(row), starts(row - 1)
    next_start, after_start = starts(row + 1), starts(row + 2)
    one = jnp.ones(shape, F32)
    zero = jnp.zeros(shape, F32)
    mask_ref[M_ONE] = jnp.where(here_start, zero, one)
    mask_ref[M_TWO] = jnp.where(here_start | prior_start, zero, one)
    mask_ref[L_ONE] = jnp.where(next_start, zero, one)
    mask_ref[L_TWO] = jnp.where(next_start | after_start, zero, one)
    mask_ref[FIRST] = jnp.where(own == at_first, one, zero)
    mask_ref[TAIL] = jnp.where(own == at_last, one, zero)
    mask_ref[NOTBEG] = jnp.where(at_first == before, one, zero)
    mask_ref[NEXTCONT] = jnp.where(starts(base + PIECE), zero, one)
    mask_ref[WHOLE] = jnp.where(at_first == at_last, one, zero)

    block = pl.ds(pl.multiple_of((here // 4) * 128, 128), 128)
    shift = lax.rem(128 - 32 * lax.rem(here, 4), 128)
    prep_ref[...] = jnp.zeros((PIECE, PIECE), F32)
    for a in range(3):
        for j in range(3):
            prep_ref[a * 3 + j : a * 3 + j + 1, :] = taps_ref[a, j : j + 1, block]
    prep_ref[9:10, :] = gain_ref[0:1, block]
    prep_ref[0:16, :] = pltpu.roll(prep_ref[0:16, :], shift, 1)
    prep_ref[16:18, 0:MODES] = pole_ref[pl.ds(2 * here, 2), :]
    prep_ref[24:26, 0:MODES] = res_ref[pl.ds(2 * here, 2), :]
    turned = prep_ref[...].T

    def column(rows, at):
        return jnp.broadcast_to(turned[0:rows, at : at + 1], (rows, PIECE))

    for j in range(3):
        for a in range(3):
            tapb_ref[j, a * OWN : (a + 1) * OWN, :] = column(OWN, a * 3 + j)
    gainb_ref[...] = column(OWN, 9)
    pole = jnp.concatenate([column(MODES, 16), column(MODES, 17)], axis=0)
    residue = jnp.concatenate([column(MODES, 24), column(MODES, 25)], axis=0)
    weight = residue * jnp.sqrt(1.0 - pole * pole)
    lane = lane_ids((2 * MODES, PIECE))
    powers = jnp.ones((2 * MODES, PIECE), F32)
    falling = powers
    square = pole
    for bit in range(7):
        up = ((lane >> bit) & 1) == 1
        powers = jnp.where(up, powers * square, powers)
        falling = jnp.where(up, falling, falling * square)
        square = square * square
    rising = weight * (powers * pole)
    shrinking = weight * (falling * pole)
    taper = weight * powers

    sub_ids = lax.broadcasted_iota(jnp.int32, (PIECE, PIECE), 0)
    col_ids = lane_ids((PIECE, PIECE))
    tf_ref[...] = jnp.zeros(tf_ref.shape, BF16)
    tb_ref[...] = jnp.zeros(tb_ref.shape, BF16)
    wr_ref[...] = jnp.zeros(wr_ref.shape, BF16)
    ws_ref[...] = jnp.zeros(ws_ref.shape, BF16)
    for g in range(2):
        line = jnp.sum(taper[g * MODES : (g + 1) * MODES], axis=0, keepdims=True)
        spread = pltpu.roll(
            jnp.broadcast_to(line, (PIECE, PIECE)), 0, 1, stride=1, stride_axis=0
        )
        toeplitz = jnp.where(col_ids >= sub_ids, spread, 0.0)
        at = slice(g * PIECE, (g + 1) * PIECE)
        for part, tile in enumerate(split(toeplitz)):
            tf_ref[part, at, at] = tile
        for part, tile in enumerate(split(toeplitz.T)):
            tb_ref[part, at, at] = tile
        for ref, source in ((wr_ref, rising), (ws_ref, shrinking)):
            high, low = split(source[g * MODES : (g + 1) * MODES])
            ref[g * MODES : (g + 1) * MODES, at] = high
            ref[32 + g * MODES : 32 + (g + 1) * MODES, at] = high
            ref[64 + g * MODES : 64 + (g + 1) * MODES, at] = low
    blank = jnp.zeros((32, PIECE), F32)
    fall_cols = jnp.concatenate([falling, falling, falling, blank], axis=0).T
    power_cols = jnp.concatenate([powers, powers, powers, blank], axis=0).T
    group_zero = (col_ids & 16) == 0
    for ref, cols in ((we_ref, fall_cols), (wh_ref, power_cols)):
        for part, tile in enumerate(split(cols)):
            wide = tile.astype(F32)
            ref[part, 0:PIECE, :] = jnp.where(group_zero, wide, 0.0).astype(BF16)
            ref[part, PIECE:, :] = jnp.where(group_zero, 0.0, wide).astype(BF16)
    leap = fall_cols[0:1, :] * fall_cols[126:127, :]

    def store_lhs(ref, at, values):
        for part, tile in enumerate(split(values)):
            ref[part, pl.ds(at, 16), 0:PIECE] = tile[0:16]
            ref[part, pl.ds(at, 16), PIECE:] = tile[16:32]

    edge = lane_ids((96, PIECE))
    roll_ref[...] = jnp.zeros(roll_ref.shape, F32)
    acc_ref[...] = jnp.zeros(acc_ref.shape, F32)

    def ahead(p, carry):
        slot = inv_ref[p]
        tile = x_ref[pl.ds(slot * 8, 8)].reshape(PIECE, PIECE).astype(F32).T
        xt_ref[p] = tile
        x = tile[0:96]
        back_one = pltpu.roll(x, 1, 1)
        back_two = pltpu.roll(x, 2, 1)
        x_one = jnp.where(edge < 1, roll_ref[0], back_one)
        x_two = jnp.where(edge < 2, roll_ref[1], back_two)
        roll_ref[0] = back_one
        roll_ref[1] = back_two
        feats = (
            tapb_ref[0] * x
            + mask_ref[M_ONE, pl.ds(p, 1), :] * (tapb_ref[1] * x_one)
            + mask_ref[M_TWO, pl.ds(p, 1), :] * (tapb_ref[2] * x_two)
        )
        feat_ref[p] = feats
        z = feats[32:64] * feats[64:96]
        gu = tile[96:128] * feats[0:32]
        z_ref[p] = z
        gu_ref[p] = gu
        acc_ref[0, 96:128, :] += gu * z
        first = mask_ref[FIRST, pl.ds(p, 1), :]
        tail = mask_ref[TAIL, pl.ds(p, 1), :]
        at = pl.multiple_of(p * 16, 16)
        store_lhs(lzf_ref, at, z * first)
        store_lhs(lzt_ref, at, z * tail)
        store_lhs(lgt_ref, at, gu * tail)
        store_lhs(lgf_ref, at, gu * first)
        return carry

    lax.fori_loop(0, NPIECES, ahead, 0, unroll=2)

    line = lane_ids((1, PIECE))
    extras = []
    for k in range(1, NSEQ):
        p = begins[k] // PIECE
        rows = p * PIECE + line
        inner = lax.rem(begins[k], PIECE) != 0
        later = (rows >= begins[k]) & (rows < begins[k + 1]) & inner
        sooner = (rows >= begins[k - 1]) & (rows < begins[k]) & inner
        later = jnp.where(later, 1.0, 0.0)
        sooner = jnp.where(sooner, 1.0, 0.0)
        extras.append((p, later, sooner))
        store_lhs(lzf_ref, BASE + (k - 1) * 16, z_ref[p] * later)
        store_lhs(lgt_ref, BASE + (k - 1) * 16, gu_ref[p] * sooner)
    none = jnp.zeros((OWN, PIECE), F32)
    store_lhs(lzf_ref, VROWS - 16, none)
    store_lhs(lgt_ref, VROWS - 16, none)

    def both(ref):
        return ref[0], ref[1]

    e_ref[...] = dot3(both(lzt_ref), both(we_ref))
    h_ref[...] = dot3(both(lgf_ref), both(wh_ref))

    def scan(step, carry):
        state, back = carry
        p = step
        at = pl.ds(pl.multiple_of(p * 16, 16), 16)
        found = e_ref[at, :]
        state = state * mask_ref[NOTBEG, pl.ds(p, 1), :]
        e_ref[at, :] = state
        state = found + (mask_ref[WHOLE, pl.ds(p, 1), :] * leap) * state
        p = NPIECES - 1 - step
        at = pl.ds(pl.multiple_of(p * 16, 16), 16)
        found = h_ref[at, :]
        back = back * mask_ref[NEXTCONT, pl.ds(p, 1), :]
        h_ref[at, :] = back
        back = found + (mask_ref[WHOLE, pl.ds(p, 1), :] * leap) * back
        return state, back

    idle = jnp.zeros((16, PIECE), F32)
    lax.fori_loop(0, NPIECES, scan, (idle, idle), unroll=4)

    def three(states):
        high = states.astype(BF16).astype(F32)
        lane = lane_ids(states.shape)
        low = (lane >= 32) & (lane < 64)
        return jnp.where(low, states - high, high).astype(BF16)

    u_ref[...] = dot3(both(lzf_ref), both(tf_ref))
    gz_ref[...] = dot3(both(lgt_ref), both(tb_ref))
    u_ref[0:BASE, :] += jnp.dot(three(e_ref[...]), wr_ref[...], preferred_element_type=F32)
    gz_ref[0:BASE, :] += jnp.dot(three(h_ref[...]), ws_ref[...], preferred_element_type=F32)
    for k, (p, later, sooner) in enumerate(extras):
        at = pl.ds(pl.multiple_of(p * 16, 16), 16)
        more = slice(BASE + k * 16, BASE + (k + 1) * 16)
        for ref, mask in ((u_ref, later), (gz_ref, sooner)):
            for half in (slice(0, PIECE), slice(PIECE, 2 * PIECE)):
                ref[at, half] = jnp.where(mask > 0.0, ref[more, half], ref[at, half])

    roll_ref[...] = jnp.zeros(roll_ref.shape, F32)

    def behind(step, carry):
        p = NPIECES - 1 - step
        slot = inv_ref[p]
        at = pl.ds(pl.multiple_of(p * 16, 16), 16)
        u = jnp.concatenate([u_ref[at, 0:PIECE], u_ref[at, PIECE:]], axis=0)
        gz = jnp.concatenate([gz_ref[at, 0:PIECE], gz_ref[at, PIECE:]], axis=0)
        gain = gainb_ref[...]
        filtered = u + gain * z_ref[p]
        out = feat_ref[p, 0:32, :] * filtered
        grad_front = xt_ref[p, 96:128, :] * filtered
        gz = gz + gain * gu_ref[p]
        grads = jnp.concatenate(
            [grad_front, gz * feat_ref[p, 64:96, :], gz * feat_ref[p, 32:64, :]], axis=0
        )
        next_one = pltpu.roll(grads, PIECE - 1, 1)
        next_two = pltpu.roll(grads, PIECE - 2, 1)
        g_one = mask_ref[L_ONE, pl.ds(p, 1), :] * jnp.where(
            edge >= PIECE - 1, roll_ref[0], next_one
        )
        g_two = mask_ref[L_TWO, pl.ds(p, 1), :] * jnp.where(
            edge >= PIECE - 2, roll_ref[1], next_two
        )
        roll_ref[0] = next_one
        roll_ref[1] = next_two
        back = tapb_ref[0] * grads + tapb_ref[1] * g_one + tapb_ref[2] * g_two
        x = xt_ref[p, 0:96, :]
        acc_ref[0, 0:96, :] += grads * x
        acc_ref[1, 0:96, :] += g_one * x
        acc_ref[2, 0:96, :] += g_two * x
        tile = jnp.concatenate([out, back], axis=0).T.astype(BF16)
        y_ref[pl.ds(slot * 8, 8)] = tile.reshape(8, 16, PIECE)
        return carry

    lax.fori_loop(0, NPIECES, behind, 0, unroll=2)
    norm = 1.0 / math.sqrt(TOKENS)
    g_ref[...] = jnp.zeros(g_ref.shape, F32)
    for j in range(3):
        g_ref[j : j + 1, :] = norm * jnp.sum(acc_ref[j].T, axis=0, keepdims=True)


def vmem_params():
    return pltpu.CompilerParams(vmem_limit_bytes=48 * 1024 * 1024)


VM = pl.BlockSpec(memory_space=pltpu.VMEM)
SM = pl.BlockSpec(memory_space=pltpu.SMEM)


def run_pack(*arrays):
    return pl.pallas_call(
        pack_kernel,
        out_shape=jax.ShapeDtypeStruct((256, 16, 128), BF16),
        in_specs=[VM] * 4,
        out_specs=VM,
        compiler_params=vmem_params(),
        name="pack",
    )(*arrays)


def run_unpack(blocks):
    return pl.pallas_call(
        unpack_kernel,
        out_shape=[jax.ShapeDtypeStruct((16, 8192), BF16)] * 4,
        in_specs=[VM],
        out_specs=[VM] * 4,
        compiler_params=vmem_params(),
        name="unpack",
    )(blocks)


def run_main(lens, pieces, here, blocks, taps, residues, poles, gain):
    scratch = [
        pltpu.SMEM((NPIECES,), jnp.int32),
        pltpu.VMEM((9, NPIECES, PIECE), F32),
        pltpu.VMEM((PIECE, PIECE), F32),
        pltpu.VMEM((3, 96, PIECE), F32),
        pltpu.VMEM((OWN, PIECE), F32),
        pltpu.VMEM((2, 256, 256), BF16),
        pltpu.VMEM((2, 256, 256), BF16),
        pltpu.VMEM((2, 256, PIECE), BF16),
        pltpu.VMEM((2, 256, PIECE), BF16),
        pltpu.VMEM((PIECE, 256), BF16),
        pltpu.VMEM((PIECE, 256), BF16),
        pltpu.VMEM((NPIECES, PIECE, PIECE), F32),
        pltpu.VMEM((NPIECES, 96, PIECE), F32),
        pltpu.VMEM((NPIECES, OWN, PIECE), F32),
        pltpu.VMEM((NPIECES, OWN, PIECE), F32),
        pltpu.VMEM((2, VROWS, 256), BF16),
        pltpu.VMEM((2, BASE, 256), BF16),
        pltpu.VMEM((2, VROWS, 256), BF16),
        pltpu.VMEM((2, BASE, 256), BF16),
        pltpu.VMEM((VROWS, 256), F32),
        pltpu.VMEM((VROWS, 256), F32),
        pltpu.VMEM((BASE, PIECE), F32),
        pltpu.VMEM((BASE, PIECE), F32),
        pltpu.VMEM((2, 96, PIECE), F32),
        pltpu.VMEM((3, PIECE, PIECE), F32),
    ]
    return pl.pallas_call(
        main_kernel,
        out_shape=[
            jax.ShapeDtypeStruct((256, 16, 128), BF16),
            jax.ShapeDtypeStruct((8, 128), F32),
        ],
        in_specs=[SM, SM, SM, VM, VM, VM, VM, VM],
        out_specs=[VM, VM],
        scratch_shapes=scratch,
        compiler_params=vmem_params(),
        name="block",
    )(lens, pieces, here, blocks, taps, residues, poles, gain)


def exchange(blocks):
    return lax.all_to_all(blocks, BOTH, split_axis=0, concat_axis=0, tiled=True)


def local(
    gate_rows,
    key_rows,
    value_rows,
    out_grad,
    conv_taps,
    filter_residues,
    filter_poles,
    skip_gain,
    seq_lengths,
    piece_list,
):
    here = lax.axis_index("ctx").astype(jnp.int32).reshape(1)
    blocks = exchange(run_pack(gate_rows, key_rows, value_rows, out_grad))
    results, sums = run_main(
        seq_lengths,
        piece_list,
        here,
        blocks,
        conv_taps,
        filter_residues,
        filter_poles,
        skip_gain.reshape(1, -1),
    )
    every = lax.all_gather(sums, "ctx", axis=0, tiled=False)
    out_rows, gate_back, key_back, value_back = run_unpack(exchange(results))
    tap_total = every[:, 0:3, 0:96].reshape(32, 3, 3, OWN).transpose(2, 1, 0, 3)
    skip_total = every[:, 0, 96:128].reshape(1024)
    return (
        out_rows,
        gate_back,
        key_back,
        value_back,
        tap_total.reshape(3, 3, 1024),
        skip_total,
    )


def solution(mesh):
    rows = P(BOTH, None)
    return jax.shard_map(
        local,
        mesh=mesh,
        in_specs=(
            rows, rows, rows, rows,
            P(None, None, "mp"), P("mp", None), P("mp", None), P("mp"), P(), P(),
        ),
        out_specs=(rows, rows, rows, rows, P(None, None, "mp"), P("mp")),
        check_vma=False,
    )
```

time: 494 us -> 140 us (0.28)
  blocking collectives: 262 us -> 60.1 us
  local copies, waits for them, and re-layouts: 114 us -> 6.31 us
  other arithmetic: 31.8 us -> 0 us
  matrix products: 22.9 us -> 0 us
  waiting for transfers between devices: 9.47 us -> 31 us
  Pallas kernels: 0 us -> 20.8 us
  between operations: 20.8 us -> 0.73 us
  starting transfers between devices: 29.6 us -> 20.8 us
    psum x1 -> x0, blocking collectives: 140 us -> none  [local(): tap_total, skip_total = lax.psum((tap_local, skip_local), 'ctx')]
    gather x4 -> x0, local copies, waits for them, and re-layouts: 61.9 us -> none  [the longest x2 61.9 us: local(): kernel[:, jnp.clip(lag, 0, plen - 1)]]
    all_gather x2 -> x1, blocking collectives: 101 us -> 60.1 us  [local(): every = lax.all_gather(sums, 'ctx', axis=0, tiled=False)]
    dot_general x6 -> x0, matrix products: 22.9 us -> none  [the longest x1 8.39 us: local_piece(): jnp.einsum('gcs,gts->gct', mixed_cols, matrix, precision=HIGHEST)]
    all_to_all x6 -> x2, waiting for transfers between devices: 9.46 us -> 31 us  [exchange(): return lax.all_to_all(blocks, BOTH, split_axis=0, concat_axis=0, tiled=True)]
    pallas_call x0 -> x3, Pallas kernels: none -> 20.8 us  [the longest x1 10.6 us: run_main(): pl.pallas_call(main_kernel, out_shape=[jax.ShapeDtypeStruct((256, 16, 128...]
    all_to_all x2 -> x0, blocking collectives: 20.6 us -> none  [the longest x1 10.7 us: local(): lax.all_to_all(input_bf[:, :, 0].reshape(tok_dev, width), 'mp', split_axi...]
    unnamed x3 -> x0, other arithmetic: 11.4 us -> none
  transfers between devices with their start and end apart: 7 -> 2, of which waited for: 3 -> 1; matrix products, arithmetic and copies ran while one was open for 21% -> 1% of each run, Pallas kernels for 0% -> 0%
where the time goes in v1:
time: 140 us
  blocking collectives  60.1 us (43%)
  waiting for transfers between devices  31 us (22%)
  Pallas kernels  20.8 us (15%)
  starting transfers between devices  20.8 us (15%)
  local copies, waits for them, and re-layouts  6.31 us (5%)
    all_gather x1, blocking collectives, local(): every = lax.all_gather(sums, 'ctx', axis=0, tiled=False)  60.1 us
    all_to_all x2, waiting for transfers between devices, exchange(): return lax.all_to_all(blocks, BOTH, split_axis=0, concat_axis=0, tiled=True)  31 us
    all_to_all x2, starting transfers between devices, exchange(): return lax.all_to_all(blocks, BOTH, split_axis=0, concat_axis=0, tiled=True)  20.8 us
    pallas_call x1, Pallas kernels, run_main(): pl.pallas_call(main_kernel, out_shape=[jax.ShapeDtypeStruct((256, 16, 128...  10.6 us
    pallas_call x1, Pallas kernels, run_pack(): pl.pallas_call(pack_kernel, out_shape=jax.ShapeDtypeStruct((256, 16, 128)...  5.13 us
    pallas_call x1, Pallas kernels, run_unpack(): pl.pallas_call(unpack_kernel, out_shape=[jax.ShapeDtypeStruct((16, 8192),...  5.11 us
    unnamed x23, local copies, waits for them, and re-layouts  4.64 us
  transfers between devices with their start and end apart: 2, of which 1 were waited for; matrix products, arithmetic and copies ran while one was open for 1% of the time, Pallas kernels for 0%

profile of v1, /device:TPU:8, one launch (start us, length us, event | category | flops | bytes accessed | tf_op | source)
XLA Modules:
  0.0 139.8 jit_solution(6839299718024834751)
XLA Ops:
  0.6 0.0 copy-start
  0.6 0.9 copy-done
  1.6 0.0 copy-start.1
  1.6 0.9 copy-done.1
  2.5 0.0 copy-start.2
  2.5 0.9 copy-done.2
  3.5 0.0 copy-start.3
  3.5 0.9 copy-done.3
  4.4 5.1 %pack.1 = bf16[256,16,128]{2,1,0:T(8,128)(2,1)} custom-call(bf16[16,8192]{1,0:T(8,128)(2,1)S(1)} %copy-done, bf16[16,8192]{1,0:T(8,128)(2,1)S(1)} %copy-done.1, bf16[16,8192]{1,0:T(8,128)(2,1)S(1)} %copy-done.2, bf16[16,8192]{1,0:T(8,128)(2,1)S(1)} %copy-done.3), custom_call_target="tpu_custom_call" | custom-call | tf_op jit(solution)/shard_map/pack/pallas_call | solution.py:348
  9.6 0.0 copy-start.8
  9.6 0.0 copy-start.9
  9.6 14.6 %all-to-all-start = ((bf16[256,16,128]{2,1,0:T(8,128)(2,1)}), bf16[256,16,128]{2,1,0:T(8,128)(2,1)S(1)}, u32[]{:S(2)}, u32[]{:S(2)}) async-start(bf16[256,16,128]{2,1,0:T(8,128)(2,1)} %pack.1), calls=%async_computation | async-start | bytes 2097152 | tf_op jit(solution)/shard_map/all_to_all | solution.py:412
  24.2 0.0 copy-start.4
  24.2 0.0 copy-done.8
  24.2 0.1 copy.22.res_ref
  24.3 0.0 copy-done.9
  24.3 0.1 copy.23.pole_ref
  24.4 0.0 copy-start.5
  24.4 31.0 %all-to-all-done.x_ref = bf16[256,16,128]{2,1,0:T(8,128)(2,1)S(1)} async-done(((bf16[256,16,128]{2,1,0:T(8,128)(2,1)}), bf16[256,16,128]{2,1,0:T(8,128)(2,1)S(1)}, u32[]{:S(2)}, u32[]{:S(2)}) %all-to-all-start) | async-done | bytes 1048608 | tf_op jit(solution)/shard_map/all_to_all | solution.py:412
  55.4 0.0 copy-start.6
  55.4 0.0 copy-start.7
  55.4 0.0 copy-done.4
  55.4 0.0 copy-done.5
  55.4 0.6 copy-done.6
  56.0 0.0 copy-done.7
  56.0 10.6 %block.1 = (bf16[256,16,128]{2,1,0:T(8,128)(2,1)}, f32[8,128]{1,0:T(8,128)S(1)}) custom-call(s32[8]{0:T(128)S(1)} %copy-done.6, s32[32]{0:T(128)S(1)} %copy-done.7, s32[1]{0:T(128)} %bitcast.here_ref, bf16[256,16,128]{2,1,0:T(8,128)(2,1)S(1)} %all-to-all-done.x_ref, f32[3,3,1024]{2,1,0:T(4,128)S(1)} %copy-done.4, f32[64,16]{1,0:T(8,128)S(1)} %copy.22.res_ref, ...), custom_call_target="tpu_custom_call" | custom-call | tf_op jit(solution)/shard_map/block/pallas_call | solution.py:397
  66.6 6.2 %all-to-all-start.1 = ((bf16[256,16,128]{2,1,0:T(8,128)(2,1)}), bf16[256,16,128]{2,1,0:T(8,128)(2,1)S(1)}, u32[]{:S(2)}, u32[]{:S(2)}) async-start(bf16[256,16,128]{2,1,0:T(8,128)(2,1)} %get-tuple-element.12), calls=%async_computation.1 | async-start | bytes 2097152 | tf_op jit(solution)/shard_map/all_to_all | solution.py:412
  72.8 60.1 %all-gather = f32[256,128]{1,0:T(8,128)S(1)} all-gather(f32[8,128]{1,0:T(8,128)S(1)} %get-tuple-element.17), channel_id=2, replica_groups=mesh['ctx'=32,'mp'=8] {'ctx'}, dimensions={0}, use_global_device_ids=true | all-gather | bytes 135168 | tf_op jit(solution)/shard_map/all_gather | solution.py:439
  133.0 0.1 reshape.26
  133.1 0.7 reshape.27
  133.9 0.1 slice_reduce_fusion
  134.0 0.7 reshape_squeeze.3
  134.6 0.0 all-to-all-done.1.x_ref
  134.7 5.1 %unpack.1 = (bf16[16,8192]{1,0:T(8,128)(2,1)}, bf16[16,8192]{1,0:T(8,128)(2,1)}, bf16[16,8192]{1,0:T(8,128)(2,1)}, bf16[16,8192]{1,0:T(8,128)(2,1)}) custom-call(bf16[256,16,128]{2,1,0:T(8,128)(2,1)S(1)} %all-to-all-done.1.x_ref), custom_call_target="tpu_custom_call" | custom-call | tf_op jit(solution)/shard_map/unpack/pallas_call | solution.py:359
  (3 shorter events, 0.0 us)
Async XLA Ops:
  0.6 1.0 copy-start
  1.6 0.9 copy-start.1
  2.5 0.9 copy-start.2
  3.5 0.9 copy-start.3
  9.6 14.6 %copy-start.8 = (f32[64,16]{0,1:T(8,128)S(1)}, f32[64,16]{0,1:T(8,128)}, u32[]{:S(2)}) copy-start(f32[64,16]{0,1:T(8,128)} %param.15) | copy-start | bytes 12292
  9.6 14.7 %copy-start.9 = (f32[64,16]{0,1:T(8,128)S(1)}, f32[64,16]{0,1:T(8,128)}, u32[]{:S(2)}) copy-start(f32[64,16]{0,1:T(8,128)} %param.16) | copy-start | bytes 12292
  9.6 45.8 %all-to-all-start = ((bf16[256,16,128]{2,1,0:T(8,128)(2,1)}), bf16[256,16,128]{2,1,0:T(8,128)(2,1)S(1)}, u32[]{:S(2)}, u32[]{:S(2)}) async-start(bf16[256,16,128]{2,1,0:T(8,128)(2,1)} %pack.1), calls=%async_computation | async-start | bytes 2097152 | tf_op jit(solution)/shard_map/all_to_all | solution.py:412
  24.2 31.2 %copy-start.4 = (f32[3,3,1024]{2,1,0:T(4,128)S(1)}, f32[3,3,1024]{2,1,0:T(4,128)}, u32[]{:S(2)}) copy-start(f32[3,3,1024]{2,1,0:T(4,128)} %taps_ref.1) | copy-start | bytes 110596
  24.4 31.0 %copy-start.5 = (f32[1024]{0:T(1024)S(1)}, f32[1024]{0:T(1024)}, u32[]{:S(2)}) copy-start(f32[1024]{0:T(1024)} %param.17) | copy-start | bytes 12292
  55.4 0.7 copy-start.6
  55.4 0.7 copy-start.7
  66.6 68.0 %all-to-all-start.1 = ((bf16[256,16,128]{2,1,0:T(8,128)(2,1)}), bf16[256,16,128]{2,1,0:T(8,128)(2,1)S(1)}, u32[]{:S(2)}, u32[]{:S(2)}) async-start(bf16[256,16,128]{2,1,0:T(8,128)(2,1)} %get-tuple-element.12), calls=%async_computation.1 | async-start | bytes 2097152 | tf_op jit(solution)/shard_map/all_to_all | solution.py:412

commit v2 on v1

v2 whole, which is shorter than its diff:
```python
import math

import jax
import jax.numpy as jnp
from jax import lax
from jax.experimental import pallas as pl
from jax.experimental.pallas import tpu as pltpu
from jax.sharding import PartitionSpec as P

BOTH = ("ctx", "mp")
PIECE = 128
NPIECES = 32
NSEQ = 8
MODES = 16
OWN = 32
TOKENS = 4096
BASE = NPIECES * 16
VROWS = BASE + NSEQ * 16
PARTS = 4
PART = 8192 // PARTS
CHUNK = 8
F32 = jnp.float32
BF16 = jnp.bfloat16


def lane_ids(shape):
    return lax.broadcasted_iota(jnp.int32, shape, 1)


def block_ids():
    return lane_ids((16, PIECE)) // OWN


def pack_kernel(a_ref, b_ref, c_ref, d_ref, o_ref, stage_ref, sem):
    refs = (a_ref, b_ref, c_ref, d_ref)

    def copy(a, part):
        cols = pl.ds(part * PART, PART)
        return pltpu.make_async_copy(
            refs[a].at[:, cols], stage_ref.at[a, :, cols], sem.at[a, part]
        )

    for part in range(PARTS):
        for a in range(4):
            copy(a, part).start()
    spot = block_ids()
    for part in range(PARTS):
        for a in range(4):
            copy(a, part).wait()

        def step(i, carry):
            at = part * (64 // PARTS) + i
            cols = pl.ds(pl.multiple_of(at * PIECE, PIECE), PIECE)
            turned = [
                pltpu.roll(stage_ref[a, :, cols].astype(F32), OWN * a, 1) if a
                else stage_ref[a, :, cols].astype(F32)
                for a in range(4)
            ]
            for k in range(4):
                tile = turned[(3 - k) % 4]
                for pos in range(3):
                    tile = jnp.where(spot == pos, turned[(pos - k) % 4], tile)
                o_ref[(4 * (at % 8) + k) * 8 + at // 8] = tile.astype(BF16)
            return carry

        lax.fori_loop(0, 64 // PARTS, step, 0, unroll=64 // PARTS)


def unpack_kernel(x_ref, a_ref, b_ref, c_ref, d_ref, stage_ref, sem):
    refs = (a_ref, b_ref, c_ref, d_ref)

    def copy(a, part):
        cols = pl.ds(part * PART, PART)
        return pltpu.make_async_copy(
            stage_ref.at[a, :, cols], refs[a].at[:, cols], sem.at[a, part]
        )

    spot = block_ids()
    for part in range(PARTS):

        def step(i, carry):
            at = part * (64 // PARTS) + i
            cols = pl.ds(pl.multiple_of(at * PIECE, PIECE), PIECE)
            tiles = [x_ref[(4 * (at % 8) + k) * 8 + at // 8].astype(F32) for k in range(4)]
            for a in range(4):
                mixed = tiles[(3 - a) % 4]
                for pos in range(3):
                    mixed = jnp.where(spot == pos, tiles[(pos - a) % 4], mixed)
                if a:
                    mixed = pltpu.roll(mixed, PIECE - OWN * a, 1)
                stage_ref[a, :, cols] = mixed.astype(BF16)
            return carry

        lax.fori_loop(0, 64 // PARTS, step, 0, unroll=64 // PARTS)
        for a in range(4):
            copy(a, part).start()
    for part in range(PARTS):
        for a in range(4):
            copy(a, part).wait()


def split(values):
    high = values.astype(BF16)
    return high, (values - high.astype(F32)).astype(BF16)


def dot3(left, right):
    def dot(a, b):
        return jnp.dot(a, b, preferred_element_type=F32)

    return dot(left[0], right[0]) + (dot(left[1], right[0]) + dot(left[0], right[1]))


(M_ONE, M_TWO, L_ONE, L_TWO, FIRST, TAIL, NOTBEG, NEXTCONT, WHOLE) = range(9)


def begins_of(lens_ref):
    begins = [jnp.int32(0)]
    for k in range(NSEQ):
        begins.append(begins[-1] + lens_ref[k])
    return begins


def prep_kernel(
    lens_ref, here_ref, taps_ref, res_ref, pole_ref, gain_ref,
    mask_ref, tapb_ref, tf_ref, tb_ref, we_ref, wh_ref, wr_ref, ws_ref,
    prep_ref,
):
    here = here_ref[0]
    begins = begins_of(lens_ref)

    shape = (NPIECES, PIECE)
    base = lax.broadcasted_iota(jnp.int32, shape, 0) * PIECE
    row = base + lane_ids(shape)

    def count(ids, upto=NSEQ):
        total = jnp.zeros(shape, jnp.int32)
        for k in range(upto):
            total = total + (begins[k] <= ids).astype(jnp.int32)
        return total

    def starts(ids):
        hit = ids == begins[0]
        for k in range(1, NSEQ + 1):
            hit = hit | (ids == begins[k])
        return hit

    own = count(row)
    at_first, at_last, before = count(base), count(base + PIECE - 1), count(base - 1)
    here_start, prior_start = starts(row), starts(row - 1)
    next_start, after_start = starts(row + 1), starts(row + 2)
    one = jnp.ones(shape, F32)
    zero = jnp.zeros(shape, F32)
    mask_ref[M_ONE] = jnp.where(here_start, zero, one)
    mask_ref[M_TWO] = jnp.where(here_start | prior_start, zero, one)
    mask_ref[L_ONE] = jnp.where(next_start, zero, one)
    mask_ref[L_TWO] = jnp.where(next_start | after_start, zero, one)
    mask_ref[FIRST] = jnp.where(own == at_first, one, zero)
    mask_ref[TAIL] = jnp.where(own == at_last, one, zero)
    mask_ref[NOTBEG] = jnp.where(at_first == before, one, zero)
    mask_ref[NEXTCONT] = jnp.where(starts(base + PIECE), zero, one)

    block = pl.ds(pl.multiple_of((here // 4) * 128, 128), 128)
    shift = lax.rem(128 - 32 * lax.rem(here, 4), 128)
    prep_ref[...] = jnp.zeros((PIECE, PIECE), F32)
    for a in range(3):
        for j in range(3):
            prep_ref[a * 3 + j : a * 3 + j + 1, :] = taps_ref[a, j : j + 1, block]
    prep_ref[9:10, :] = gain_ref[0:1, block]
    prep_ref[0:16, :] = pltpu.roll(prep_ref[0:16, :], shift, 1)
    prep_ref[16:18, 0:MODES] = pole_ref[pl.ds(2 * here, 2), :]
    prep_ref[24:26, 0:MODES] = res_ref[pl.ds(2 * here, 2), :]
    turned = prep_ref[...].T

    def column(rows, at):
        return jnp.broadcast_to(turned[0:rows, at : at + 1], (rows, PIECE))

    for j in range(3):
        for a in range(3):
            tapb_ref[j, a * OWN : (a + 1) * OWN, :] = column(OWN, a * 3 + j)
    tapb_ref[3, 0:OWN, :] = column(OWN, 9)
    tapb_ref[3, OWN:96, :] = jnp.zeros((64, PIECE), F32)
    pole = jnp.concatenate([column(MODES, 16), column(MODES, 17)], axis=0)
    residue = jnp.concatenate([column(MODES, 24), column(MODES, 25)], axis=0)
    weight = residue * jnp.sqrt(1.0 - pole * pole)
    lane = lane_ids((2 * MODES, PIECE))
    powers = jnp.ones((2 * MODES, PIECE), F32)
    falling = powers
    square = pole
    for bit in range(7):
        up = ((lane >> bit) & 1) == 1
        powers = jnp.where(up, powers * square, powers)
        falling = jnp.where(up, falling, falling * square)
        square = square * square
    rising = weight * (powers * pole)
    shrinking = weight * (falling * pole)
    taper = weight * powers

    sub_ids = lax.broadcasted_iota(jnp.int32, (PIECE, PIECE), 0)
    col_ids = lane_ids((PIECE, PIECE))
    tf_ref[...] = jnp.zeros(tf_ref.shape, BF16)
    tb_ref[...] = jnp.zeros(tb_ref.shape, BF16)
    wr_ref[...] = jnp.zeros(wr_ref.shape, BF16)
    ws_ref[...] = jnp.zeros(ws_ref.shape, BF16)
    for g in range(2):
        line = jnp.sum(taper[g * MODES : (g + 1) * MODES], axis=0, keepdims=True)
        spread = pltpu.roll(
            jnp.broadcast_to(line, (PIECE, PIECE)), 0, 1, stride=1, stride_axis=0
        )
        toeplitz = jnp.where(col_ids >= sub_ids, spread, 0.0)
        at = slice(g * PIECE, (g + 1) * PIECE)
        for part, tile in enumerate(split(toeplitz)):
            tf_ref[part, at, at] = tile
        for part, tile in enumerate(split(toeplitz.T)):
            tb_ref[part, at, at] = tile
        for ref, source in ((wr_ref, rising), (ws_ref, shrinking)):
            high, low = split(source[g * MODES : (g + 1) * MODES])
            ref[g * MODES : (g + 1) * MODES, at] = high
            ref[32 + g * MODES : 32 + (g + 1) * MODES, at] = high
            ref[64 + g * MODES : 64 + (g + 1) * MODES, at] = low
    blank = jnp.zeros((32, PIECE), F32)
    fall_cols = jnp.concatenate([falling, falling, falling, blank], axis=0).T
    power_cols = jnp.concatenate([powers, powers, powers, blank], axis=0).T
    group_zero = (col_ids & 16) == 0
    for ref, cols in ((we_ref, fall_cols), (wh_ref, power_cols)):
        for part, tile in enumerate(split(cols)):
            wide = tile.astype(F32)
            ref[part, 0:PIECE, :] = jnp.where(group_zero, wide, 0.0).astype(BF16)
            ref[part, PIECE:, :] = jnp.where(group_zero, 0.0, wide).astype(BF16)
    leap = fall_cols[0:1, :] * fall_cols[126:127, :]
    mask_ref[WHOLE] = leap * jnp.where(at_first == at_last, one, zero)

def store_lhs(ref, at, values):
    for part, tile in enumerate(split(values)):
        ref[part, pl.ds(at, 16), 0:PIECE] = tile[0:16]
        ref[part, pl.ds(at, 16), PIECE:] = tile[16:32]


def main_kernel(
    lens_ref, list_ref, here_ref, x_ref,
    mask_ref, tapb_ref, tf_ref, tb_ref, we_ref, wh_ref, wr_ref, ws_ref,
    y_ref, g_ref,
    xt_ref, feat_ref, z_ref, gu_ref,
    lzf_ref, lzt_ref, lgt_ref, lgf_ref,
    u_ref, gz_ref, e_ref, h_ref, gs_ref, ys_ref, acc_ref,
):
    begins = begins_of(lens_ref)
    turn = lax.rem(here_ref[0], 4)

    def place(pos):
        return pl.ds(pl.multiple_of(lax.rem(pos + turn, 4) * OWN, OWN), OWN)

    def unplace(pos):
        return pl.ds(pl.multiple_of(lax.rem(pos + 4 - turn, 4) * OWN, OWN), OWN)

    xt_ref[0] = jnp.zeros((PIECE, PIECE), F32)
    gs_ref[NPIECES] = jnp.zeros((96, PIECE), F32)
    acc_ref[...] = jnp.zeros(acc_ref.shape, F32)

    def turn_in(s, carry):
        tile = x_ref[pl.ds(s * 8, 8)].reshape(PIECE, PIECE).astype(F32).T
        p = list_ref[s] + 1
        for pos in range(4):
            xt_ref[p, unplace(pos), :] = tile[pos * OWN : (pos + 1) * OWN]
        return carry

    lax.fori_loop(0, NPIECES, turn_in, 0, unroll=CHUNK)

    lane = lane_ids((OWN, PIECE))

    def mask(which, p):
        return mask_ref[which, pl.ds(p, 1), :]

    def part(a):
        return slice(a * OWN, (a + 1) * OWN)

    def ahead(chunk, carry):
        skip = jnp.zeros((OWN, PIECE), F32)
        for i in range(CHUNK):
            p = chunk * CHUNK + i
            feats = []
            for a in range(3):
                x = xt_ref[p + 1, part(a), :]
                prior = xt_ref[p, part(a), :]
                x_one = pltpu.roll(jnp.where(lane == PIECE - 1, prior, x), 1, 1)
                x_two = pltpu.roll(jnp.where(lane >= PIECE - 2, prior, x), 2, 1)
                feat = (
                    tapb_ref[0, part(a), :] * x
                    + mask(M_ONE, p) * (tapb_ref[1, part(a), :] * x_one)
                    + mask(M_TWO, p) * (tapb_ref[2, part(a), :] * x_two)
                )
                feat_ref[p, part(a), :] = feat
                feats.append(feat)
            z = feats[1] * feats[2]
            gu = xt_ref[p + 1, part(3), :] * feats[0]
            z_ref[p] = z
            gu_ref[p] = gu
            skip = skip + gu * z
            first = mask(FIRST, p)
            tail = mask(TAIL, p)
            at = pl.multiple_of(p * 16, 16)
            store_lhs(lzf_ref, at, z * first)
            store_lhs(lzt_ref, at, z * tail)
            store_lhs(lgt_ref, at, gu * tail)
            store_lhs(lgf_ref, at, gu * first)
        acc_ref[0, part(3), :] += skip
        return carry

    lax.fori_loop(0, NPIECES // CHUNK, ahead, 0)

    line = lane_ids((1, PIECE))
    extras = []
    for k in range(1, NSEQ):
        p = begins[k] // PIECE
        rows = p * PIECE + line
        inner = lax.rem(begins[k], PIECE) != 0
        later = (rows >= begins[k]) & (rows < begins[k + 1]) & inner
        sooner = (rows >= begins[k - 1]) & (rows < begins[k]) & inner
        later = jnp.where(later, 1.0, 0.0)
        sooner = jnp.where(sooner, 1.0, 0.0)
        extras.append((p, later, sooner))
        store_lhs(lzf_ref, BASE + (k - 1) * 16, z_ref[p] * later)
        store_lhs(lgt_ref, BASE + (k - 1) * 16, gu_ref[p] * sooner)
    none = jnp.zeros((OWN, PIECE), F32)
    store_lhs(lzf_ref, VROWS - 16, none)
    store_lhs(lgt_ref, VROWS - 16, none)

    def both(ref):
        return ref[0], ref[1]

    e_ref[...] = dot3(both(lzt_ref), both(we_ref))
    h_ref[...] = dot3(both(lgf_ref), both(wh_ref))

    def scan(step, carry):
        state, back = carry
        p = step
        at = pl.ds(pl.multiple_of(p * 16, 16), 16)
        found = e_ref[at, :]
        state = state * mask(NOTBEG, p)
        e_ref[at, :] = state
        state = found + mask(WHOLE, p) * state
        p = NPIECES - 1 - step
        at = pl.ds(pl.multiple_of(p * 16, 16), 16)
        found = h_ref[at, :]
        back = back * mask(NEXTCONT, p)
        h_ref[at, :] = back
        back = found + mask(WHOLE, p) * back
        return state, back

    idle = jnp.zeros((16, PIECE), F32)
    lax.fori_loop(0, NPIECES, scan, (idle, idle), unroll=8)

    def three(states):
        high = states.astype(BF16).astype(F32)
        lane = lane_ids(states.shape)
        low = (lane >= 32) & (lane < 64)
        return jnp.where(low, states - high, high).astype(BF16)

    u_ref[...] = dot3(both(lzf_ref), both(tf_ref))
    gz_ref[...] = dot3(both(lgt_ref), both(tb_ref))
    u_ref[0:BASE, :] += jnp.dot(three(e_ref[...]), wr_ref[...], preferred_element_type=F32)
    gz_ref[0:BASE, :] += jnp.dot(three(h_ref[...]), ws_ref[...], preferred_element_type=F32)
    for k, (p, later, sooner) in enumerate(extras):
        at = pl.ds(pl.multiple_of(p * 16, 16), 16)
        more = slice(BASE + k * 16, BASE + (k + 1) * 16)
        for ref, kept in ((u_ref, later), (gz_ref, sooner)):
            for half in (slice(0, PIECE), slice(PIECE, 2 * PIECE)):
                ref[at, half] = jnp.where(kept > 0.0, ref[more, half], ref[at, half])

    def gradients(p, carry):
        at = pl.ds(pl.multiple_of(p * 16, 16), 16)
        gain = tapb_ref[3, 0:OWN, :]
        u = jnp.concatenate([u_ref[at, 0:PIECE], u_ref[at, PIECE:]], axis=0)
        gz = jnp.concatenate([gz_ref[at, 0:PIECE], gz_ref[at, PIECE:]], axis=0)
        filtered = u + gain * z_ref[p]
        gz = gz + gain * gu_ref[p]
        ys_ref[p, place(0), :] = feat_ref[p, part(0), :] * filtered
        gs_ref[p, part(0), :] = xt_ref[p + 1, part(3), :] * filtered
        gs_ref[p, part(1), :] = gz * feat_ref[p, part(2), :]
        gs_ref[p, part(2), :] = gz * feat_ref[p, part(1), :]
        return carry

    lax.fori_loop(0, NPIECES, gradients, 0, unroll=CHUNK)

    def behind(chunk, carry):
        for a in range(3):
            sums = [jnp.zeros((OWN, PIECE), F32) for _ in range(3)]
            for i in range(CHUNK):
                p = chunk * CHUNK + i
                grad = gs_ref[p, part(a), :]
                after = gs_ref[p + 1, part(a), :]
                x = xt_ref[p + 1, part(a), :]
                g_one = pltpu.roll(jnp.where(lane == 0, after, grad), PIECE - 1, 1)
                g_two = pltpu.roll(jnp.where(lane < 2, after, grad), PIECE - 2, 1)
                g_one = mask(L_ONE, p) * g_one
                g_two = mask(L_TWO, p) * g_two
                ys_ref[p, place(a + 1), :] = (
                    tapb_ref[0, part(a), :] * grad
                    + tapb_ref[1, part(a), :] * g_one
                    + tapb_ref[2, part(a), :] * g_two
                )
                for j, g in enumerate((grad, g_one, g_two)):
                    sums[j] = sums[j] + g * x
            for j in range(3):
                acc_ref[j, part(a), :] += sums[j]
        return carry

    lax.fori_loop(0, NPIECES // CHUNK, behind, 0)

    def turn_out(s, carry):
        tile = ys_ref[list_ref[s]].T.astype(BF16)
        y_ref[pl.ds(s * 8, 8)] = tile.reshape(8, 16, PIECE)
        return carry

    lax.fori_loop(0, NPIECES, turn_out, 0, unroll=CHUNK)
    norm = 1.0 / math.sqrt(TOKENS)
    g_ref[...] = jnp.zeros(g_ref.shape, F32)
    for j in range(3):
        g_ref[j : j + 1, :] = norm * jnp.sum(acc_ref[j].T, axis=0, keepdims=True)


def place_kernel(here_ref, parts_ref, taps_ref, skip_ref):
    here = here_ref[0]
    spot = lane_ids((8, PIECE)) // OWN
    for j in range(3):
        rows = []
        for k in range(4):
            picked = [parts_ref[(4 * q + k) ^ here, j : j + 1, :] for q in range(8)]
            rows.append(jnp.concatenate(picked, axis=0))
        for a in range(4 if j == 0 else 3):
            moved = [
                pltpu.roll(rows[k], ((k - a) % 4) * OWN, 1) if k != a else rows[k]
                for k in range(4)
            ]
            line = moved[3]
            for k in range(3):
                line = jnp.where(spot == k, moved[k], line)
            for q in range(8):
                cols = slice(q * PIECE, (q + 1) * PIECE)
                if a < 3:
                    taps_ref[a, j : j + 1, cols] = line[q : q + 1]
                else:
                    skip_ref[0:1, cols] = line[q : q + 1]


VM = pl.BlockSpec(memory_space=pltpu.VMEM)
SM = pl.BlockSpec(memory_space=pltpu.SMEM)
ANY = pl.BlockSpec(memory_space=pl.ANY)


def cost(flops, moved):
    return pl.CostEstimate(flops=flops, bytes_accessed=moved, transcendentals=0)


STAGE = [pltpu.VMEM((4, 16, 8192), BF16), pltpu.SemaphoreType.DMA((4, PARTS))]


def run_pack(*arrays):
    return pl.pallas_call(
        pack_kernel,
        out_shape=jax.ShapeDtypeStruct((256, 16, 128), BF16),
        in_specs=[ANY] * 4,
        out_specs=VM,
        scratch_shapes=STAGE,
        name="pack",
    )(*arrays)


def run_unpack(blocks):
    return pl.pallas_call(
        unpack_kernel,
        out_shape=[jax.ShapeDtypeStruct((16, 8192), BF16)] * 4,
        in_specs=[VM],
        out_specs=[ANY] * 4,
        scratch_shapes=STAGE,
        name="unpack",
    )(blocks)


def run_prep(lens, here, taps, residues, poles, gain):
    shapes = [
        ((9, NPIECES, PIECE), F32),
        ((4, 96, PIECE), F32),
        ((2, 256, 256), BF16),
        ((2, 256, 256), BF16),
        ((2, 256, PIECE), BF16),
        ((2, 256, PIECE), BF16),
        ((PIECE, 256), BF16),
        ((PIECE, 256), BF16),
    ]
    return pl.pallas_call(
        prep_kernel,
        out_shape=[jax.ShapeDtypeStruct(*shape) for shape in shapes],
        in_specs=[SM, SM, VM, VM, VM, VM],
        out_specs=[VM] * 8,
        scratch_shapes=[pltpu.VMEM((PIECE, PIECE), F32)],
        cost_estimate=cost(4_000_000, 1 << 20),
        name="prep",
    )(lens, here, taps, residues, poles, gain)


def run_main(lens, pieces, here, blocks, *prepared):
    scratch = [
        pltpu.VMEM((NPIECES + 1, PIECE, PIECE), F32),
        pltpu.VMEM((NPIECES, 96, PIECE), F32),
        pltpu.VMEM((NPIECES, OWN, PIECE), F32),
        pltpu.VMEM((NPIECES, OWN, PIECE), F32),
        pltpu.VMEM((2, VROWS, 256), BF16),
        pltpu.VMEM((2, BASE, 256), BF16),
        pltpu.VMEM((2, VROWS, 256), BF16),
        pltpu.VMEM((2, BASE, 256), BF16),
        pltpu.VMEM((VROWS, 256), F32),
        pltpu.VMEM((VROWS, 256), F32),
        pltpu.VMEM((BASE, PIECE), F32),
        pltpu.VMEM((BASE, PIECE), F32),
        pltpu.VMEM((NPIECES + 1, 96, PIECE), F32),
        pltpu.VMEM((NPIECES, PIECE, PIECE), F32),
        pltpu.VMEM((3, PIECE, PIECE), F32),
    ]
    return pl.pallas_call(
        main_kernel,
        out_shape=[
            jax.ShapeDtypeStruct((256, 16, 128), BF16),
            jax.ShapeDtypeStruct((8, 128), F32),
        ],
        in_specs=[SM, SM, SM] + [VM] * 9,
        out_specs=[VM, VM],
        scratch_shapes=scratch,
        compiler_params=pltpu.CompilerParams(vmem_limit_bytes=48 * 1024 * 1024),
        name="block",
    )(lens, pieces, here, blocks, *prepared)


def run_place(here, parts):
    return pl.pallas_call(
        place_kernel,
        out_shape=[
            jax.ShapeDtypeStruct((3, 3, 1024), F32),
            jax.ShapeDtypeStruct((1, 1024), F32),
        ],
        in_specs=[SM, VM],
        out_specs=[VM, VM],
        cost_estimate=cost(1_000_000, 1 << 17),
        name="place",
    )(here, parts)


def exchange(blocks):
    return lax.all_to_all(blocks, BOTH, split_axis=0, concat_axis=0, tiled=True)


def gather_sums(sums):
    held = sums[None]
    for bit in (1, 2, 4, 8, 16):
        pairs = [(i, i ^ bit) for i in range(32)]
        held = jnp.concatenate([held, lax.ppermute(held, "ctx", pairs)], axis=0)
    return held


def local(
    gate_rows,
    key_rows,
    value_rows,
    out_grad,
    conv_taps,
    filter_residues,
    filter_poles,
    skip_gain,
    seq_lengths,
    piece_list,
):
    here = lax.axis_index("ctx").astype(jnp.int32).reshape(1)
    blocks = exchange(run_pack(gate_rows, key_rows, value_rows, out_grad))
    prepared = run_prep(
        seq_lengths,
        here,
        conv_taps,
        filter_residues,
        filter_poles,
        skip_gain.reshape(1, -1),
    )
    results, sums = run_main(seq_lengths, piece_list, here, blocks, *prepared)
    outs = run_unpack(exchange(results))
    taps_grad, skip_grad = run_place(here, gather_sums(sums))
    return (*outs, taps_grad, skip_grad.reshape(1024))


def solution(mesh):
    rows = P(BOTH, None)
    return jax.shard_map(
        local,
        mesh=mesh,
        in_specs=(
            rows, rows, rows, rows,
            P(None, None, "mp"), P("mp", None), P("mp", None), P("mp"), P(), P(),
        ),
        out_specs=(rows, rows, rows, rows, P(None, None, "mp"), P("mp")),
        check_vma=False,
    )
```

time: 140 us -> 123 us (0.88); the launches traced: 140 us -> 121 us
  blocking collectives: 60.1 us -> 0 us
  waiting for transfers between devices: 31 us -> 59.5 us
  starting transfers between devices: 20.8 us -> 34.1 us
  Pallas kernels: 20.8 us -> 16 us
  local copies, waits for them, and re-layouts: 6.31 us -> 10.9 us
    all_gather x1 -> x0, blocking collectives: 60.1 us -> none  [local(): every = lax.all_gather(sums, 'ctx', axis=0, tiled=False)]
    ppermute x0 -> x5, waiting for transfers between devices: none -> 32 us  [gather_sums(): held = jnp.concatenate([held, lax.ppermute(held, 'ctx', pairs)], axis=0)]
    ppermute x0 -> x5, starting transfers between devices: none -> 13.3 us  [gather_sums(): held = jnp.concatenate([held, lax.ppermute(held, 'ctx', pairs)], axis=0)]
    unnamed x23 -> x34, local copies, waits for them, and re-layouts: 4.64 us -> 10.9 us
    pallas_call x0 -> x2, Pallas kernels: none -> 3.89 us  [the longest x1 2.24 us: run_prep(): pl.pallas_call(prep_kernel, out_shape=[jax.ShapeDtypeStruct(*shape) for s...]
    pallas_call x1, Pallas kernels: 10.6 us -> 6.94 us  [run_main(): pl.pallas_call(main_kernel, out_shape=[jax.ShapeDtypeStruct((256, 16, 128...]
    all_to_all x2, waiting for transfers between devices: 31 us -> 27.5 us  [exchange(): return lax.all_to_all(blocks, BOTH, split_axis=0, concat_axis=0, tiled=True)]
    pallas_call x1, Pallas kernels: 5.11 us -> 2.54 us  [run_unpack(): pl.pallas_call(unpack_kernel, out_shape=[jax.ShapeDtypeStruct((16, 8192),...]
  transfers between devices with their start and end apart: 2 -> 7, of which waited for: 1 -> 6; matrix products, arithmetic and copies ran while one was open for 1% -> 1% of each run, Pallas kernels for 0% -> 3%
where the time goes in v2:
time: 123 us; the launch traced here: 121 us
  waiting for transfers between devices  59.5 us (48%)
  starting transfers between devices  34.1 us (28%)
  Pallas kernels  16 us (13%)
  local copies, waits for them, and re-layouts  10.9 us (9%)
    ppermute x5, waiting for transfers between devices, gather_sums(): held = jnp.concatenate([held, lax.ppermute(held, 'ctx', pairs)], axis=0)  32 us
    all_to_all x2, waiting for transfers between devices, exchange(): return lax.all_to_all(blocks, BOTH, split_axis=0, concat_axis=0, tiled=True)  27.5 us
    all_to_all x2, starting transfers between devices, exchange(): return lax.all_to_all(blocks, BOTH, split_axis=0, concat_axis=0, tiled=True)  20.8 us
    ppermute x5, starting transfers between devices, gather_sums(): held = jnp.concatenate([held, lax.ppermute(held, 'ctx', pairs)], axis=0)  13.3 us
    unnamed x34, local copies, waits for them, and re-layouts  10.9 us
    pallas_call x1, Pallas kernels, run_main(): pl.pallas_call(main_kernel, out_shape=[jax.ShapeDtypeStruct((256, 16, 128...  6.94 us
    pallas_call x1, Pallas kernels, run_pack(): pl.pallas_call(pack_kernel, out_shape=jax.ShapeDtypeStruct((256, 16, 128)...  2.66 us
    pallas_call x1, Pallas kernels, run_unpack(): pl.pallas_call(unpack_kernel, out_shape=[jax.ShapeDtypeStruct((16, 8192),...  2.54 us
  transfers between devices with their start and end apart: 7, of which 6 were waited for; matrix products, arithmetic and copies ran while one was open for 1% of the time, Pallas kernels for 3%

profile of v2, /device:TPU:8, one launch (start us, length us, event | category | flops | bytes accessed | tf_op | source)
XLA Modules:
  0.0 121.4 jit_solution(11457907027633544476)
XLA Ops:
  0.6 2.7 %pack.1 = bf16[256,16,128]{2,1,0:T(8,128)(2,1)} custom-call(bf16[16,8192]{1,0:T(8,128)(2,1)} %a_ref.1, bf16[16,8192]{1,0:T(8,128)(2,1)} %b_ref.1, bf16[16,8192]{1,0:T(8,128)(2,1)} %c_ref.1, bf16[16,8192]{1,0:T(8,128)(2,1)} %d_ref.1), custom_call_target="tpu_custom_call" | custom-call | tf_op jit(solution)/shard_map/pack/pallas_call | solution.py:459
  3.3 0.0 copy-start.12
  3.3 14.6 %all-to-all-start = ((bf16[256,16,128]{2,1,0:T(8,128)(2,1)}), bf16[256,16,128]{2,1,0:T(8,128)(2,1)S(1)}, u32[]{:S(2)}, u32[]{:S(2)}) async-start(bf16[256,16,128]{2,1,0:T(8,128)(2,1)} %pack.1), calls=%async_computation | async-start | bytes 2097152 | tf_op jit(solution)/shard_map/all_to_all | solution.py:549
  17.9 0.0 copy-done.12
  18.0 0.0 copy-start.13
  18.0 0.7 copy.16.res_ref
  18.7 0.0 copy-done.13
  18.7 0.7 copy.17.pole_ref
  19.3 2.2 %prep.1 = (f32[9,32,128]{2,1,0:T(8,128)}, f32[4,96,128]{2,1,0:T(8,128)}, bf16[2,256,256]{2,1,0:T(8,128)(2,1)}, bf16[2,256,256]{2,1,0:T(8,128)(2,1)}, bf16[2,256,...) custom-call(s32[8]{0:T(128)} %lens_ref.3, ...), custom_call_target="tpu_custom_call" | custom-call | flops 4000000 | bytes 1048576 | tf_op jit(solution)/shard_map/prep/pallas_call | solution.py:491
  21.6 27.5 %all-to-all-done.x_ref = bf16[256,16,128]{2,1,0:T(8,128)(2,1)S(1)} async-done(((bf16[256,16,128]{2,1,0:T(8,128)(2,1)}), bf16[256,16,128]{2,1,0:T(8,128)(2,1)S(1)}, u32[]{:S(2)}, u32[]{:S(2)}) %all-to-all-start) | async-done | bytes 1048608 | tf_op jit(solution)/shard_map/all_to_all | solution.py:549
  49.1 0.0 copy-start.8
  49.1 0.0 copy-start.9
  49.1 0.7 copy-done.8
  49.8 0.0 copy-done.9
  49.8 0.0 copy-start
  49.8 0.9 copy-done
  50.7 0.0 copy-start.1
  50.7 0.9 copy-done.1
  51.7 0.0 copy-start.2
  51.7 0.9 copy-done.2
  52.6 0.0 copy-start.3
  52.6 0.9 copy-done.3
  53.5 0.0 copy-start.4
  53.5 0.9 copy-done.4
  54.4 0.0 copy-start.5
  54.4 0.9 copy-done.5
  55.3 0.0 copy-start.6
  55.3 0.8 copy-done.6
  56.2 0.0 copy-start.7
  56.2 0.8 copy-done.7
  57.0 6.9 %block.1 = (bf16[256,16,128]{2,1,0:T(8,128)(2,1)}, f32[8,128]{1,0:T(8,128)S(1)}) custom-call(s32[8]{0:T(128)S(1)} %copy-done.8, s32[32]{0:T(128)S(1)} %copy-done.9, s32[1]{0:T(128)} %bitcast.here_ref, bf16[256,16,128]{2,1,0:T(8,128)(2,1)S(1)} %all-to-all-done.x_ref, f32[9,32,128]{2,1,0:T(8,128)S(1)} %copy-done.3, f32[4,96,128]{2,1,0:T(8,128)S(1)} %copy-done.2, ...), custom_call_target="tpu_custom_call" | custom-call | tf_op jit(solution)/shard_map/block/pallas_call | solution.py:520
  64.0 6.2 %all-to-all-start.1 = ((bf16[256,16,128]{2,1,0:T(8,128)(2,1)}), bf16[256,16,128]{2,1,0:T(8,128)(2,1)S(1)}, u32[]{:S(2)}, u32[]{:S(2)}) async-start(bf16[256,16,128]{2,1,0:T(8,128)(2,1)} %get-tuple-element.30), calls=%async_computation.1 | async-start | bytes 2097152 | tf_op jit(solution)/shard_map/all_to_all | solution.py:549
  70.2 1.7 %collective-permute-start = (f32[1,8,128]{2,1,0:T(8,128)S(1)}, f32[1,8,128]{2,1,0:T(8,128)S(1)}, u32[]{:S(2)}, u32[]{:S(2)}) collective-permute-start(f32[1,8,128]{2,1,0:T(8,128)S(1)} %bitcast.6), channel_id=1, source_target_pairs={{0,8},{8,0},{16,24},{24,16},{32,40},{40,32},{48,56},{56,48},{64,72... | collective-permute-start | bytes 12296 | tf_op jit(solution)/shard_map/ppermute | solution.py:556
  71.9 21.7 %collective-permute-done = f32[1,8,128]{2,1,0:T(8,128)S(1)} collective-permute-done((f32[1,8,128]{2,1,0:T(8,128)S(1)}, f32[1,8,128]{2,1,0:T(8,128)S(1)}, u32[]{:S(2)}, u32[]{:S(2)}) %collective-permute-start) | collective-permute-done | bytes 4128 | tf_op jit(solution)/shard_map/ppermute | solution.py:556
  93.6 1.1 collective-permute-start.1
  94.7 3.5 %collective-permute-done.1 = f32[2,8,128]{2,1,0:T(8,128)S(1)} collective-permute-done((f32[2,8,128]{2,1,0:T(8,128)S(1)}, f32[2,8,128]{2,1,0:T(8,128)S(1)}, u32[]{:S(2)}, u32[]{:S(2)}) %collective-permute-start.1) | collective-permute-done | bytes 8224 | tf_op jit(solution)/shard_map/ppermute | solution.py:556
  98.2 5.6 %collective-permute-start.2 = (f32[4,8,128]{2,1,0:T(8,128)S(1)}, f32[4,8,128]{2,1,0:T(8,128)S(1)}, u32[]{:S(2)}, u32[]{:S(2)}) collective-permute-start(f32[4,8,128]{2,1,0:T(8,128)S(1)} %pad_maximum_fusion.1), channel_id=1, source_target_pairs={{0,32},{8,40},{16,48},{24,56},{32,0},{40,8},{48,16},{56,24},{64,96... | collective-permute-start | bytes 49160 | tf_op jit(solution)/shard_map/ppermute | solution.py:556
  103.8 2.0 %collective-permute-done.2 = f32[4,8,128]{2,1,0:T(8,128)S(1)} collective-permute-done((f32[4,8,128]{2,1,0:T(8,128)S(1)}, f32[4,8,128]{2,1,0:T(8,128)S(1)}, u32[]{:S(2)}, u32[]{:S(2)}) %collective-permute-start.2) | collective-permute-done | bytes 16416 | tf_op jit(solution)/shard_map/ppermute | solution.py:556
  105.8 1.5 %collective-permute-start.3 = (f32[8,8,128]{2,1,0:T(8,128)S(1)}, f32[8,8,128]{2,1,0:T(8,128)S(1)}, u32[]{:S(2)}, u32[]{:S(2)}) collective-permute-start(f32[8,8,128]{2,1,0:T(8,128)S(1)} %pad_maximum_fusion), channel_id=1, source_target_pairs={{0,64},{8,72},{16,80},{24,88},{32,96},{40,104},{48,112},{56,120},{... | collective-permute-start | bytes 98312 | tf_op jit(solution)/shard_map/ppermute | solution.py:556
  107.3 2.4 %collective-permute-done.3 = f32[8,8,128]{2,1,0:T(8,128)S(1)} collective-permute-done((f32[8,8,128]{2,1,0:T(8,128)S(1)}, f32[8,8,128]{2,1,0:T(8,128)S(1)}, u32[]{:S(2)}, u32[]{:S(2)}) %collective-permute-start.3) | collective-permute-done | bytes 32800 | tf_op jit(solution)/shard_map/ppermute | solution.py:556
  109.7 3.4 %collective-permute-start.4 = (f32[16,8,128]{2,1,0:T(8,128)S(1)}, f32[16,8,128]{2,1,0:T(8,128)S(1)}, u32[]{:S(2)}, u32[]{:S(2)}) collective-permute-start(f32[16,8,128]{2,1,0:T(8,128)S(1)} %get-tuple-element.38), channel_id=1, source_target_pairs={{0,128},{8,136},{16,144},{24,152},{32,160},{40,168},{48,176},{56,1... | collective-permute-start | bytes 196616 | tf_op jit(solution)/shard_map/ppermute | solution.py:556
  113.1 2.4 %collective-permute-done.4 = f32[16,8,128]{2,1,0:T(8,128)S(1)} collective-permute-done((f32[16,8,128]{2,1,0:T(8,128)S(1)}, f32[16,8,128]{2,1,0:T(8,128)S(1)}, u32[]{:S(2)}, u32[]{:S(2)}) %collective-permute-start.4) | collective-permute-done | bytes 65568 | tf_op jit(solution)/shard_map/ppermute | solution.py:556
  115.5 0.0 copy-start.11
  115.5 0.7 copy-done.11
  116.2 1.7 %place.1 = (f32[3,3,1024]{2,1,0:T(4,128)}, f32[1,1024]{1,0:T(1,128)}) custom-call(s32[1]{0:T(128)} %bitcast.here_ref, f32[32,8,128]{2,1,0:T(8,128)} %copy-done.11), custom_call_target="tpu_custom_call" | custom-call | flops 1000000 | bytes 131072 | tf_op jit(solution)/shard_map/place/pallas_call | solution.py:535
  117.8 0.0 all-to-all-done.1.x_ref
  117.8 1.0 copy-done.10
  118.8 2.5 %unpack.1 = (bf16[16,8192]{1,0:T(8,128)(2,1)}, bf16[16,8192]{1,0:T(8,128)(2,1)}, bf16[16,8192]{1,0:T(8,128)(2,1)}, bf16[16,8192]{1,0:T(8,128)(2,1)}) custom-call(bf16[256,16,128]{2,1,0:T(8,128)(2,1)} %copy-done.10), custom_call_target="tpu_custom_call" | custom-call | tf_op jit(solution)/shard_map/unpack/pallas_call | solution.py:470
  (10 shorter events, 0.0 us)
Async XLA Ops:
  3.3 14.6 %copy-start.12 = (f32[64,16]{0,1:T(8,128)S(1)}, f32[64,16]{0,1:T(8,128)}, u32[]{:S(2)}) copy-start(f32[64,16]{0,1:T(8,128)} %param.15) | copy-start | bytes 12292
  3.3 45.8 %all-to-all-start = ((bf16[256,16,128]{2,1,0:T(8,128)(2,1)}), bf16[256,16,128]{2,1,0:T(8,128)(2,1)S(1)}, u32[]{:S(2)}, u32[]{:S(2)}) async-start(bf16[256,16,128]{2,1,0:T(8,128)(2,1)} %pack.1), calls=%async_computation | async-start | bytes 2097152 | tf_op jit(solution)/shard_map/all_to_all | solution.py:549
  18.0 0.7 copy-start.13
  49.1 0.7 copy-start.8
  49.1 0.7 copy-start.9
  49.8 0.9 copy-start
  50.7 0.9 copy-start.1
  51.7 0.9 copy-start.2
  52.6 0.9 copy-start.3
  53.5 0.9 copy-start.4
  54.4 0.9 copy-start.5
  55.3 0.8 copy-start.6
  56.2 0.8 copy-start.7
  64.0 53.9 %all-to-all-start.1 = ((bf16[256,16,128]{2,1,0:T(8,128)(2,1)}), bf16[256,16,128]{2,1,0:T(8,128)(2,1)S(1)}, u32[]{:S(2)}, u32[]{:S(2)}) async-start(bf16[256,16,128]{2,1,0:T(8,128)(2,1)} %get-tuple-element.30), calls=%async_computation.1 | async-start | bytes 2097152 | tf_op jit(solution)/shard_map/all_to_all | solution.py:549
  70.2 23.4 %collective-permute-start = (f32[1,8,128]{2,1,0:T(8,128)S(1)}, f32[1,8,128]{2,1,0:T(8,128)S(1)}, u32[]{:S(2)}, u32[]{:S(2)}) collective-permute-start(f32[1,8,128]{2,1,0:T(8,128)S(1)} %bitcast.6), channel_id=1, source_target_pairs={{0,8},{8,0},{16,24},{24,16},{32,40},{40,32},{48,56},{56,48},{64,72... | collective-permute-start | bytes 12296 | tf_op jit(solution)/shard_map/ppermute | solution.py:556
  93.6 4.6 %collective-permute-start.1 = (f32[2,8,128]{2,1,0:T(8,128)S(1)}, f32[2,8,128]{2,1,0:T(8,128)S(1)}, u32[]{:S(2)}, u32[]{:S(2)}) collective-permute-start(f32[2,8,128]{2,1,0:T(8,128)S(1)} %pad_maximum_fusion.2), channel_id=1, source_target_pairs={{0,16},{8,24},{16,0},{24,8},{32,48},{40,56},{48,32},{56,40},{64,80... | collective-permute-start | bytes 24584 | tf_op jit(solution)/shard_map/ppermute | solution.py:556
  98.2 7.6 %collective-permute-start.2 = (f32[4,8,128]{2,1,0:T(8,128)S(1)}, f32[4,8,128]{2,1,0:T(8,128)S(1)}, u32[]{:S(2)}, u32[]{:S(2)}) collective-permute-start(f32[4,8,128]{2,1,0:T(8,128)S(1)} %pad_maximum_fusion.1), channel_id=1, source_target_pairs={{0,32},{8,40},{16,48},{24,56},{32,0},{40,8},{48,16},{56,24},{64,96... | collective-permute-start | bytes 49160 | tf_op jit(solution)/shard_map/ppermute | solution.py:556
  105.8 3.9 %collective-permute-start.3 = (f32[8,8,128]{2,1,0:T(8,128)S(1)}, f32[8,8,128]{2,1,0:T(8,128)S(1)}, u32[]{:S(2)}, u32[]{:S(2)}) collective-permute-start(f32[8,8,128]{2,1,0:T(8,128)S(1)} %pad_maximum_fusion), channel_id=1, source_target_pairs={{0,64},{8,72},{16,80},{24,88},{32,96},{40,104},{48,112},{56,120},{... | collective-permute-start | bytes 98312 | tf_op jit(solution)/shard_map/ppermute | solution.py:556
  109.7 5.8 %collective-permute-start.4 = (f32[16,8,128]{2,1,0:T(8,128)S(1)}, f32[16,8,128]{2,1,0:T(8,128)S(1)}, u32[]{:S(2)}, u32[]{:S(2)}) collective-permute-start(f32[16,8,128]{2,1,0:T(8,128)S(1)} %get-tuple-element.38), channel_id=1, source_target_pairs={{0,128},{8,136},{16,144},{24,152},{32,160},{40,168},{48,176},{56,1... | collective-permute-start | bytes 196616 | tf_op jit(solution)/shard_map/ppermute | solution.py:556
  115.5 0.7 copy-start.11
  117.8 1.0 copy-start.10

commit v3 on v2

v3 whole, which is shorter than its diff:
```python
import math

import jax
import jax.numpy as jnp
from jax import lax
from jax.experimental import pallas as pl
from jax.experimental.pallas import tpu as pltpu
from jax.sharding import PartitionSpec as P

BOTH = ("ctx", "mp")
PIECE = 128
NPIECES = 32
NSEQ = 8
MODES = 16
OWN = 32
TOKENS = 4096
BASE = NPIECES * 16
VROWS = BASE + NSEQ * 16
PARTS = 4
PART = 8192 // PARTS
CHUNK = 8
MASKS = 9 * NPIECES
PLAN_ROWS = MASKS + 3 * 96 + OWN
T_AHEAD, T_BACK, C_AHEAD, C_BACK, E_BOTH = 0, 512, 1024, 1152, 1280
MAT_ROWS = 1792
LIMIT_MB = 48
F32 = jnp.float32
BF16 = jnp.bfloat16


def lane_ids(shape):
    return lax.broadcasted_iota(jnp.int32, shape, 1)


def block_ids():
    return lane_ids((16, PIECE)) // OWN


def pack_kernel(a_ref, b_ref, c_ref, d_ref, out_ref, stage_ref, o_ref, sem, out_sem):
    refs = (a_ref, b_ref, c_ref, d_ref)

    def copy(a, part):
        cols = pl.ds(part * PART, PART)
        return pltpu.make_async_copy(
            refs[a].at[:, cols], stage_ref.at[a, :, cols], sem.at[a, part]
        )

    def send(part):
        js = pl.ds(part * (8 // PARTS), 8 // PARTS)
        return pltpu.make_async_copy(o_ref.at[:, js], out_ref.at[:, js], out_sem.at[part])

    for part in range(PARTS):
        for a in range(4):
            copy(a, part).start()
    spot = block_ids()
    for part in range(PARTS):
        for a in range(4):
            copy(a, part).wait()

        def step(i, carry):
            at = part * (64 // PARTS) + i
            cols = pl.ds(pl.multiple_of(at * PIECE, PIECE), PIECE)
            turned = [
                pltpu.roll(stage_ref[a, :, cols].astype(F32), OWN * a, 1) if a
                else stage_ref[a, :, cols].astype(F32)
                for a in range(4)
            ]
            for k in range(4):
                tile = turned[(3 - k) % 4]
                for pos in range(3):
                    tile = jnp.where(spot == pos, turned[(pos - k) % 4], tile)
                o_ref[4 * (at % 8) + k, at // 8] = tile.astype(BF16)
            return carry

        lax.fori_loop(0, 64 // PARTS, step, 0, unroll=64 // PARTS)
        send(part).start()
    for part in range(PARTS):
        send(part).wait()


def place_sums(here, parts_ref, taps_ref, skip_ref):
    spot = lane_ids((8, PIECE)) // OWN

    def order(flip):
        return (flip >> 3) + 4 * (flip & 3) + 16 * ((flip >> 2) & 1)

    for j in range(3):
        rows = []
        for k in range(4):
            picked = [
                parts_ref[order((4 * q + k) ^ here), j : j + 1, :] for q in range(8)
            ]
            rows.append(jnp.concatenate(picked, axis=0))
        for a in range(4 if j == 0 else 3):
            moved = [
                pltpu.roll(rows[k], ((k - a) % 4) * OWN, 1) if k != a else rows[k]
                for k in range(4)
            ]
            line = moved[3]
            for k in range(3):
                line = jnp.where(spot == k, moved[k], line)
            for q in range(8):
                cols = slice(q * PIECE, (q + 1) * PIECE)
                if a < 3:
                    taps_ref[a, j : j + 1, cols] = line[q : q + 1]
                else:
                    skip_ref[0:1, cols] = line[q : q + 1]


def unpack_kernel(
    here_ref, x_ref, parts_ref, a_ref, b_ref, c_ref, d_ref, taps_ref, skip_ref,
    stage_ref, tapv_ref, skipv_ref, sem, small_sem,
):
    refs = (a_ref, b_ref, c_ref, d_ref)

    def copy(a, part):
        cols = pl.ds(part * PART, PART)
        return pltpu.make_async_copy(
            stage_ref.at[a, :, cols], refs[a].at[:, cols], sem.at[a, part]
        )

    spot = block_ids()
    for part in range(PARTS):

        def step(i, carry):
            at = part * (64 // PARTS) + i
            cols = pl.ds(pl.multiple_of(at * PIECE, PIECE), PIECE)
            tiles = [x_ref[4 * (at % 8) + k, at // 8].astype(F32) for k in range(4)]
            for a in range(4):
                mixed = tiles[(3 - a) % 4]
                for pos in range(3):
                    mixed = jnp.where(spot == pos, tiles[(pos - a) % 4], mixed)
                if a:
                    mixed = pltpu.roll(mixed, PIECE - OWN * a, 1)
                stage_ref[a, :, cols] = mixed.astype(BF16)
            return carry

        lax.fori_loop(0, 64 // PARTS, step, 0, unroll=64 // PARTS)
        for a in range(4):
            copy(a, part).start()
    place_sums(here_ref[0], parts_ref, tapv_ref, skipv_ref)
    taps_out = pltpu.make_async_copy(tapv_ref, taps_ref, small_sem.at[0])
    skip_out = pltpu.make_async_copy(skipv_ref, skip_ref, small_sem.at[1])
    taps_out.start()
    skip_out.start()
    for part in range(PARTS):
        for a in range(4):
            copy(a, part).wait()
    taps_out.wait()
    skip_out.wait()


def split(values):
    high = values.astype(BF16)
    return high, (values - high.astype(F32)).astype(BF16)


def dot3(left, right):
    def dot(a, b):
        return jnp.dot(a, b, preferred_element_type=F32)

    return dot(left[0], right[0]) + (dot(left[1], right[0]) + dot(left[0], right[1]))


(M_ONE, M_TWO, L_ONE, L_TWO, FIRST, TAIL, NOTBEG, NEXTCONT, WHOLE) = range(9)


def begins_of(lens_ref):
    begins = [jnp.int32(0)]
    for k in range(NSEQ):
        begins.append(begins[-1] + lens_ref[k])
    return begins


def prep_kernel(
    lens_ref, here_ref, taps_ref, res_ref, pole_ref, gain_ref,
    plan_ref, mats_ref,
    prep_ref,
):
    mask_ref = plan_ref.at[0:MASKS]
    tapb_ref = plan_ref.at[MASKS:]
    here = here_ref[0]
    begins = begins_of(lens_ref)

    shape = (NPIECES, PIECE)
    base = lax.broadcasted_iota(jnp.int32, shape, 0) * PIECE
    row = base + lane_ids(shape)

    def count(ids, upto=NSEQ):
        total = jnp.zeros(shape, jnp.int32)
        for k in range(upto):
            total = total + (begins[k] <= ids).astype(jnp.int32)
        return total

    def starts(ids):
        hit = ids == begins[0]
        for k in range(1, NSEQ + 1):
            hit = hit | (ids == begins[k])
        return hit

    own = count(row)
    at_first, at_last, before = count(base), count(base + PIECE - 1), count(base - 1)
    here_start, prior_start = starts(row), starts(row - 1)
    next_start, after_start = starts(row + 1), starts(row + 2)
    one = jnp.ones(shape, F32)
    zero = jnp.zeros(shape, F32)
    mask_ref[0:32, :] = jnp.where(here_start, zero, one)
    mask_ref[32:64, :] = jnp.where(here_start | prior_start, zero, one)
    mask_ref[64:96, :] = jnp.where(next_start, zero, one)
    mask_ref[96:128, :] = jnp.where(next_start | after_start, zero, one)
    mask_ref[128:160, :] = jnp.where(own == at_first, one, zero)
    mask_ref[160:192, :] = jnp.where(own == at_last, one, zero)
    mask_ref[192:224, :] = jnp.where(at_first == before, one, zero)
    mask_ref[224:256, :] = jnp.where(starts(base + PIECE), zero, one)

    block = pl.ds(pl.multiple_of((here // 4) * 128, 128), 128)
    shift = lax.rem(128 - 32 * lax.rem(here, 4), 128)
    prep_ref[...] = jnp.zeros((PIECE, PIECE), F32)
    for a in range(3):
        for j in range(3):
            prep_ref[a * 3 + j : a * 3 + j + 1, :] = taps_ref[a, j : j + 1, block]
    prep_ref[9:10, :] = gain_ref[0:1, block]
    prep_ref[0:16, :] = pltpu.roll(prep_ref[0:16, :], shift, 1)
    prep_ref[16:18, 0:MODES] = pole_ref[pl.ds(2 * here, 2), :]
    prep_ref[24:26, 0:MODES] = res_ref[pl.ds(2 * here, 2), :]
    turned = prep_ref[...].T

    def column(rows, at):
        return jnp.broadcast_to(turned[0:rows, at : at + 1], (rows, PIECE))

    for j in range(3):
        for a in range(3):
            tapb_ref[j * 96 + a * OWN : j * 96 + (a + 1) * OWN, :] = column(OWN, a * 3 + j)
    tapb_ref[288 : 288 + OWN, :] = column(OWN, 9)
    pole = jnp.concatenate([column(MODES, 16), column(MODES, 17)], axis=0)
    residue = jnp.concatenate([column(MODES, 24), column(MODES, 25)], axis=0)
    weight = residue * jnp.sqrt(1.0 - pole * pole)
    lane = lane_ids((2 * MODES, PIECE))
    powers = jnp.ones((2 * MODES, PIECE), F32)
    falling = powers
    square = pole
    for bit in range(7):
        up = ((lane >> bit) & 1) == 1
        powers = jnp.where(up, powers * square, powers)
        falling = jnp.where(up, falling, falling * square)
        square = square * square
    rising = weight * (powers * pole)
    shrinking = weight * (falling * pole)
    taper = weight * powers

    sub_ids = lax.broadcasted_iota(jnp.int32, (PIECE, PIECE), 0)
    col_ids = lane_ids((PIECE, PIECE))
    mats_ref[...] = jnp.zeros(mats_ref.shape, BF16)
    for g in range(2):
        line = jnp.sum(taper[g * MODES : (g + 1) * MODES], axis=0, keepdims=True)
        spread = pltpu.roll(
            jnp.broadcast_to(line, (PIECE, PIECE)), 0, 1, stride=1, stride_axis=0
        )
        toeplitz = jnp.where(col_ids >= sub_ids, spread, 0.0)
        at = slice(g * PIECE, (g + 1) * PIECE)
        for start, square_tile in ((T_AHEAD, toeplitz), (T_BACK, toeplitz.T)):
            for part, tile in enumerate(split(square_tile)):
                top = start + part * 256 + g * PIECE
                mats_ref[top : top + PIECE, at] = tile
        for start, source in ((C_AHEAD, rising), (C_BACK, shrinking)):
            high, low = split(source[g * MODES : (g + 1) * MODES])
            for top, tile in ((0, high), (32, high), (64, low)):
                top = start + top + g * MODES
                mats_ref[top : top + MODES, at] = tile
    blank = jnp.zeros((32, PIECE), F32)
    fall_cols = jnp.concatenate([falling, falling, falling, blank], axis=0).T
    power_cols = jnp.concatenate([powers, powers, powers, blank], axis=0).T
    group_zero = (col_ids & 16) == 0
    for half, cols in enumerate((fall_cols, power_cols)):
        at = slice(half * PIECE, (half + 1) * PIECE)
        for part, tile in enumerate(split(cols)):
            wide = tile.astype(F32)
            top = E_BOTH + part * 256
            mats_ref[top : top + PIECE, at] = jnp.where(group_zero, wide, 0.0).astype(BF16)
            mats_ref[top + PIECE : top + 256, at] = jnp.where(group_zero, 0.0, wide).astype(BF16)
    leap = fall_cols[0:1, :] * fall_cols[126:127, :]
    mask_ref[256:288, :] = leap * jnp.where(at_first == at_last, one, zero)

def store_lhs(ref, at, values):
    for part, tile in enumerate(split(values)):
        ref[part, pl.ds(at, 16), 0:PIECE] = tile[0:16]
        ref[part, pl.ds(at, 16), PIECE:] = tile[16:32]


def main_kernel(
    meta_ref, x_ref, plan_ref, mats_ref,
    out_ref, g_ref,
    inv_ref, xt_ref, feat_ref, z_ref, gu_ref, lzf_ref, lgt_ref,
    u_ref, gz_ref, e_ref, h_ref, gs_ref, ys_ref, y_ref, acc_ref, sem,
):
    lens_ref = meta_ref
    here = meta_ref[NSEQ + NPIECES]
    turn = lax.rem(here, 4)

    def place(pos):
        return pl.ds(pl.multiple_of(lax.rem(pos + turn, 4) * OWN, OWN), OWN)

    def unplace(pos):
        return pl.ds(pl.multiple_of(lax.rem(pos + 4 - turn, 4) * OWN, OWN), OWN)

    xt_ref[NPIECES] = jnp.zeros((PIECE, PIECE), F32)
    gs_ref[NPIECES] = jnp.zeros((96, PIECE), F32)
    acc_ref[...] = jnp.zeros(acc_ref.shape, F32)

    def turn_in(s, carry):
        tile = x_ref[pl.ds(s * 8, 8)].reshape(PIECE, PIECE)
        tile = tile.T.astype(F32)
        for pos in range(4):
            xt_ref[s, unplace(pos), :] = tile[pos * OWN : (pos + 1) * OWN]
        return carry

    lax.fori_loop(0, NPIECES, turn_in, 0, unroll=CHUNK)
    begins = begins_of(lens_ref)
    inv_ref[0] = NPIECES

    def invert(s, carry):
        inv_ref[meta_ref[NSEQ + s] + 1] = s
        return carry

    lax.fori_loop(0, NPIECES, invert, 0, unroll=4)

    lane = lane_ids((OWN, PIECE))

    def mask(which, p):
        return plan_ref[pl.ds(which * NPIECES + p, 1), :]

    def part(a):
        return slice(a * OWN, (a + 1) * OWN)

    def tap(j, a):
        top = MASKS + j * 96 + a * OWN
        return plan_ref[top : top + OWN, :]

    def mats(top, depth, cols=slice(0, 256)):
        return mats_ref[top : top + depth, cols], mats_ref[top + depth : top + 2 * depth, cols]

    def ahead(chunk, carry):
        skip = jnp.zeros((OWN, PIECE), F32)
        for i in range(CHUNK):
            p = chunk * CHUNK + i
            slot, before = inv_ref[p + 1], inv_ref[p]
            feats = []
            for a in range(3):
                x = xt_ref[slot, part(a), :]
                prior = xt_ref[before, part(a), :]
                x_one = pltpu.roll(jnp.where(lane == PIECE - 1, prior, x), 1, 1)
                x_two = pltpu.roll(jnp.where(lane >= PIECE - 2, prior, x), 2, 1)
                feat = (
                    tap(0, a) * x
                    + mask(M_ONE, p) * (tap(1, a) * x_one)
                    + mask(M_TWO, p) * (tap(2, a) * x_two)
                )
                feat_ref[p, part(a), :] = feat
                feats.append(feat)
            z = feats[1] * feats[2]
            gu = xt_ref[slot, part(3), :] * feats[0]
            z_ref[p] = z
            gu_ref[p] = gu
            skip = skip + gu * z
            first = mask(FIRST, p)
            tail = mask(TAIL, p)
            at = pl.multiple_of(p * 16, 16)
            store_lhs(lzf_ref, at, z * first)
            store_lhs(lgt_ref, at, gu * tail)
        acc_ref[0, part(3), :] += skip
        return carry

    lax.fori_loop(0, NPIECES // CHUNK, ahead, 0)

    line = lane_ids((1, PIECE))
    extras = []
    for k in range(1, NSEQ):
        p = begins[k] // PIECE
        rows = p * PIECE + line
        inner = lax.rem(begins[k], PIECE) != 0
        later = (rows >= begins[k]) & (rows < begins[k + 1]) & inner
        sooner = (rows >= begins[k - 1]) & (rows < begins[k]) & inner
        later = jnp.where(later, 1.0, 0.0)
        sooner = jnp.where(sooner, 1.0, 0.0)
        extras.append((p, later, sooner, inner))
        store_lhs(lzf_ref, BASE + (k - 1) * 16, z_ref[p] * later)
        store_lhs(lgt_ref, BASE + (k - 1) * 16, gu_ref[p] * sooner)
    none = jnp.zeros((OWN, PIECE), F32)
    store_lhs(lzf_ref, VROWS - 16, none)
    store_lhs(lgt_ref, VROWS - 16, none)

    def both(ref):
        return ref[0], ref[1]

    e_ref[...] = dot3(both(lzf_ref), mats(E_BOTH, 256, slice(0, PIECE)))
    h_ref[...] = dot3(both(lgt_ref), mats(E_BOTH, 256, slice(PIECE, 256)))
    for ref, ks in ((e_ref, range(NSEQ - 1)), (h_ref, range(NSEQ - 2, -1, -1))):
        for k in ks:
            p, _, _, inner = extras[k]
            at = pl.ds(pl.multiple_of(p * 16, 16), 16)
            ref[at, :] = jnp.where(inner, ref[BASE + k * 16 : BASE + (k + 1) * 16, :], ref[at, :])

    def scan(step, carry):
        state, back = carry
        p = step
        at = pl.ds(pl.multiple_of(p * 16, 16), 16)
        found = e_ref[at, :]
        state = state * mask(NOTBEG, p)
        e_ref[at, :] = state
        state = found + mask(WHOLE, p) * state
        p = NPIECES - 1 - step
        at = pl.ds(pl.multiple_of(p * 16, 16), 16)
        found = h_ref[at, :]
        back = back * mask(NEXTCONT, p)
        h_ref[at, :] = back
        back = found + mask(WHOLE, p) * back
        return state, back

    idle = jnp.zeros((16, PIECE), F32)
    lax.fori_loop(0, NPIECES, scan, (idle, idle), unroll=8)

    def three(states):
        high = states.astype(BF16).astype(F32)
        lane = lane_ids(states.shape)
        low = (lane >= 32) & (lane < 64)
        return jnp.where(low, states - high, high).astype(BF16)

    u_ref[...] = dot3(both(lzf_ref), mats(T_AHEAD, 256))
    gz_ref[...] = dot3(both(lgt_ref), mats(T_BACK, 256))
    u_ref[0:BASE, :] += jnp.dot(three(e_ref[0:BASE, :]), mats_ref[C_AHEAD : C_AHEAD + PIECE, :], preferred_element_type=F32)
    gz_ref[0:BASE, :] += jnp.dot(three(h_ref[0:BASE, :]), mats_ref[C_BACK : C_BACK + PIECE, :], preferred_element_type=F32)
    for k, (p, later, sooner, _) in enumerate(extras):
        at = pl.ds(pl.multiple_of(p * 16, 16), 16)
        more = slice(BASE + k * 16, BASE + (k + 1) * 16)
        for ref, kept in ((u_ref, later), (gz_ref, sooner)):
            for half in (slice(0, PIECE), slice(PIECE, 2 * PIECE)):
                ref[at, half] = jnp.where(kept > 0.0, ref[more, half], ref[at, half])

    def gradients(p, carry):
        at = pl.ds(pl.multiple_of(p * 16, 16), 16)
        gain = tap(3, 0)
        u = jnp.concatenate([u_ref[at, 0:PIECE], u_ref[at, PIECE:]], axis=0)
        gz = jnp.concatenate([gz_ref[at, 0:PIECE], gz_ref[at, PIECE:]], axis=0)
        filtered = u + gain * z_ref[p]
        gz = gz + gain * gu_ref[p]
        ys_ref[p, place(0), :] = (feat_ref[p, part(0), :] * filtered).astype(BF16)
        gs_ref[p, part(0), :] = xt_ref[inv_ref[p + 1], part(3), :] * filtered
        gs_ref[p, part(1), :] = gz * feat_ref[p, part(2), :]
        gs_ref[p, part(2), :] = gz * feat_ref[p, part(1), :]
        return carry

    lax.fori_loop(0, NPIECES, gradients, 0, unroll=CHUNK)

    def behind(chunk, carry):
        for a in range(3):
            sums = [jnp.zeros((OWN, PIECE), F32) for _ in range(3)]
            for i in range(CHUNK):
                p = chunk * CHUNK + i
                grad = gs_ref[p, part(a), :]
                after = gs_ref[p + 1, part(a), :]
                x = xt_ref[inv_ref[p + 1], part(a), :]
                g_one = pltpu.roll(jnp.where(lane == 0, after, grad), PIECE - 1, 1)
                g_two = pltpu.roll(jnp.where(lane < 2, after, grad), PIECE - 2, 1)
                g_one = mask(L_ONE, p) * g_one
                g_two = mask(L_TWO, p) * g_two
                back = (
                    tap(0, a) * grad
                    + tap(1, a) * g_one
                    + tap(2, a) * g_two
                )
                ys_ref[p, place(a + 1), :] = back.astype(BF16)
                for j, g in enumerate((grad, g_one, g_two)):
                    sums[j] = sums[j] + g * x
            for j in range(3):
                acc_ref[j, part(a), :] += sums[j]
        return carry

    lax.fori_loop(0, NPIECES // CHUNK, behind, 0)

    norm = 1.0 / math.sqrt(TOKENS)
    g_ref[...] = jnp.zeros(g_ref.shape, F32)
    for j in range(3):
        g_ref[j : j + 1, :] = norm * jnp.sum(acc_ref[j].T, axis=0, keepdims=True)

    def send(part):
        rows = pl.ds(part * 64, 64)
        return pltpu.make_async_copy(y_ref.at[rows], out_ref.at[rows], sem.at[part])

    for part in range(4):

        def turn_out(i, carry):
            s = part * 8 + i
            tile = ys_ref[meta_ref[NSEQ + s]].T
            y_ref[pl.ds(s * 8, 8)] = tile.reshape(8, 16, PIECE)
            return carry

        lax.fori_loop(0, 8, turn_out, 0, unroll=8)
        send(part).start()
    for part in range(4):
        send(part).wait()


VM = pl.BlockSpec(memory_space=pltpu.VMEM)
SM = pl.BlockSpec(memory_space=pltpu.SMEM)
ANY = pl.BlockSpec(memory_space=pl.ANY)


def cost(flops, moved):
    return pl.CostEstimate(flops=flops, bytes_accessed=moved, transcendentals=0)


def run_pack(*arrays):
    blocks = pl.pallas_call(
        pack_kernel,
        out_shape=jax.ShapeDtypeStruct((32, 8, 16, 128), BF16),
        in_specs=[ANY] * 4,
        out_specs=ANY,
        scratch_shapes=[
            pltpu.VMEM((4, 16, 8192), BF16),
            pltpu.VMEM((32, 8, 16, 128), BF16),
            pltpu.SemaphoreType.DMA((4, PARTS)),
            pltpu.SemaphoreType.DMA((PARTS,)),
        ],
        name="pack",
    )(*arrays)
    return blocks.reshape(256, 16, 128)


def run_unpack(here, blocks, sums):
    return pl.pallas_call(
        unpack_kernel,
        out_shape=[jax.ShapeDtypeStruct((16, 8192), BF16)] * 4
        + [
            jax.ShapeDtypeStruct((3, 3, 1024), F32),
            jax.ShapeDtypeStruct((1, 1024), F32),
        ],
        in_specs=[SM, VM, VM],
        out_specs=[ANY] * 6,
        scratch_shapes=[
            pltpu.VMEM((4, 16, 8192), BF16),
            pltpu.VMEM((3, 3, 1024), F32),
            pltpu.VMEM((1, 1024), F32),
            pltpu.SemaphoreType.DMA((4, PARTS)),
            pltpu.SemaphoreType.DMA((2,)),
        ],
        compiler_params=pltpu.CompilerParams(vmem_limit_bytes=24 << 20),
        name="unpack",
    )(here, blocks.reshape(32, 8, 16, 128), sums)


def run_prep(lens, here, taps, residues, poles, gain):
    shapes = [((PLAN_ROWS, PIECE), F32), ((MAT_ROWS, 256), BF16)]
    return pl.pallas_call(
        prep_kernel,
        out_shape=[jax.ShapeDtypeStruct(*shape) for shape in shapes],
        in_specs=[SM, SM, VM, VM, VM, VM],
        out_specs=[VM] * 2,
        scratch_shapes=[pltpu.VMEM((PIECE, PIECE), F32)],
        cost_estimate=cost(4_000_000, 1 << 20),
        name="prep",
    )(lens, here, taps, residues, poles, gain)


def run_main(meta, blocks, plan, mats):
    scratch = [
        pltpu.SMEM((NPIECES + 1,), jnp.int32),
        pltpu.VMEM((NPIECES + 1, PIECE, PIECE), F32),
        pltpu.VMEM((NPIECES, 96, PIECE), F32),
        pltpu.VMEM((NPIECES, OWN, PIECE), F32),
        pltpu.VMEM((NPIECES, OWN, PIECE), F32),
        pltpu.VMEM((2, VROWS, 256), BF16),
        pltpu.VMEM((2, VROWS, 256), BF16),
        pltpu.VMEM((VROWS, 256), F32),
        pltpu.VMEM((VROWS, 256), F32),
        pltpu.VMEM((VROWS, PIECE), F32),
        pltpu.VMEM((VROWS, PIECE), F32),
        pltpu.VMEM((NPIECES + 1, 96, PIECE), F32),
        pltpu.VMEM((NPIECES, PIECE, PIECE), BF16),
        pltpu.VMEM((256, 16, 128), BF16),
        pltpu.VMEM((3, PIECE, PIECE), F32),
        pltpu.SemaphoreType.DMA((4,)),
    ]
    return pl.pallas_call(
        main_kernel,
        out_shape=[
            jax.ShapeDtypeStruct((256, 16, 128), BF16),
            jax.ShapeDtypeStruct((8, 128), F32),
        ],
        in_specs=[SM, VM, VM, VM],
        out_specs=[ANY, VM],
        scratch_shapes=scratch,
        compiler_params=pltpu.CompilerParams(vmem_limit_bytes=LIMIT_MB << 20),
        name="block",
    )(meta, blocks, plan, mats)


def exchange(blocks):
    return lax.all_to_all(blocks, BOTH, split_axis=0, concat_axis=0, tiled=True)


def gather_sums(sums):
    held = sums[None]
    for flips in ((8, 16, 24), (1, 2, 3), (4,)):
        got = [held]
        for flip in flips:
            pairs = [(i, i ^ flip) for i in range(32)]
            got.append(lax.ppermute(held, "ctx", pairs))
        held = jnp.concatenate(got, axis=0)
    return held


def local(
    gate_rows,
    key_rows,
    value_rows,
    out_grad,
    conv_taps,
    filter_residues,
    filter_poles,
    skip_gain,
    seq_lengths,
    piece_list,
):
    here = lax.axis_index("ctx").astype(jnp.int32).reshape(1)
    blocks = exchange(run_pack(gate_rows, key_rows, value_rows, out_grad))
    plan, mats = run_prep(
        seq_lengths,
        here,
        conv_taps,
        filter_residues,
        filter_poles,
        skip_gain.reshape(1, -1),
    )
    plan = jnp.pad(plan, ((0, 8), (0, 0)))
    mats = jnp.pad(mats, ((0, 16), (0, 0)))
    meta = jnp.concatenate([seq_lengths, piece_list, here])
    results, sums = run_main(meta, blocks, plan, mats)
    *outs, taps_grad, skip_grad = run_unpack(here, exchange(results), gather_sums(sums))
    return (*outs, taps_grad, skip_grad.reshape(1024))


def solution(mesh):
    rows = P(BOTH, None)
    return jax.shard_map(
        local,
        mesh=mesh,
        in_specs=(
            rows, rows, rows, rows,
            P(None, None, "mp"), P("mp", None), P("mp", None), P("mp"), P(), P(),
        ),
        out_specs=(rows, rows, rows, rows, P(None, None, "mp"), P("mp")),
        check_vma=False,
    )
```

time: 123 us -> 97.5 us (0.79)
  waiting for transfers between devices: 59.5 us -> 44.2 us
  local copies, waits for them, and re-layouts: 10.9 us -> 3.68 us
  Pallas kernels: 16 us -> 12.9 us
    ppermute x5 -> x7, waiting for transfers between devices: 32 us -> 19.3 us  [gather_sums(): got.append(lax.ppermute(held, 'ctx', pairs))]
    unnamed x34 -> x16, local copies, waits for them, and re-layouts: 10.9 us -> 1.43 us
    all_to_all x2, waiting for transfers between devices: 27.5 us -> 25 us  [exchange(): return lax.all_to_all(blocks, BOTH, split_axis=0, concat_axis=0, tiled=True)]
    pad x0 -> x2, local copies, waits for them, and re-layouts: none -> 2.24 us  [the longest x1 1.25 us: local(): mats = jnp.pad(mats, ((0, 16), (0, 0)))]
    pallas_call x2 -> x1, Pallas kernels: 4.32 us -> 2.44 us  [run_pack(): pl.pallas_call(pack_kernel, out_shape=jax.ShapeDtypeStruct((32, 8, 16, 12...]
    ppermute x5 -> x7, starting transfers between devices: 13.3 us -> 14.1 us  [gather_sums(): got.append(lax.ppermute(held, 'ctx', pairs))]
  transfers between devices with their start and end apart: 7 -> 9, of which waited for: 6 -> 6; matrix products, arithmetic and copies ran while one was open for 1% -> 4% of each run, Pallas kernels for 3% -> 2%
where the time goes in v3:
time: 97.5 us; the launch traced here: 96.5 us
  waiting for transfers between devices  44.2 us (45%)
  starting transfers between devices  34.9 us (36%)
  Pallas kernels  12.9 us (13%)
  local copies, waits for them, and re-layouts  3.68 us (4%)
    all_to_all x2, waiting for transfers between devices, exchange(): return lax.all_to_all(blocks, BOTH, split_axis=0, concat_axis=0, tiled=True)  25 us
    all_to_all x2, starting transfers between devices, exchange(): return lax.all_to_all(blocks, BOTH, split_axis=0, concat_axis=0, tiled=True)  20.8 us
    ppermute x7, waiting for transfers between devices, gather_sums(): got.append(lax.ppermute(held, 'ctx', pairs))  19.3 us
    ppermute x7, starting transfers between devices, gather_sums(): got.append(lax.ppermute(held, 'ctx', pairs))  14.1 us
    pallas_call x1, Pallas kernels, run_main(): pl.pallas_call(main_kernel, out_shape=[jax.ShapeDtypeStruct((256, 16, 128...  6.64 us
    pallas_call x1, Pallas kernels, run_pack(): pl.pallas_call(pack_kernel, out_shape=jax.ShapeDtypeStruct((32, 8, 16, 12...  2.44 us
    pallas_call x1, Pallas kernels, run_prep(): pl.pallas_call(prep_kernel, out_shape=[jax.ShapeDtypeStruct(*shape) for s...  2.39 us
  transfers between devices with their start and end apart: 9, of which 6 were waited for; matrix products, arithmetic and copies ran while one was open for 4% of the time, Pallas kernels for 2%

profile of v3, /device:TPU:8, one launch (start us, length us, event | category | flops | bytes accessed | tf_op | source)
XLA Modules:
  0.0 96.5 jit_solution(14628431720305656961)
XLA Ops:
  0.6 2.4 %pack.1 = bf16[32,8,16,128]{3,2,1,0:T(8,128)(2,1)} custom-call(bf16[16,8192]{1,0:T(8,128)(2,1)} %a_ref.1, bf16[16,8192]{1,0:T(8,128)(2,1)} %b_ref.1, bf16[16,8192]{1,0:T(8,128)(2,1)} %c_ref.1, bf16[16,8192]{1,0:T(8,128)(2,1)} %d_ref.1), custom_call_target="tpu_custom_call" | custom-call | tf_op jit(solution)/shard_map/pack/pallas_call | solution.py:513
  3.1 0.0 copy-start
  3.1 14.6 %all-to-all-start = ((bf16[256,16,128]{2,1,0:T(8,128)(2,1)}), bf16[256,16,128]{2,1,0:T(8,128)(2,1)S(1)}, u32[]{:S(2)}, u32[]{:S(2)}) async-start(bf16[256,16,128]{2,1,0:T(8,128)(2,1)} %bitcast.13), calls=%async_computation | async-start | bytes 2097152 | tf_op jit(solution)/shard_map/all_to_all | solution.py:598
  17.7 0.0 copy-done
  17.7 0.0 copy-start.1
  17.7 0.7 copy.16.res_ref
  18.4 0.0 copy-done.1
  18.4 0.7 copy.17.pole_ref
  19.1 2.4 %prep.1 = (f32[608,128]{1,0:T(8,128)}, bf16[1792,256]{1,0:T(8,128)(2,1)}) custom-call(s32[8]{0:T(128)} %lens_ref.1, s32[1]{0:T(128)} %bitcast.here_ref, f32[3,3,1024]{2,1,0:T(4,128)} %taps_ref.1, f32[64,16]{1,0:T(8,128)} %copy.16.res_ref, f32[64,16]{1,0:T(8,128)} %copy.17.pole_ref, f32[1,1024]{1,0:T(1,128)} %bitcast.14), custom_call_target="tpu_custom_call" | custom-call | flops 4000000 | bytes 1048576 | tf_op jit(solution)/shard_map/prep/pallas_call | solution.py:553
  21.5 1.0 %pad.8.plan_ref = f32[616,128]{1,0:T(8,128)S(1)} pad(f32[608,128]{1,0:T(8,128)} %get-tuple-element.16, f32[]{:T(128)} %constant.9.clone.1), padding=0_8x0_0 | pad | bytes 626692 | tf_op jit(solution)/shard_map/jit(_pad)/pad | solution.py:634
  22.5 0.0 copy-start.2
  22.5 0.0 copy-start.3
  22.5 1.2 %pad.9.mats_ref = bf16[1808,256]{1,0:T(8,128)(2,1)S(1)} pad(bf16[1792,256]{1,0:T(8,128)(2,1)} %get-tuple-element.17, bf16[]{:T(256)} %constant.10.clone.1), padding=0_16x0_0 | pad | bytes 1843202 | tf_op jit(solution)/shard_map/jit(_pad)/pad | solution.py:635
  23.8 0.0 copy-done.2
  23.8 0.0 copy-done.3
  23.8 0.1 pad_add_fusion.meta_ref
  23.9 25.0 %all-to-all-done.x_ref = bf16[256,16,128]{2,1,0:T(8,128)(2,1)S(1)} async-done(((bf16[256,16,128]{2,1,0:T(8,128)(2,1)}), bf16[256,16,128]{2,1,0:T(8,128)(2,1)S(1)}, u32[]{:S(2)}, u32[]{:S(2)}) %all-to-all-start) | async-done | bytes 1048608 | tf_op jit(solution)/shard_map/all_to_all | solution.py:598
  48.9 6.6 %block.1 = (bf16[256,16,128]{2,1,0:T(8,128)(2,1)}, f32[8,128]{1,0:T(8,128)S(1)}) custom-call(s32[41]{0:T(128)S(1)} %pad_add_fusion.meta_ref, bf16[256,16,128]{2,1,0:T(8,128)(2,1)S(1)} %all-to-all-done.x_ref, f32[616,128]{1,0:T(8,128)S(1)} %pad.8.plan_ref, bf16[1808,256]{1,0:T(8,128)(2,1)S(1)} %pad.9.mats_ref), custom_call_target="tpu_custom_call" | custom-call | tf_op jit(solution)/shard_map/block/pallas_call | solution.py:583
  55.5 6.2 %all-to-all-start.1 = ((bf16[256,16,128]{2,1,0:T(8,128)(2,1)}), bf16[256,16,128]{2,1,0:T(8,128)(2,1)S(1)}, u32[]{:S(2)}, u32[]{:S(2)}) async-start(bf16[256,16,128]{2,1,0:T(8,128)(2,1)} %get-tuple-element.18), calls=%async_computation.1 | async-start | bytes 2097152 | tf_op jit(solution)/shard_map/all_to_all | solution.py:598
  61.8 2.8 %collective-permute-start.2 = (f32[1,8,128]{2,1,0:T(8,128)S(1)}, f32[1,8,128]{2,1,0:T(8,128)S(1)}, u32[]{:S(2)}, u32[]{:S(2)}) collective-permute-start(f32[1,8,128]{2,1,0:T(8,128)S(1)} %bitcast.9), channel_id=1, source_target_pairs={{0,192},{8,200},{16,208},{24,216},{32,224},{40,232},{48,240},{56,2... | collective-permute-start | bytes 12296 | tf_op jit(solution)/shard_map/ppermute | solution.py:607
  64.5 0.9 collective-permute-start.1
  65.4 0.6 collective-permute-start
  66.0 0.7 collective-permute-done.2
  66.7 3.0 %collective-permute-done.1 = f32[1,8,128]{2,1,0:T(8,128)S(1)} collective-permute-done((f32[1,8,128]{2,1,0:T(8,128)S(1)}, f32[1,8,128]{2,1,0:T(8,128)S(1)}, u32[]{:S(2)}, u32[]{:S(2)}) %collective-permute-start.1) | collective-permute-done | bytes 4128 | tf_op jit(solution)/shard_map/ppermute | solution.py:607
  69.7 0.0 collective-permute-done
  69.7 4.0 %collective-permute-start.5 = (f32[4,8,128]{2,1,0:T(8,128)S(1)}, f32[4,8,128]{2,1,0:T(8,128)S(1)}, u32[]{:S(2)}, u32[]{:S(2)}) collective-permute-start(f32[4,8,128]{2,1,0:T(8,128)S(1)} %pad_maximum_fusion), channel_id=1, source_target_pairs={{0,24},{8,16},{16,8},{24,0},{32,56},{40,48},{48,40},{56,32},{64,88... | collective-permute-start | bytes 49160 | tf_op jit(solution)/shard_map/ppermute | solution.py:607
  73.7 0.0 collective-permute-start.4
  73.7 0.7 collective-permute-start.3
  74.4 11.4 %collective-permute-done.3 = f32[4,8,128]{2,1,0:T(8,128)S(1)} collective-permute-done((f32[4,8,128]{2,1,0:T(8,128)S(1)}, f32[4,8,128]{2,1,0:T(8,128)S(1)}, u32[]{:S(2)}, u32[]{:S(2)}) %collective-permute-start.3) | collective-permute-done | bytes 16416 | tf_op jit(solution)/shard_map/ppermute | solution.py:607
  85.8 1.1 %collective-permute-done.4 = f32[4,8,128]{2,1,0:T(8,128)S(1)} collective-permute-done((f32[4,8,128]{2,1,0:T(8,128)S(1)}, f32[4,8,128]{2,1,0:T(8,128)S(1)}, u32[]{:S(2)}, u32[]{:S(2)}) %collective-permute-start.4) | collective-permute-done | bytes 16416 | tf_op jit(solution)/shard_map/ppermute | solution.py:607
  86.9 0.0 collective-permute-done.5
  86.9 5.2 %collective-permute-start.6 = (f32[16,8,128]{2,1,0:T(8,128)S(1)}, f32[16,8,128]{2,1,0:T(8,128)S(1)}, u32[]{:S(2)}, u32[]{:S(2)}) collective-permute-start(f32[16,8,128]{2,1,0:T(8,128)S(1)} %get-tuple-element.26), channel_id=1, source_target_pairs={{0,32},{8,40},{16,48},{24,56},{32,0},{40,8},{48,16},{56,24},{64,96... | collective-permute-start | bytes 196616 | tf_op jit(solution)/shard_map/ppermute | solution.py:607
  92.1 3.0 %collective-permute-done.6 = f32[16,8,128]{2,1,0:T(8,128)S(1)} collective-permute-done((f32[16,8,128]{2,1,0:T(8,128)S(1)}, f32[16,8,128]{2,1,0:T(8,128)S(1)}, u32[]{:S(2)}, u32[]{:S(2)}) %collective-permute-start.6) | collective-permute-done | bytes 65568 | tf_op jit(solution)/shard_map/ppermute | solution.py:607
  95.1 0.0 all-to-all-done.1
  95.1 1.4 %unpack.1 = (bf16[16,8192]{1,0:T(8,128)(2,1)}, bf16[16,8192]{1,0:T(8,128)(2,1)}, bf16[16,8192]{1,0:T(8,128)(2,1)}, bf16[16,8192]{1,0:T(8,128)(2,1)}, f32[3,3,1024]{2,1,0:T(4,128)}, /*index=5*/f32[1,1024]{1,0:T(1,128)}) custom-call(s32[1]{0:T(128)} %bitcast.here_ref, bf16[32,8,16,128]{3,2,1,0:T(8,128)(2,1)S(1)} %bitcast.8, ...), custom_call_target="tpu_custom_call" | custom-call | tf_op jit(solution)/shard_map/unpack/pallas_call | solution.py:530
  (9 shorter events, 0.0 us)
Async XLA Ops:
  3.1 14.6 %copy-start = (f32[64,16]{0,1:T(8,128)S(1)}, f32[64,16]{0,1:T(8,128)}, u32[]{:S(2)}) copy-start(f32[64,16]{0,1:T(8,128)} %param.15) | copy-start | bytes 12292
  3.1 45.8 %all-to-all-start = ((bf16[256,16,128]{2,1,0:T(8,128)(2,1)}), bf16[256,16,128]{2,1,0:T(8,128)(2,1)S(1)}, u32[]{:S(2)}, u32[]{:S(2)}) async-start(bf16[256,16,128]{2,1,0:T(8,128)(2,1)} %bitcast.13), calls=%async_computation | async-start | bytes 2097152 | tf_op jit(solution)/shard_map/all_to_all | solution.py:598
  17.7 0.7 copy-start.1
  22.5 1.3 %copy-start.2 = (s32[8]{0:T(128)S(1)}, s32[8]{0:T(128)}, u32[]{:S(2)}) copy-start(s32[8]{0:T(128)} %lens_ref.1) | copy-start | bytes 100
  22.5 1.3 %copy-start.3 = (s32[32]{0:T(128)S(1)}, s32[32]{0:T(128)}, u32[]{:S(2)}) copy-start(s32[32]{0:T(128)} %param.19) | copy-start | bytes 388
  55.5 39.6 %all-to-all-start.1 = ((bf16[256,16,128]{2,1,0:T(8,128)(2,1)}), bf16[256,16,128]{2,1,0:T(8,128)(2,1)S(1)}, u32[]{:S(2)}, u32[]{:S(2)}) async-start(bf16[256,16,128]{2,1,0:T(8,128)(2,1)} %get-tuple-element.18), calls=%async_computation.1 | async-start | bytes 2097152 | tf_op jit(solution)/shard_map/all_to_all | solution.py:598
  61.8 4.9 %collective-permute-start.2 = (f32[1,8,128]{2,1,0:T(8,128)S(1)}, f32[1,8,128]{2,1,0:T(8,128)S(1)}, u32[]{:S(2)}, u32[]{:S(2)}) collective-permute-start(f32[1,8,128]{2,1,0:T(8,128)S(1)} %bitcast.9), channel_id=1, source_target_pairs={{0,192},{8,200},{16,208},{24,216},{32,224},{40,232},{48,240},{56,2... | collective-permute-start | bytes 12296 | tf_op jit(solution)/shard_map/ppermute | solution.py:607
  64.5 5.2 %collective-permute-start.1 = (f32[1,8,128]{2,1,0:T(8,128)S(1)}, f32[1,8,128]{2,1,0:T(8,128)S(1)}, u32[]{:S(2)}, u32[]{:S(2)}) collective-permute-start(f32[1,8,128]{2,1,0:T(8,128)S(1)} %bitcast.10), channel_id=1, source_target_pairs={{0,128},{8,136},{16,144},{24,152},{32,160},{40,168},{48,176},{56,1... | collective-permute-start | bytes 12296 | tf_op jit(solution)/shard_map/ppermute | solution.py:607
  65.4 4.3 %collective-permute-start = (f32[1,8,128]{2,1,0:T(8,128)S(1)}, f32[1,8,128]{2,1,0:T(8,128)S(1)}, u32[]{:S(2)}, u32[]{:S(2)}) collective-permute-start(f32[1,8,128]{2,1,0:T(8,128)S(1)} %bitcast.11), channel_id=1, source_target_pairs={{0,64},{8,72},{16,80},{24,88},{32,96},{40,104},{48,112},{56,120},{... | collective-permute-start | bytes 12296 | tf_op jit(solution)/shard_map/ppermute | solution.py:607
  69.7 17.2 %collective-permute-start.5 = (f32[4,8,128]{2,1,0:T(8,128)S(1)}, f32[4,8,128]{2,1,0:T(8,128)S(1)}, u32[]{:S(2)}, u32[]{:S(2)}) collective-permute-start(f32[4,8,128]{2,1,0:T(8,128)S(1)} %pad_maximum_fusion), channel_id=1, source_target_pairs={{0,24},{8,16},{16,8},{24,0},{32,56},{40,48},{48,40},{56,32},{64,88... | collective-permute-start | bytes 49160 | tf_op jit(solution)/shard_map/ppermute | solution.py:607
  73.7 13.2 %collective-permute-start.4 = (f32[4,8,128]{2,1,0:T(8,128)S(1)}, f32[4,8,128]{2,1,0:T(8,128)S(1)}, u32[]{:S(2)}, u32[]{:S(2)}) collective-permute-start(f32[4,8,128]{2,1,0:T(8,128)S(1)} %pad_maximum_fusion), channel_id=1, source_target_pairs={{0,16},{8,24},{16,0},{24,8},{32,48},{40,56},{48,32},{56,40},{64,80... | collective-permute-start | bytes 49160 | tf_op jit(solution)/shard_map/ppermute | solution.py:607
  73.7 12.1 %collective-permute-start.3 = (f32[4,8,128]{2,1,0:T(8,128)S(1)}, f32[4,8,128]{2,1,0:T(8,128)S(1)}, u32[]{:S(2)}, u32[]{:S(2)}) collective-permute-start(f32[4,8,128]{2,1,0:T(8,128)S(1)} %pad_maximum_fusion), channel_id=1, source_target_pairs={{0,8},{8,0},{16,24},{24,16},{32,40},{40,32},{48,56},{56,48},{64,72... | collective-permute-start | bytes 49160 | tf_op jit(solution)/shard_map/ppermute | solution.py:607
  86.9 8.3 %collective-permute-start.6 = (f32[16,8,128]{2,1,0:T(8,128)S(1)}, f32[16,8,128]{2,1,0:T(8,128)S(1)}, u32[]{:S(2)}, u32[]{:S(2)}) collective-permute-start(f32[16,8,128]{2,1,0:T(8,128)S(1)} %get-tuple-element.26), channel_id=1, source_target_pairs={{0,32},{8,40},{16,48},{24,56},{32,0},{40,8},{48,16},{56,24},{64,96... | collective-permute-start | bytes 196616 | tf_op jit(solution)/shard_map/ppermute | solution.py:607

commit v4 on v3

--- a/solution.py
+++ b/solution.py
@@ -156,10 +156,9 @@
 
 
 def dot3(left, right):
-    def dot(a, b):
-        return jnp.dot(a, b, preferred_element_type=F32)
-
-    return dot(left[0], right[0]) + (dot(left[1], right[0]) + dot(left[0], right[1]))
+    left = jnp.concatenate([left[0], left[1], left[0]], axis=1)
+    right = jnp.concatenate([right[0], right[0], right[1]], axis=0)
+    return jnp.dot(left, right, preferred_element_type=F32)
 
 
 (M_ONE, M_TWO, L_ONE, L_TWO, FIRST, TAIL, NOTBEG, NEXTCONT, WHOLE) = range(9)
@@ -287,6 +286,12 @@
         ref[part, pl.ds(at, 16), PIECE:] = tile[16:32]
 
 
+def unrolled(count, body, carry):
+    for i in range(count):
+        carry = body(i, carry)
+    return carry
+
+
 def main_kernel(
     meta_ref, x_ref, plan_ref, mats_ref,
     out_ref, g_ref,
@@ -314,7 +319,7 @@
             xt_ref[s, unplace(pos), :] = tile[pos * OWN : (pos + 1) * OWN]
         return carry
 
-    lax.fori_loop(0, NPIECES, turn_in, 0, unroll=CHUNK)
+    unrolled(NPIECES, turn_in, 0)
     begins = begins_of(lens_ref)
     inv_ref[0] = NPIECES
 
@@ -340,37 +345,34 @@
         return mats_ref[top : top + depth, cols], mats_ref[top + depth : top + 2 * depth, cols]
 
     def ahead(chunk, carry):
-        skip = jnp.zeros((OWN, PIECE), F32)
-        for i in range(CHUNK):
-            p = chunk * CHUNK + i
-            slot, before = inv_ref[p + 1], inv_ref[p]
-            feats = []
-            for a in range(3):
-                x = xt_ref[slot, part(a), :]
-                prior = xt_ref[before, part(a), :]
+        pieces = range(chunk * CHUNK, (chunk + 1) * CHUNK)
+        slots = [inv_ref[p] for p in range(chunk * CHUNK, (chunk + 1) * CHUNK + 1)]
+        for a in range(3):
+            taps = [tap(j, a) for j in range(3)]
+            prior = xt_ref[slots[0], part(a), :]
+            for i, p in enumerate(pieces):
+                x = xt_ref[slots[i + 1], part(a), :]
                 x_one = pltpu.roll(jnp.where(lane == PIECE - 1, prior, x), 1, 1)
                 x_two = pltpu.roll(jnp.where(lane >= PIECE - 2, prior, x), 2, 1)
-                feat = (
-                    tap(0, a) * x
-                    + mask(M_ONE, p) * (tap(1, a) * x_one)
-                    + mask(M_TWO, p) * (tap(2, a) * x_two)
+                feat_ref[p, part(a), :] = (
+                    taps[0] * x
+                    + mask(M_ONE, p) * (taps[1] * x_one)
+                    + mask(M_TWO, p) * (taps[2] * x_two)
                 )
-                feat_ref[p, part(a), :] = feat
-                feats.append(feat)
-            z = feats[1] * feats[2]
-            gu = xt_ref[slot, part(3), :] * feats[0]
+                prior = x
+        skip = jnp.zeros((OWN, PIECE), F32)
+        for i, p in enumerate(pieces):
+            z = feat_ref[p, part(1), :] * feat_ref[p, part(2), :]
+            gu = xt_ref[slots[i + 1], part(3), :] * feat_ref[p, part(0), :]
             z_ref[p] = z
             gu_ref[p] = gu
             skip = skip + gu * z
-            first = mask(FIRST, p)
-            tail = mask(TAIL, p)
-            at = pl.multiple_of(p * 16, 16)
-            store_lhs(lzf_ref, at, z * first)
-            store_lhs(lgt_ref, at, gu * tail)
+            store_lhs(lzf_ref, p * 16, z * mask(FIRST, p))
+            store_lhs(lgt_ref, p * 16, gu * mask(TAIL, p))
         acc_ref[0, part(3), :] += skip
         return carry
 
-    lax.fori_loop(0, NPIECES // CHUNK, ahead, 0)
+    unrolled(NPIECES // CHUNK, ahead, 0)
 
     line = lane_ids((1, PIECE))
     extras = []
@@ -403,13 +405,13 @@
     def scan(step, carry):
         state, back = carry
         p = step
-        at = pl.ds(pl.multiple_of(p * 16, 16), 16)
+        at = pl.ds(p * 16, 16)
         found = e_ref[at, :]
         state = state * mask(NOTBEG, p)
         e_ref[at, :] = state
         state = found + mask(WHOLE, p) * state
         p = NPIECES - 1 - step
-        at = pl.ds(pl.multiple_of(p * 16, 16), 16)
+        at = pl.ds(p * 16, 16)
         found = h_ref[at, :]
         back = back * mask(NEXTCONT, p)
         h_ref[at, :] = back
@@ -417,7 +419,7 @@
         return state, back
 
     idle = jnp.zeros((16, PIECE), F32)
-    lax.fori_loop(0, NPIECES, scan, (idle, idle), unroll=8)
+    unrolled(NPIECES, scan, (idle, idle))
 
     def three(states):
         high = states.astype(BF16).astype(F32)
@@ -437,7 +439,7 @@
                 ref[at, half] = jnp.where(kept > 0.0, ref[more, half], ref[at, half])
 
     def gradients(p, carry):
-        at = pl.ds(pl.multiple_of(p * 16, 16), 16)
+        at = pl.ds(p * 16, 16)
         gain = tap(3, 0)
         u = jnp.concatenate([u_ref[at, 0:PIECE], u_ref[at, PIECE:]], axis=0)
         gz = jnp.concatenate([gz_ref[at, 0:PIECE], gz_ref[at, PIECE:]], axis=0)
@@ -449,38 +451,30 @@
         gs_ref[p, part(2), :] = gz * feat_ref[p, part(1), :]
         return carry
 
-    lax.fori_loop(0, NPIECES, gradients, 0, unroll=CHUNK)
+    unrolled(NPIECES, gradients, 0)
 
     def behind(chunk, carry):
         for a in range(3):
+            taps = [tap(j, a) for j in range(3)]
             sums = [jnp.zeros((OWN, PIECE), F32) for _ in range(3)]
-            for i in range(CHUNK):
-                p = chunk * CHUNK + i
+            after = gs_ref[(chunk + 1) * CHUNK, part(a), :]
+            for p in reversed(range(chunk * CHUNK, (chunk + 1) * CHUNK)):
                 grad = gs_ref[p, part(a), :]
-                after = gs_ref[p + 1, part(a), :]
                 x = xt_ref[inv_ref[p + 1], part(a), :]
                 g_one = pltpu.roll(jnp.where(lane == 0, after, grad), PIECE - 1, 1)
                 g_two = pltpu.roll(jnp.where(lane < 2, after, grad), PIECE - 2, 1)
                 g_one = mask(L_ONE, p) * g_one
                 g_two = mask(L_TWO, p) * g_two
-                back = (
-                    tap(0, a) * grad
-                    + tap(1, a) * g_one
-                    + tap(2, a) * g_two
-                )
+                back = taps[0] * grad + taps[1] * g_one + taps[2] * g_two
                 ys_ref[p, place(a + 1), :] = back.astype(BF16)
                 for j, g in enumerate((grad, g_one, g_two)):
                     sums[j] = sums[j] + g * x
+                after = grad
             for j in range(3):
                 acc_ref[j, part(a), :] += sums[j]
         return carry
 
-    lax.fori_loop(0, NPIECES // CHUNK, behind, 0)
-
-    norm = 1.0 / math.sqrt(TOKENS)
-    g_ref[...] = jnp.zeros(g_ref.shape, F32)
-    for j in range(3):
-        g_ref[j : j + 1, :] = norm * jnp.sum(acc_ref[j].T, axis=0, keepdims=True)
+    unrolled(NPIECES // CHUNK, behind, 0)
 
     def send(part):
         rows = pl.ds(part * 64, 64)
@@ -494,8 +488,12 @@
             y_ref[pl.ds(s * 8, 8)] = tile.reshape(8, 16, PIECE)
             return carry
 
-        lax.fori_loop(0, 8, turn_out, 0, unroll=8)
+        unrolled(8, turn_out, 0)
         send(part).start()
+    norm = 1.0 / math.sqrt(TOKENS)
+    g_ref[3:4, :] = jnp.zeros((1, PIECE), F32)
+    for j in range(3):
+        g_ref[j : j + 1, :] = norm * jnp.sum(acc_ref[j].T, axis=0, keepdims=True)
     for part in range(4):
         send(part).wait()
 
@@ -584,7 +582,7 @@
         main_kernel,
         out_shape=[
             jax.ShapeDtypeStruct((256, 16, 128), BF16),
-            jax.ShapeDtypeStruct((8, 128), F32),
+            jax.ShapeDtypeStruct((4, 128), F32),
         ],
         in_specs=[SM, VM, VM, VM],
         out_specs=[ANY, VM],

time: 97.5 us -> 95 us (0.974)
  waiting for transfers between devices: 44.2 us -> 42.9 us
  Pallas kernels: 12.9 us -> 11.9 us
    ppermute x7, waiting for transfers between devices: 19.3 us -> 17.9 us  [gather_sums(): got.append(lax.ppermute(held, 'ctx', pairs))]
  transfers between devices with their start and end apart: 9 -> 9, of which waited for: 6 -> 7; matrix products, arithmetic and copies ran while one was open for 4% -> 4% of each run, Pallas kernels for 2% -> 3%
where the time goes in v4:
time: 95 us; the launch traced here: 94.4 us
  waiting for transfers between devices  42.9 us (45%)
  starting transfers between devices  35.1 us (37%)
  Pallas kernels  11.9 us (13%)
  local copies, waits for them, and re-layouts  3.72 us (4%)
    all_to_all x2, waiting for transfers between devices, exchange(): return lax.all_to_all(blocks, BOTH, split_axis=0, concat_axis=0, tiled=True)  25 us
    all_to_all x2, starting transfers between devices, exchange(): return lax.all_to_all(blocks, BOTH, split_axis=0, concat_axis=0, tiled=True)  20.8 us
    ppermute x7, waiting for transfers between devices, gather_sums(): got.append(lax.ppermute(held, 'ctx', pairs))  17.9 us
    ppermute x7, starting transfers between devices, gather_sums(): got.append(lax.ppermute(held, 'ctx', pairs))  14.2 us
    pallas_call x1, Pallas kernels, run_main(): pl.pallas_call(main_kernel, out_shape=[jax.ShapeDtypeStruct((256, 16, 128...  5.7 us
    pallas_call x1, Pallas kernels, run_pack(): pl.pallas_call(pack_kernel, out_shape=jax.ShapeDtypeStruct((32, 8, 16, 12...  2.44 us
    pallas_call x1, Pallas kernels, run_prep(): pl.pallas_call(prep_kernel, out_shape=[jax.ShapeDtypeStruct(*shape) for s...  2.39 us
  transfers between devices with their start and end apart: 9, of which 7 were waited for; matrix products, arithmetic and copies ran while one was open for 4% of the time, Pallas kernels for 3%

profile of v4, /device:TPU:8, one launch (start us, length us, event | category | flops | bytes accessed | tf_op | source)
XLA Modules:
  0.0 94.4 jit_solution(4871933369406003162)
XLA Ops:
  0.6 2.4 %pack.1 = bf16[32,8,16,128]{3,2,1,0:T(8,128)(2,1)} custom-call(bf16[16,8192]{1,0:T(8,128)(2,1)} %a_ref.1, bf16[16,8192]{1,0:T(8,128)(2,1)} %b_ref.1, bf16[16,8192]{1,0:T(8,128)(2,1)} %c_ref.1, bf16[16,8192]{1,0:T(8,128)(2,1)} %d_ref.1), custom_call_target="tpu_custom_call" | custom-call | tf_op jit(solution)/shard_map/pack/pallas_call | solution.py:511
  3.1 0.0 copy-start
  3.1 14.6 %all-to-all-start = ((bf16[256,16,128]{2,1,0:T(8,128)(2,1)}), bf16[256,16,128]{2,1,0:T(8,128)(2,1)S(1)}, u32[]{:S(2)}, u32[]{:S(2)}) async-start(bf16[256,16,128]{2,1,0:T(8,128)(2,1)} %bitcast.13), calls=%async_computation | async-start | bytes 2097152 | tf_op jit(solution)/shard_map/all_to_all | solution.py:596
  17.7 0.0 copy-done
  17.7 0.0 copy-start.1
  17.7 0.7 copy.16.res_ref
  18.4 0.0 copy-done.1
  18.4 0.7 copy.17.pole_ref
  19.1 2.4 %prep.1 = (f32[608,128]{1,0:T(8,128)}, bf16[1792,256]{1,0:T(8,128)(2,1)}) custom-call(s32[8]{0:T(128)} %lens_ref.1, s32[1]{0:T(128)} %bitcast.here_ref, f32[3,3,1024]{2,1,0:T(4,128)} %taps_ref.1, f32[64,16]{1,0:T(8,128)} %copy.16.res_ref, f32[64,16]{1,0:T(8,128)} %copy.17.pole_ref, f32[1,1024]{1,0:T(1,128)} %bitcast.14), custom_call_target="tpu_custom_call" | custom-call | flops 4000000 | bytes 1048576 | tf_op jit(solution)/shard_map/prep/pallas_call | solution.py:551
  21.5 1.0 %pad.8.plan_ref = f32[616,128]{1,0:T(8,128)S(1)} pad(f32[608,128]{1,0:T(8,128)} %get-tuple-element.16, f32[]{:T(128)} %constant.9.clone.1), padding=0_8x0_0 | pad | bytes 626692 | tf_op jit(solution)/shard_map/jit(_pad)/pad | solution.py:632
  22.5 0.0 copy-start.2
  22.5 0.0 copy-start.3
  22.5 1.2 %pad.9.mats_ref = bf16[1808,256]{1,0:T(8,128)(2,1)S(1)} pad(bf16[1792,256]{1,0:T(8,128)(2,1)} %get-tuple-element.17, bf16[]{:T(256)} %constant.10.clone.1), padding=0_16x0_0 | pad | bytes 1843202 | tf_op jit(solution)/shard_map/jit(_pad)/pad | solution.py:633
  23.8 0.0 copy-done.2
  23.8 0.0 copy-done.3
  23.8 0.1 pad_add_fusion.meta_ref
  23.9 25.0 %all-to-all-done.x_ref = bf16[256,16,128]{2,1,0:T(8,128)(2,1)S(1)} async-done(((bf16[256,16,128]{2,1,0:T(8,128)(2,1)}), bf16[256,16,128]{2,1,0:T(8,128)(2,1)S(1)}, u32[]{:S(2)}, u32[]{:S(2)}) %all-to-all-start) | async-done | bytes 1048608 | tf_op jit(solution)/shard_map/all_to_all | solution.py:596
  48.9 5.7 %block.1 = (bf16[256,16,128]{2,1,0:T(8,128)(2,1)}, f32[4,128]{1,0:T(4,128)S(1)}) custom-call(s32[41]{0:T(128)S(1)} %pad_add_fusion.meta_ref, bf16[256,16,128]{2,1,0:T(8,128)(2,1)S(1)} %all-to-all-done.x_ref, f32[616,128]{1,0:T(8,128)S(1)} %pad.8.plan_ref, bf16[1808,256]{1,0:T(8,128)(2,1)S(1)} %pad.9.mats_ref), custom_call_target="tpu_custom_call" | custom-call | tf_op jit(solution)/shard_map/block/pallas_call | solution.py:581
  54.6 6.2 %all-to-all-start.1 = ((bf16[256,16,128]{2,1,0:T(8,128)(2,1)}), bf16[256,16,128]{2,1,0:T(8,128)(2,1)S(1)}, u32[]{:S(2)}, u32[]{:S(2)}) async-start(bf16[256,16,128]{2,1,0:T(8,128)(2,1)} %get-tuple-element.18), calls=%async_computation.1 | async-start | bytes 2097152 | tf_op jit(solution)/shard_map/all_to_all | solution.py:596
  60.8 2.8 %collective-permute-start.2 = (f32[1,4,128]{2,1,0:T(4,128)S(1)}, f32[1,4,128]{2,1,0:T(4,128)S(1)}, u32[]{:S(2)}, u32[]{:S(2)}) collective-permute-start(f32[1,4,128]{2,1,0:T(4,128)S(1)} %bitcast.9), channel_id=1, source_target_pairs={{0,192},{8,200},{16,208},{24,216},{32,224},{40,232},{48,240},{56,2... | collective-permute-start | bytes 6152 | tf_op jit(solution)/shard_map/ppermute | solution.py:605
  63.6 0.9 collective-permute-start.1
  64.4 0.6 collective-permute-start
  65.0 0.7 collective-permute-done.2
  65.7 3.0 %collective-permute-done.1 = f32[1,4,128]{2,1,0:T(4,128)S(1)} collective-permute-done((f32[1,4,128]{2,1,0:T(4,128)S(1)}, f32[1,4,128]{2,1,0:T(4,128)S(1)}, u32[]{:S(2)}, u32[]{:S(2)}) %collective-permute-start.1) | collective-permute-done | bytes 2080 | tf_op jit(solution)/shard_map/ppermute | solution.py:605
  68.7 0.0 collective-permute-done
  68.7 4.1 %collective-permute-start.5 = (f32[4,4,128]{2,1,0:T(4,128)S(1)}, f32[4,4,128]{2,1,0:T(4,128)S(1)}, u32[]{:S(2)}, u32[]{:S(2)}) collective-permute-start(f32[4,4,128]{2,1,0:T(4,128)S(1)} %pad_maximum_fusion), channel_id=1, source_target_pairs={{0,24},{8,16},{16,8},{24,0},{32,56},{40,48},{48,40},{56,32},{64,88... | collective-permute-start | bytes 24584 | tf_op jit(solution)/shard_map/ppermute | solution.py:605
  72.8 0.0 collective-permute-start.4
  72.8 0.7 collective-permute-start.3
  73.5 11.1 %collective-permute-done.3 = f32[4,4,128]{2,1,0:T(4,128)S(1)} collective-permute-done((f32[4,4,128]{2,1,0:T(4,128)S(1)}, f32[4,4,128]{2,1,0:T(4,128)S(1)}, u32[]{:S(2)}, u32[]{:S(2)}) %collective-permute-start.3) | collective-permute-done | bytes 8224 | tf_op jit(solution)/shard_map/ppermute | solution.py:605
  84.6 0.1 collective-permute-done.4
  84.6 0.5 collective-permute-done.5
  85.2 5.3 %collective-permute-start.6 = (f32[16,4,128]{2,1,0:T(4,128)S(1)}, f32[16,4,128]{2,1,0:T(4,128)S(1)}, u32[]{:S(2)}, u32[]{:S(2)}) collective-permute-start(f32[16,4,128]{2,1,0:T(4,128)S(1)} %get-tuple-element.26), channel_id=1, source_target_pairs={{0,32},{8,40},{16,48},{24,56},{32,0},{40,8},{48,16},{56,24},{64,96... | collective-permute-start | bytes 98312 | tf_op jit(solution)/shard_map/ppermute | solution.py:605
  90.4 2.6 %collective-permute-done.6 = f32[16,4,128]{2,1,0:T(4,128)S(1)} collective-permute-done((f32[16,4,128]{2,1,0:T(4,128)S(1)}, f32[16,4,128]{2,1,0:T(4,128)S(1)}, u32[]{:S(2)}, u32[]{:S(2)}) %collective-permute-start.6) | collective-permute-done | bytes 32800 | tf_op jit(solution)/shard_map/ppermute | solution.py:605
  93.0 0.0 all-to-all-done.1
  93.0 1.4 %unpack.1 = (bf16[16,8192]{1,0:T(8,128)(2,1)}, bf16[16,8192]{1,0:T(8,128)(2,1)}, bf16[16,8192]{1,0:T(8,128)(2,1)}, bf16[16,8192]{1,0:T(8,128)(2,1)}, f32[3,3,1024]{2,1,0:T(4,128)}, /*index=5*/f32[1,1024]{1,0:T(1,128)}) custom-call(s32[1]{0:T(128)} %bitcast.here_ref, bf16[32,8,16,128]{3,2,1,0:T(8,128)(2,1)S(1)} %bitcast.8, ...), custom_call_target="tpu_custom_call" | custom-call | tf_op jit(solution)/shard_map/unpack/pallas_call | solution.py:528
  (9 shorter events, 0.1 us)
Async XLA Ops:
  3.1 14.6 %copy-start = (f32[64,16]{0,1:T(8,128)S(1)}, f32[64,16]{0,1:T(8,128)}, u32[]{:S(2)}) copy-start(f32[64,16]{0,1:T(8,128)} %param.15) | copy-start | bytes 12292
  3.1 45.8 %all-to-all-start = ((bf16[256,16,128]{2,1,0:T(8,128)(2,1)}), bf16[256,16,128]{2,1,0:T(8,128)(2,1)S(1)}, u32[]{:S(2)}, u32[]{:S(2)}) async-start(bf16[256,16,128]{2,1,0:T(8,128)(2,1)} %bitcast.13), calls=%async_computation | async-start | bytes 2097152 | tf_op jit(solution)/shard_map/all_to_all | solution.py:596
  17.7 0.7 copy-start.1
  22.5 1.3 %copy-start.2 = (s32[8]{0:T(128)S(1)}, s32[8]{0:T(128)}, u32[]{:S(2)}) copy-start(s32[8]{0:T(128)} %lens_ref.1) | copy-start | bytes 100
  22.5 1.3 %copy-start.3 = (s32[32]{0:T(128)S(1)}, s32[32]{0:T(128)}, u32[]{:S(2)}) copy-start(s32[32]{0:T(128)} %param.19) | copy-start | bytes 388
  54.6 38.4 %all-to-all-start.1 = ((bf16[256,16,128]{2,1,0:T(8,128)(2,1)}), bf16[256,16,128]{2,1,0:T(8,128)(2,1)S(1)}, u32[]{:S(2)}, u32[]{:S(2)}) async-start(bf16[256,16,128]{2,1,0:T(8,128)(2,1)} %get-tuple-element.18), calls=%async_computation.1 | async-start | bytes 2097152 | tf_op jit(solution)/shard_map/all_to_all | solution.py:596
  60.8 4.9 %collective-permute-start.2 = (f32[1,4,128]{2,1,0:T(4,128)S(1)}, f32[1,4,128]{2,1,0:T(4,128)S(1)}, u32[]{:S(2)}, u32[]{:S(2)}) collective-permute-start(f32[1,4,128]{2,1,0:T(4,128)S(1)} %bitcast.9), channel_id=1, source_target_pairs={{0,192},{8,200},{16,208},{24,216},{32,224},{40,232},{48,240},{56,2... | collective-permute-start | bytes 6152 | tf_op jit(solution)/shard_map/ppermute | solution.py:605
  63.6 5.1 %collective-permute-start.1 = (f32[1,4,128]{2,1,0:T(4,128)S(1)}, f32[1,4,128]{2,1,0:T(4,128)S(1)}, u32[]{:S(2)}, u32[]{:S(2)}) collective-permute-start(f32[1,4,128]{2,1,0:T(4,128)S(1)} %bitcast.10), channel_id=1, source_target_pairs={{0,128},{8,136},{16,144},{24,152},{32,160},{40,168},{48,176},{56,1... | collective-permute-start | bytes 6152 | tf_op jit(solution)/shard_map/ppermute | solution.py:605
  64.4 4.2 %collective-permute-start = (f32[1,4,128]{2,1,0:T(4,128)S(1)}, f32[1,4,128]{2,1,0:T(4,128)S(1)}, u32[]{:S(2)}, u32[]{:S(2)}) collective-permute-start(f32[1,4,128]{2,1,0:T(4,128)S(1)} %bitcast.11), channel_id=1, source_target_pairs={{0,64},{8,72},{16,80},{24,88},{32,96},{40,104},{48,112},{56,120},{... | collective-permute-start | bytes 6152 | tf_op jit(solution)/shard_map/ppermute | solution.py:605
  68.7 16.5 %collective-permute-start.5 = (f32[4,4,128]{2,1,0:T(4,128)S(1)}, f32[4,4,128]{2,1,0:T(4,128)S(1)}, u32[]{:S(2)}, u32[]{:S(2)}) collective-permute-start(f32[4,4,128]{2,1,0:T(4,128)S(1)} %pad_maximum_fusion), channel_id=1, source_target_pairs={{0,24},{8,16},{16,8},{24,0},{32,56},{40,48},{48,40},{56,32},{64,88... | collective-permute-start | bytes 24584 | tf_op jit(solution)/shard_map/ppermute | solution.py:605
  72.8 11.8 %collective-permute-start.4 = (f32[4,4,128]{2,1,0:T(4,128)S(1)}, f32[4,4,128]{2,1,0:T(4,128)S(1)}, u32[]{:S(2)}, u32[]{:S(2)}) collective-permute-start(f32[4,4,128]{2,1,0:T(4,128)S(1)} %pad_maximum_fusion), channel_id=1, source_target_pairs={{0,16},{8,24},{16,0},{24,8},{32,48},{40,56},{48,32},{56,40},{64,80... | collective-permute-start | bytes 24584 | tf_op jit(solution)/shard_map/ppermute | solution.py:605
  72.8 11.7 %collective-permute-start.3 = (f32[4,4,128]{2,1,0:T(4,128)S(1)}, f32[4,4,128]{2,1,0:T(4,128)S(1)}, u32[]{:S(2)}, u32[]{:S(2)}) collective-permute-start(f32[4,4,128]{2,1,0:T(4,128)S(1)} %pad_maximum_fusion), channel_id=1, source_target_pairs={{0,8},{8,0},{16,24},{24,16},{32,40},{40,32},{48,56},{56,48},{64,72... | collective-permute-start | bytes 24584 | tf_op jit(solution)/shard_map/ppermute | solution.py:605
  85.2 7.8 %collective-permute-start.6 = (f32[16,4,128]{2,1,0:T(4,128)S(1)}, f32[16,4,128]{2,1,0:T(4,128)S(1)}, u32[]{:S(2)}, u32[]{:S(2)}) collective-permute-start(f32[16,4,128]{2,1,0:T(4,128)S(1)} %get-tuple-element.26), channel_id=1, source_target_pairs={{0,32},{8,40},{16,48},{24,56},{32,0},{40,8},{48,16},{56,24},{64,96... | collective-permute-start | bytes 98312 | tf_op jit(solution)/shard_map/ppermute | solution.py:605

commit v5 on v4

--- a/solution.py
+++ b/solution.py
@@ -18,7 +18,7 @@
 VROWS = BASE + NSEQ * 16
 PARTS = 4
 PART = 8192 // PARTS
-CHUNK = 8
+CHUNK = 4
 MASKS = 9 * NPIECES
 PLAN_ROWS = MASKS + 3 * 96 + OWN
 T_AHEAD, T_BACK, C_AHEAD, C_BACK, E_BOTH = 0, 512, 1024, 1152, 1280
@@ -308,26 +308,22 @@
     def unplace(pos):
         return pl.ds(pl.multiple_of(lax.rem(pos + 4 - turn, 4) * OWN, OWN), OWN)
 
-    xt_ref[NPIECES] = jnp.zeros((PIECE, PIECE), F32)
+    begins = begins_of(lens_ref)
+
+    def invert(s, carry):
+        inv_ref[meta_ref[NSEQ + s]] = s
+        return carry
+
+    lax.fori_loop(0, NPIECES, invert, 0, unroll=4)
     gs_ref[NPIECES] = jnp.zeros((96, PIECE), F32)
     acc_ref[...] = jnp.zeros(acc_ref.shape, F32)
-
-    def turn_in(s, carry):
-        tile = x_ref[pl.ds(s * 8, 8)].reshape(PIECE, PIECE)
+    blank = jnp.zeros((OWN, PIECE), F32)
+
+    def turn_in(p):
+        tile = x_ref[pl.ds(inv_ref[p] * 8, 8)].reshape(PIECE, PIECE)
         tile = tile.T.astype(F32)
         for pos in range(4):
-            xt_ref[s, unplace(pos), :] = tile[pos * OWN : (pos + 1) * OWN]
-        return carry
-
-    unrolled(NPIECES, turn_in, 0)
-    begins = begins_of(lens_ref)
-    inv_ref[0] = NPIECES
-
-    def invert(s, carry):
-        inv_ref[meta_ref[NSEQ + s] + 1] = s
-        return carry
-
-    lax.fori_loop(0, NPIECES, invert, 0, unroll=4)
+            xt_ref[p, unplace(pos), :] = tile[pos * OWN : (pos + 1) * OWN]
 
     lane = lane_ids((OWN, PIECE))
 
@@ -346,12 +342,13 @@
 
     def ahead(chunk, carry):
         pieces = range(chunk * CHUNK, (chunk + 1) * CHUNK)
-        slots = [inv_ref[p] for p in range(chunk * CHUNK, (chunk + 1) * CHUNK + 1)]
+        for p in pieces:
+            turn_in(p)
         for a in range(3):
             taps = [tap(j, a) for j in range(3)]
-            prior = xt_ref[slots[0], part(a), :]
-            for i, p in enumerate(pieces):
-                x = xt_ref[slots[i + 1], part(a), :]
+            prior = xt_ref[pieces[0] - 1, part(a), :] if chunk else blank
+            for p in pieces:
+                x = xt_ref[p, part(a), :]
                 x_one = pltpu.roll(jnp.where(lane == PIECE - 1, prior, x), 1, 1)
                 x_two = pltpu.roll(jnp.where(lane >= PIECE - 2, prior, x), 2, 1)
                 feat_ref[p, part(a), :] = (
@@ -361,9 +358,9 @@
                 )
                 prior = x
         skip = jnp.zeros((OWN, PIECE), F32)
-        for i, p in enumerate(pieces):
+        for p in pieces:
             z = feat_ref[p, part(1), :] * feat_ref[p, part(2), :]
-            gu = xt_ref[slots[i + 1], part(3), :] * feat_ref[p, part(0), :]
+            gu = xt_ref[p, part(3), :] * feat_ref[p, part(0), :]
             z_ref[p] = z
             gu_ref[p] = gu
             skip = skip + gu * z
@@ -446,12 +443,17 @@
         filtered = u + gain * z_ref[p]
         gz = gz + gain * gu_ref[p]
         ys_ref[p, place(0), :] = (feat_ref[p, part(0), :] * filtered).astype(BF16)
-        gs_ref[p, part(0), :] = xt_ref[inv_ref[p + 1], part(3), :] * filtered
+        gs_ref[p, part(0), :] = xt_ref[p, part(3), :] * filtered
         gs_ref[p, part(1), :] = gz * feat_ref[p, part(2), :]
         gs_ref[p, part(2), :] = gz * feat_ref[p, part(1), :]
         return carry
 
     unrolled(NPIECES, gradients, 0)
+
+    def send(p):
+        return pltpu.make_async_copy(
+            y_ref.at[pl.ds(p * 64, 64)], out_ref.at[pl.ds(p * 64, 64)], sem.at[p]
+        )
 
     def behind(chunk, carry):
         for a in range(3):
@@ -460,7 +462,7 @@
             after = gs_ref[(chunk + 1) * CHUNK, part(a), :]
             for p in reversed(range(chunk * CHUNK, (chunk + 1) * CHUNK)):
                 grad = gs_ref[p, part(a), :]
-                x = xt_ref[inv_ref[p + 1], part(a), :]
+                x = xt_ref[p, part(a), :]
                 g_one = pltpu.roll(jnp.where(lane == 0, after, grad), PIECE - 1, 1)
                 g_two = pltpu.roll(jnp.where(lane < 2, after, grad), PIECE - 2, 1)
                 g_one = mask(L_ONE, p) * g_one
@@ -475,27 +477,18 @@
         return carry
 
     unrolled(NPIECES // CHUNK, behind, 0)
-
-    def send(part):
-        rows = pl.ds(part * 64, 64)
-        return pltpu.make_async_copy(y_ref.at[rows], out_ref.at[rows], sem.at[part])
-
     for part in range(4):
-
-        def turn_out(i, carry):
-            s = part * 8 + i
+        for s in range(part * 8, part * 8 + 8):
             tile = ys_ref[meta_ref[NSEQ + s]].T
-            y_ref[pl.ds(s * 8, 8)] = tile.reshape(8, 16, PIECE)
-            return carry
-
-        unrolled(8, turn_out, 0)
+            y_ref[s * 8 : s * 8 + 8] = tile.reshape(8, 16, PIECE)
         send(part).start()
+
     norm = 1.0 / math.sqrt(TOKENS)
     g_ref[3:4, :] = jnp.zeros((1, PIECE), F32)
     for j in range(3):
         g_ref[j : j + 1, :] = norm * jnp.sum(acc_ref[j].T, axis=0, keepdims=True)
-    for part in range(4):
-        send(part).wait()
+    for p in range(4):
+        send(p).wait()
 
 
 VM = pl.BlockSpec(memory_space=pltpu.VMEM)
@@ -561,8 +554,8 @@
 
 def run_main(meta, blocks, plan, mats):
     scratch = [
-        pltpu.SMEM((NPIECES + 1,), jnp.int32),
-        pltpu.VMEM((NPIECES + 1, PIECE, PIECE), F32),
+        pltpu.SMEM((NPIECES,), jnp.int32),
+        pltpu.VMEM((NPIECES, PIECE, PIECE), F32),
         pltpu.VMEM((NPIECES, 96, PIECE), F32),
         pltpu.VMEM((NPIECES, OWN, PIECE), F32),
         pltpu.VMEM((NPIECES, OWN, PIECE), F32),
@@ -574,7 +567,7 @@
         pltpu.VMEM((VROWS, PIECE), F32),
         pltpu.VMEM((NPIECES + 1, 96, PIECE), F32),
         pltpu.VMEM((NPIECES, PIECE, PIECE), BF16),
-        pltpu.VMEM((256, 16, 128), BF16),
+        pltpu.VMEM((256, 16, PIECE), BF16),
         pltpu.VMEM((3, PIECE, PIECE), F32),
         pltpu.SemaphoreType.DMA((4,)),
     ]

time: 95 us -> 94.8 us (level)
  no operation moved by 1% of the time
where the time goes in v5:
time: 94.8 us; the launch traced here: 94.2 us
  waiting for transfers between devices  42.9 us (45%)
  starting transfers between devices  35.1 us (37%)
  Pallas kernels  11.7 us (12%)
  local copies, waits for them, and re-layouts  3.72 us (4%)
    all_to_all x2, waiting for transfers between devices, exchange(): return lax.all_to_all(blocks, BOTH, split_axis=0, concat_axis=0, tiled=True)  25 us
    all_to_all x2, starting transfers between devices, exchange(): return lax.all_to_all(blocks, BOTH, split_axis=0, concat_axis=0, tiled=True)  20.8 us
    ppermute x7, waiting for transfers between devices, gather_sums(): got.append(lax.ppermute(held, 'ctx', pairs))  17.9 us
    ppermute x7, starting transfers between devices, gather_sums(): got.append(lax.ppermute(held, 'ctx', pairs))  14.2 us
    pallas_call x1, Pallas kernels, run_main(): pl.pallas_call(main_kernel, out_shape=[jax.ShapeDtypeStruct((256, 16, 128...  5.44 us
    pallas_call x1, Pallas kernels, run_pack(): pl.pallas_call(pack_kernel, out_shape=jax.ShapeDtypeStruct((32, 8, 16, 12...  2.44 us
    pallas_call x1, Pallas kernels, run_prep(): pl.pallas_call(prep_kernel, out_shape=[jax.ShapeDtypeStruct(*shape) for s...  2.39 us
  transfers between devices with their start and end apart: 9, of which 7 were waited for; matrix products, arithmetic and copies ran while one was open for 4% of the time, Pallas kernels for 3%

profile of v5, /device:TPU:8, one launch (start us, length us, event | category | flops | bytes accessed | tf_op | source)
XLA Modules:
  0.0 94.2 jit_solution(8954532758014639640)
XLA Ops:
  0.6 2.4 %pack.1 = bf16[32,8,16,128]{3,2,1,0:T(8,128)(2,1)} custom-call(bf16[16,8192]{1,0:T(8,128)(2,1)} %a_ref.1, bf16[16,8192]{1,0:T(8,128)(2,1)} %b_ref.1, bf16[16,8192]{1,0:T(8,128)(2,1)} %c_ref.1, bf16[16,8192]{1,0:T(8,128)(2,1)} %d_ref.1), custom_call_target="tpu_custom_call" | custom-call | tf_op jit(solution)/shard_map/pack/pallas_call | solution.py:504
  3.1 0.0 copy-start
  3.1 14.6 %all-to-all-start = ((bf16[256,16,128]{2,1,0:T(8,128)(2,1)}), bf16[256,16,128]{2,1,0:T(8,128)(2,1)S(1)}, u32[]{:S(2)}, u32[]{:S(2)}) async-start(bf16[256,16,128]{2,1,0:T(8,128)(2,1)} %bitcast.13), calls=%async_computation | async-start | bytes 2097152 | tf_op jit(solution)/shard_map/all_to_all | solution.py:589
  17.7 0.0 copy-done
  17.7 0.0 copy-start.1
  17.7 0.7 copy.16.res_ref
  18.4 0.0 copy-done.1
  18.4 0.7 copy.17.pole_ref
  19.1 2.4 %prep.1 = (f32[608,128]{1,0:T(8,128)}, bf16[1792,256]{1,0:T(8,128)(2,1)}) custom-call(s32[8]{0:T(128)} %lens_ref.1, s32[1]{0:T(128)} %bitcast.here_ref, f32[3,3,1024]{2,1,0:T(4,128)} %taps_ref.1, f32[64,16]{1,0:T(8,128)} %copy.16.res_ref, f32[64,16]{1,0:T(8,128)} %copy.17.pole_ref, f32[1,1024]{1,0:T(1,128)} %bitcast.14), custom_call_target="tpu_custom_call" | custom-call | flops 4000000 | bytes 1048576 | tf_op jit(solution)/shard_map/prep/pallas_call | solution.py:544
  21.5 1.0 %pad.8.plan_ref = f32[616,128]{1,0:T(8,128)S(1)} pad(f32[608,128]{1,0:T(8,128)} %get-tuple-element.16, f32[]{:T(128)} %constant.9.clone.1), padding=0_8x0_0 | pad | bytes 626692 | tf_op jit(solution)/shard_map/jit(_pad)/pad | solution.py:625
  22.5 0.0 copy-start.2
  22.5 0.0 copy-start.3
  22.5 1.2 %pad.9.mats_ref = bf16[1808,256]{1,0:T(8,128)(2,1)S(1)} pad(bf16[1792,256]{1,0:T(8,128)(2,1)} %get-tuple-element.17, bf16[]{:T(256)} %constant.10.clone.1), padding=0_16x0_0 | pad | bytes 1843202 | tf_op jit(solution)/shard_map/jit(_pad)/pad | solution.py:626
  23.8 0.0 copy-done.2
  23.8 0.0 copy-done.3
  23.8 0.1 pad_add_fusion.meta_ref
  23.9 25.0 %all-to-all-done.x_ref = bf16[256,16,128]{2,1,0:T(8,128)(2,1)S(1)} async-done(((bf16[256,16,128]{2,1,0:T(8,128)(2,1)}), bf16[256,16,128]{2,1,0:T(8,128)(2,1)S(1)}, u32[]{:S(2)}, u32[]{:S(2)}) %all-to-all-start) | async-done | bytes 1048608 | tf_op jit(solution)/shard_map/all_to_all | solution.py:589
  48.9 5.4 %block.1 = (bf16[256,16,128]{2,1,0:T(8,128)(2,1)}, f32[4,128]{1,0:T(4,128)S(1)}) custom-call(s32[41]{0:T(128)S(1)} %pad_add_fusion.meta_ref, bf16[256,16,128]{2,1,0:T(8,128)(2,1)S(1)} %all-to-all-done.x_ref, f32[616,128]{1,0:T(8,128)S(1)} %pad.8.plan_ref, bf16[1808,256]{1,0:T(8,128)(2,1)S(1)} %pad.9.mats_ref), custom_call_target="tpu_custom_call" | custom-call | tf_op jit(solution)/shard_map/block/pallas_call | solution.py:574
  54.3 6.2 %all-to-all-start.1 = ((bf16[256,16,128]{2,1,0:T(8,128)(2,1)}), bf16[256,16,128]{2,1,0:T(8,128)(2,1)S(1)}, u32[]{:S(2)}, u32[]{:S(2)}) async-start(bf16[256,16,128]{2,1,0:T(8,128)(2,1)} %get-tuple-element.18), calls=%async_computation.1 | async-start | bytes 2097152 | tf_op jit(solution)/shard_map/all_to_all | solution.py:589
  60.6 2.8 %collective-permute-start.2 = (f32[1,4,128]{2,1,0:T(4,128)S(1)}, f32[1,4,128]{2,1,0:T(4,128)S(1)}, u32[]{:S(2)}, u32[]{:S(2)}) collective-permute-start(f32[1,4,128]{2,1,0:T(4,128)S(1)} %bitcast.9), channel_id=1, source_target_pairs={{0,192},{8,200},{16,208},{24,216},{32,224},{40,232},{48,240},{56,2... | collective-permute-start | bytes 6152 | tf_op jit(solution)/shard_map/ppermute | solution.py:598
  63.3 0.9 collective-permute-start.1
  64.2 0.6 collective-permute-start
  64.7 0.7 collective-permute-done.2
  65.4 3.0 %collective-permute-done.1 = f32[1,4,128]{2,1,0:T(4,128)S(1)} collective-permute-done((f32[1,4,128]{2,1,0:T(4,128)S(1)}, f32[1,4,128]{2,1,0:T(4,128)S(1)}, u32[]{:S(2)}, u32[]{:S(2)}) %collective-permute-start.1) | collective-permute-done | bytes 2080 | tf_op jit(solution)/shard_map/ppermute | solution.py:598
  68.4 0.0 collective-permute-done
  68.4 4.1 %collective-permute-start.5 = (f32[4,4,128]{2,1,0:T(4,128)S(1)}, f32[4,4,128]{2,1,0:T(4,128)S(1)}, u32[]{:S(2)}, u32[]{:S(2)}) collective-permute-start(f32[4,4,128]{2,1,0:T(4,128)S(1)} %pad_maximum_fusion), channel_id=1, source_target_pairs={{0,24},{8,16},{16,8},{24,0},{32,56},{40,48},{48,40},{56,32},{64,88... | collective-permute-start | bytes 24584 | tf_op jit(solution)/shard_map/ppermute | solution.py:598
  72.5 0.0 collective-permute-start.4
  72.5 0.7 collective-permute-start.3
  73.2 11.1 %collective-permute-done.3 = f32[4,4,128]{2,1,0:T(4,128)S(1)} collective-permute-done((f32[4,4,128]{2,1,0:T(4,128)S(1)}, f32[4,4,128]{2,1,0:T(4,128)S(1)}, u32[]{:S(2)}, u32[]{:S(2)}) %collective-permute-start.3) | collective-permute-done | bytes 8224 | tf_op jit(solution)/shard_map/ppermute | solution.py:598
  84.3 0.1 collective-permute-done.4
  84.4 0.5 collective-permute-done.5
  84.9 5.3 %collective-permute-start.6 = (f32[16,4,128]{2,1,0:T(4,128)S(1)}, f32[16,4,128]{2,1,0:T(4,128)S(1)}, u32[]{:S(2)}, u32[]{:S(2)}) collective-permute-start(f32[16,4,128]{2,1,0:T(4,128)S(1)} %get-tuple-element.26), channel_id=1, source_target_pairs={{0,32},{8,40},{16,48},{24,56},{32,0},{40,8},{48,16},{56,24},{64,96... | collective-permute-start | bytes 98312 | tf_op jit(solution)/shard_map/ppermute | solution.py:598
  90.2 2.6 %collective-permute-done.6 = f32[16,4,128]{2,1,0:T(4,128)S(1)} collective-permute-done((f32[16,4,128]{2,1,0:T(4,128)S(1)}, f32[16,4,128]{2,1,0:T(4,128)S(1)}, u32[]{:S(2)}, u32[]{:S(2)}) %collective-permute-start.6) | collective-permute-done | bytes 32800 | tf_op jit(solution)/shard_map/ppermute | solution.py:598
  92.8 0.0 all-to-all-done.1
  92.8 1.4 %unpack.1 = (bf16[16,8192]{1,0:T(8,128)(2,1)}, bf16[16,8192]{1,0:T(8,128)(2,1)}, bf16[16,8192]{1,0:T(8,128)(2,1)}, bf16[16,8192]{1,0:T(8,128)(2,1)}, f32[3,3,1024]{2,1,0:T(4,128)}, /*index=5*/f32[1,1024]{1,0:T(1,128)}) custom-call(s32[1]{0:T(128)} %bitcast.here_ref, bf16[32,8,16,128]{3,2,1,0:T(8,128)(2,1)S(1)} %bitcast.8, ...), custom_call_target="tpu_custom_call" | custom-call | tf_op jit(solution)/shard_map/unpack/pallas_call | solution.py:521
  (9 shorter events, 0.1 us)
Async XLA Ops:
  3.1 14.6 %copy-start = (f32[64,16]{0,1:T(8,128)S(1)}, f32[64,16]{0,1:T(8,128)}, u32[]{:S(2)}) copy-start(f32[64,16]{0,1:T(8,128)} %param.15) | copy-start | bytes 12292
  3.1 45.8 %all-to-all-start = ((bf16[256,16,128]{2,1,0:T(8,128)(2,1)}), bf16[256,16,128]{2,1,0:T(8,128)(2,1)S(1)}, u32[]{:S(2)}, u32[]{:S(2)}) async-start(bf16[256,16,128]{2,1,0:T(8,128)(2,1)} %bitcast.13), calls=%async_computation | async-start | bytes 2097152 | tf_op jit(solution)/shard_map/all_to_all | solution.py:589
  17.7 0.7 copy-start.1
  22.5 1.3 %copy-start.2 = (s32[8]{0:T(128)S(1)}, s32[8]{0:T(128)}, u32[]{:S(2)}) copy-start(s32[8]{0:T(128)} %lens_ref.1) | copy-start | bytes 100
  22.5 1.3 %copy-start.3 = (s32[32]{0:T(128)S(1)}, s32[32]{0:T(128)}, u32[]{:S(2)}) copy-start(s32[32]{0:T(128)} %param.19) | copy-start | bytes 388
  54.3 38.4 %all-to-all-start.1 = ((bf16[256,16,128]{2,1,0:T(8,128)(2,1)}), bf16[256,16,128]{2,1,0:T(8,128)(2,1)S(1)}, u32[]{:S(2)}, u32[]{:S(2)}) async-start(bf16[256,16,128]{2,1,0:T(8,128)(2,1)} %get-tuple-element.18), calls=%async_computation.1 | async-start | bytes 2097152 | tf_op jit(solution)/shard_map/all_to_all | solution.py:589
  60.6 4.9 %collective-permute-start.2 = (f32[1,4,128]{2,1,0:T(4,128)S(1)}, f32[1,4,128]{2,1,0:T(4,128)S(1)}, u32[]{:S(2)}, u32[]{:S(2)}) collective-permute-start(f32[1,4,128]{2,1,0:T(4,128)S(1)} %bitcast.9), channel_id=1, source_target_pairs={{0,192},{8,200},{16,208},{24,216},{32,224},{40,232},{48,240},{56,2... | collective-permute-start | bytes 6152 | tf_op jit(solution)/shard_map/ppermute | solution.py:598
  63.3 5.1 %collective-permute-start.1 = (f32[1,4,128]{2,1,0:T(4,128)S(1)}, f32[1,4,128]{2,1,0:T(4,128)S(1)}, u32[]{:S(2)}, u32[]{:S(2)}) collective-permute-start(f32[1,4,128]{2,1,0:T(4,128)S(1)} %bitcast.10), channel_id=1, source_target_pairs={{0,128},{8,136},{16,144},{24,152},{32,160},{40,168},{48,176},{56,1... | collective-permute-start | bytes 6152 | tf_op jit(solution)/shard_map/ppermute | solution.py:598
  64.2 4.2 %collective-permute-start = (f32[1,4,128]{2,1,0:T(4,128)S(1)}, f32[1,4,128]{2,1,0:T(4,128)S(1)}, u32[]{:S(2)}, u32[]{:S(2)}) collective-permute-start(f32[1,4,128]{2,1,0:T(4,128)S(1)} %bitcast.11), channel_id=1, source_target_pairs={{0,64},{8,72},{16,80},{24,88},{32,96},{40,104},{48,112},{56,120},{... | collective-permute-start | bytes 6152 | tf_op jit(solution)/shard_map/ppermute | solution.py:598
  68.4 16.5 %collective-permute-start.5 = (f32[4,4,128]{2,1,0:T(4,128)S(1)}, f32[4,4,128]{2,1,0:T(4,128)S(1)}, u32[]{:S(2)}, u32[]{:S(2)}) collective-permute-start(f32[4,4,128]{2,1,0:T(4,128)S(1)} %pad_maximum_fusion), channel_id=1, source_target_pairs={{0,24},{8,16},{16,8},{24,0},{32,56},{40,48},{48,40},{56,32},{64,88... | collective-permute-start | bytes 24584 | tf_op jit(solution)/shard_map/ppermute | solution.py:598
  72.5 11.8 %collective-permute-start.4 = (f32[4,4,128]{2,1,0:T(4,128)S(1)}, f32[4,4,128]{2,1,0:T(4,128)S(1)}, u32[]{:S(2)}, u32[]{:S(2)}) collective-permute-start(f32[4,4,128]{2,1,0:T(4,128)S(1)} %pad_maximum_fusion), channel_id=1, source_target_pairs={{0,16},{8,24},{16,0},{24,8},{32,48},{40,56},{48,32},{56,40},{64,80... | collective-permute-start | bytes 24584 | tf_op jit(solution)/shard_map/ppermute | solution.py:598
  72.5 11.7 %collective-permute-start.3 = (f32[4,4,128]{2,1,0:T(4,128)S(1)}, f32[4,4,128]{2,1,0:T(4,128)S(1)}, u32[]{:S(2)}, u32[]{:S(2)}) collective-permute-start(f32[4,4,128]{2,1,0:T(4,128)S(1)} %pad_maximum_fusion), channel_id=1, source_target_pairs={{0,8},{8,0},{16,24},{24,16},{32,40},{40,32},{48,56},{56,48},{64,72... | collective-permute-start | bytes 24584 | tf_op jit(solution)/shard_map/ppermute | solution.py:598
  84.9 7.8 %collective-permute-start.6 = (f32[16,4,128]{2,1,0:T(4,128)S(1)}, f32[16,4,128]{2,1,0:T(4,128)S(1)}, u32[]{:S(2)}, u32[]{:S(2)}) collective-permute-start(f32[16,4,128]{2,1,0:T(4,128)S(1)} %get-tuple-element.26), channel_id=1, source_target_pairs={{0,32},{8,40},{16,48},{24,56},{32,0},{40,8},{48,16},{56,24},{64,96... | collective-permute-start | bytes 98312 | tf_op jit(solution)/shard_map/ppermute | solution.py:598

commit v6 on v5

--- a/solution.py
+++ b/solution.py
@@ -340,6 +340,14 @@
     def mats(top, depth, cols=slice(0, 256)):
         return mats_ref[top : top + depth, cols], mats_ref[top + depth : top + 2 * depth, cols]
 
+    def products(rows):
+        z_part = lzf_ref[0, rows, :], lzf_ref[1, rows, :]
+        g_part = lgt_ref[0, rows, :], lgt_ref[1, rows, :]
+        e_ref[rows, :] = dot3(z_part, mats(E_BOTH, 256, slice(0, PIECE)))
+        h_ref[rows, :] = dot3(g_part, mats(E_BOTH, 256, slice(PIECE, 256)))
+        u_ref[rows, :] = dot3(z_part, mats(T_AHEAD, 256))
+        gz_ref[rows, :] = dot3(g_part, mats(T_BACK, 256))
+
     def ahead(chunk, carry):
         pieces = range(chunk * CHUNK, (chunk + 1) * CHUNK)
         for p in pieces:
@@ -367,6 +375,9 @@
             store_lhs(lzf_ref, p * 16, z * mask(FIRST, p))
             store_lhs(lgt_ref, p * 16, gu * mask(TAIL, p))
         acc_ref[0, part(3), :] += skip
+        if chunk * CHUNK % 16 == 16 - CHUNK:
+            top = (chunk + 1) * CHUNK * 16
+            products(slice(top - 256, top))
         return carry
 
     unrolled(NPIECES // CHUNK, ahead, 0)
@@ -391,8 +402,7 @@
     def both(ref):
         return ref[0], ref[1]
 
-    e_ref[...] = dot3(both(lzf_ref), mats(E_BOTH, 256, slice(0, PIECE)))
-    h_ref[...] = dot3(both(lgt_ref), mats(E_BOTH, 256, slice(PIECE, 256)))
+    products(slice(BASE, VROWS))
     for ref, ks in ((e_ref, range(NSEQ - 1)), (h_ref, range(NSEQ - 2, -1, -1))):
         for k in ks:
             p, _, _, inner = extras[k]
@@ -424,8 +434,6 @@
         low = (lane >= 32) & (lane < 64)
         return jnp.where(low, states - high, high).astype(BF16)
 
-    u_ref[...] = dot3(both(lzf_ref), mats(T_AHEAD, 256))
-    gz_ref[...] = dot3(both(lgt_ref), mats(T_BACK, 256))
     u_ref[0:BASE, :] += jnp.dot(three(e_ref[0:BASE, :]), mats_ref[C_AHEAD : C_AHEAD + PIECE, :], preferred_element_type=F32)
     gz_ref[0:BASE, :] += jnp.dot(three(h_ref[0:BASE, :]), mats_ref[C_BACK : C_BACK + PIECE, :], preferred_element_type=F32)
     for k, (p, later, sooner, _) in enumerate(extras):

time: 94.8 us -> 94.7 us (level)
  no operation moved by 1% of the time
where the time goes in v6:
time: 94.7 us; the launch traced here: 94.1 us
  waiting for transfers between devices  42.9 us (45%)
  starting transfers between devices  35.1 us (37%)
  Pallas kernels  11.6 us (12%)
  local copies, waits for them, and re-layouts  3.72 us (4%)
    all_to_all x2, waiting for transfers between devices, exchange(): return lax.all_to_all(blocks, BOTH, split_axis=0, concat_axis=0, tiled=True)  25 us
    all_to_all x2, starting transfers between devices, exchange(): return lax.all_to_all(blocks, BOTH, split_axis=0, concat_axis=0, tiled=True)  20.8 us
    ppermute x7, waiting for transfers between devices, gather_sums(): got.append(lax.ppermute(held, 'ctx', pairs))  17.9 us
    ppermute x7, starting transfers between devices, gather_sums(): got.append(lax.ppermute(held, 'ctx', pairs))  14.2 us
    pallas_call x1, Pallas kernels, run_main(): pl.pallas_call(main_kernel, out_shape=[jax.ShapeDtypeStruct((256, 16, 128...  5.38 us
    pallas_call x1, Pallas kernels, run_pack(): pl.pallas_call(pack_kernel, out_shape=jax.ShapeDtypeStruct((32, 8, 16, 12...  2.44 us
    pallas_call x1, Pallas kernels, run_prep(): pl.pallas_call(prep_kernel, out_shape=[jax.ShapeDtypeStruct(*shape) for s...  2.39 us
  transfers between devices with their start and end apart: 9, of which 7 were waited for; matrix products, arithmetic and copies ran while one was open for 4% of the time, Pallas kernels for 3%

profile of v6, /device:TPU:8, one launch (start us, length us, event | category | flops | bytes accessed | tf_op | source)
XLA Modules:
  0.0 94.1 jit_solution(8884639319873256391)
XLA Ops:
  0.6 2.4 %pack.1 = bf16[32,8,16,128]{3,2,1,0:T(8,128)(2,1)} custom-call(bf16[16,8192]{1,0:T(8,128)(2,1)} %a_ref.1, bf16[16,8192]{1,0:T(8,128)(2,1)} %b_ref.1, bf16[16,8192]{1,0:T(8,128)(2,1)} %c_ref.1, bf16[16,8192]{1,0:T(8,128)(2,1)} %d_ref.1), custom_call_target="tpu_custom_call" | custom-call | tf_op jit(solution)/shard_map/pack/pallas_call | solution.py:512
  3.1 0.0 copy-start
  3.1 14.6 %all-to-all-start = ((bf16[256,16,128]{2,1,0:T(8,128)(2,1)}), bf16[256,16,128]{2,1,0:T(8,128)(2,1)S(1)}, u32[]{:S(2)}, u32[]{:S(2)}) async-start(bf16[256,16,128]{2,1,0:T(8,128)(2,1)} %bitcast.13), calls=%async_computation | async-start | bytes 2097152 | tf_op jit(solution)/shard_map/all_to_all | solution.py:597
  17.7 0.0 copy-done
  17.7 0.0 copy-start.1
  17.7 0.7 copy.16.res_ref
  18.4 0.0 copy-done.1
  18.4 0.7 copy.17.pole_ref
  19.1 2.4 %prep.1 = (f32[608,128]{1,0:T(8,128)}, bf16[1792,256]{1,0:T(8,128)(2,1)}) custom-call(s32[8]{0:T(128)} %lens_ref.1, s32[1]{0:T(128)} %bitcast.here_ref, f32[3,3,1024]{2,1,0:T(4,128)} %taps_ref.1, f32[64,16]{1,0:T(8,128)} %copy.16.res_ref, f32[64,16]{1,0:T(8,128)} %copy.17.pole_ref, f32[1,1024]{1,0:T(1,128)} %bitcast.14), custom_call_target="tpu_custom_call" | custom-call | flops 4000000 | bytes 1048576 | tf_op jit(solution)/shard_map/prep/pallas_call | solution.py:552
  21.5 1.0 %pad.8.plan_ref = f32[616,128]{1,0:T(8,128)S(1)} pad(f32[608,128]{1,0:T(8,128)} %get-tuple-element.16, f32[]{:T(128)} %constant.9.clone.1), padding=0_8x0_0 | pad | bytes 626692 | tf_op jit(solution)/shard_map/jit(_pad)/pad | solution.py:633
  22.5 0.0 copy-start.2
  22.5 0.0 copy-start.3
  22.5 1.2 %pad.9.mats_ref = bf16[1808,256]{1,0:T(8,128)(2,1)S(1)} pad(bf16[1792,256]{1,0:T(8,128)(2,1)} %get-tuple-element.17, bf16[]{:T(256)} %constant.10.clone.1), padding=0_16x0_0 | pad | bytes 1843202 | tf_op jit(solution)/shard_map/jit(_pad)/pad | solution.py:634
  23.8 0.0 copy-done.2
  23.8 0.0 copy-done.3
  23.8 0.1 pad_add_fusion.meta_ref
  23.9 25.0 %all-to-all-done.x_ref = bf16[256,16,128]{2,1,0:T(8,128)(2,1)S(1)} async-done(((bf16[256,16,128]{2,1,0:T(8,128)(2,1)}), bf16[256,16,128]{2,1,0:T(8,128)(2,1)S(1)}, u32[]{:S(2)}, u32[]{:S(2)}) %all-to-all-start) | async-done | bytes 1048608 | tf_op jit(solution)/shard_map/all_to_all | solution.py:597
  48.9 5.4 %block.1 = (bf16[256,16,128]{2,1,0:T(8,128)(2,1)}, f32[4,128]{1,0:T(4,128)S(1)}) custom-call(s32[41]{0:T(128)S(1)} %pad_add_fusion.meta_ref, bf16[256,16,128]{2,1,0:T(8,128)(2,1)S(1)} %all-to-all-done.x_ref, f32[616,128]{1,0:T(8,128)S(1)} %pad.8.plan_ref, bf16[1808,256]{1,0:T(8,128)(2,1)S(1)} %pad.9.mats_ref), custom_call_target="tpu_custom_call" | custom-call | tf_op jit(solution)/shard_map/block/pallas_call | solution.py:582
  54.3 6.2 %all-to-all-start.1 = ((bf16[256,16,128]{2,1,0:T(8,128)(2,1)}), bf16[256,16,128]{2,1,0:T(8,128)(2,1)S(1)}, u32[]{:S(2)}, u32[]{:S(2)}) async-start(bf16[256,16,128]{2,1,0:T(8,128)(2,1)} %get-tuple-element.18), calls=%async_computation.1 | async-start | bytes 2097152 | tf_op jit(solution)/shard_map/all_to_all | solution.py:597
  60.5 2.8 %collective-permute-start.2 = (f32[1,4,128]{2,1,0:T(4,128)S(1)}, f32[1,4,128]{2,1,0:T(4,128)S(1)}, u32[]{:S(2)}, u32[]{:S(2)}) collective-permute-start(f32[1,4,128]{2,1,0:T(4,128)S(1)} %bitcast.9), channel_id=1, source_target_pairs={{0,192},{8,200},{16,208},{24,216},{32,224},{40,232},{48,240},{56,2... | collective-permute-start | bytes 6152 | tf_op jit(solution)/shard_map/ppermute | solution.py:606
  63.3 0.9 collective-permute-start.1
  64.1 0.6 collective-permute-start
  64.7 0.7 collective-permute-done.2
  65.4 3.0 %collective-permute-done.1 = f32[1,4,128]{2,1,0:T(4,128)S(1)} collective-permute-done((f32[1,4,128]{2,1,0:T(4,128)S(1)}, f32[1,4,128]{2,1,0:T(4,128)S(1)}, u32[]{:S(2)}, u32[]{:S(2)}) %collective-permute-start.1) | collective-permute-done | bytes 2080 | tf_op jit(solution)/shard_map/ppermute | solution.py:606
  68.4 0.0 collective-permute-done
  68.4 4.1 %collective-permute-start.5 = (f32[4,4,128]{2,1,0:T(4,128)S(1)}, f32[4,4,128]{2,1,0:T(4,128)S(1)}, u32[]{:S(2)}, u32[]{:S(2)}) collective-permute-start(f32[4,4,128]{2,1,0:T(4,128)S(1)} %pad_maximum_fusion), channel_id=1, source_target_pairs={{0,24},{8,16},{16,8},{24,0},{32,56},{40,48},{48,40},{56,32},{64,88... | collective-permute-start | bytes 24584 | tf_op jit(solution)/shard_map/ppermute | solution.py:606
  72.5 0.0 collective-permute-start.4
  72.5 0.7 collective-permute-start.3
  73.2 11.1 %collective-permute-done.3 = f32[4,4,128]{2,1,0:T(4,128)S(1)} collective-permute-done((f32[4,4,128]{2,1,0:T(4,128)S(1)}, f32[4,4,128]{2,1,0:T(4,128)S(1)}, u32[]{:S(2)}, u32[]{:S(2)}) %collective-permute-start.3) | collective-permute-done | bytes 8224 | tf_op jit(solution)/shard_map/ppermute | solution.py:606
  84.3 0.1 collective-permute-done.4
  84.3 0.5 collective-permute-done.5
  84.9 5.3 %collective-permute-start.6 = (f32[16,4,128]{2,1,0:T(4,128)S(1)}, f32[16,4,128]{2,1,0:T(4,128)S(1)}, u32[]{:S(2)}, u32[]{:S(2)}) collective-permute-start(f32[16,4,128]{2,1,0:T(4,128)S(1)} %get-tuple-element.26), channel_id=1, source_target_pairs={{0,32},{8,40},{16,48},{24,56},{32,0},{40,8},{48,16},{56,24},{64,96... | collective-permute-start | bytes 98312 | tf_op jit(solution)/shard_map/ppermute | solution.py:606
  90.1 2.6 %collective-permute-done.6 = f32[16,4,128]{2,1,0:T(4,128)S(1)} collective-permute-done((f32[16,4,128]{2,1,0:T(4,128)S(1)}, f32[16,4,128]{2,1,0:T(4,128)S(1)}, u32[]{:S(2)}, u32[]{:S(2)}) %collective-permute-start.6) | collective-permute-done | bytes 32800 | tf_op jit(solution)/shard_map/ppermute | solution.py:606
  92.7 0.0 all-to-all-done.1
  92.7 1.4 %unpack.1 = (bf16[16,8192]{1,0:T(8,128)(2,1)}, bf16[16,8192]{1,0:T(8,128)(2,1)}, bf16[16,8192]{1,0:T(8,128)(2,1)}, bf16[16,8192]{1,0:T(8,128)(2,1)}, f32[3,3,1024]{2,1,0:T(4,128)}, /*index=5*/f32[1,1024]{1,0:T(1,128)}) custom-call(s32[1]{0:T(128)} %bitcast.here_ref, bf16[32,8,16,128]{3,2,1,0:T(8,128)(2,1)S(1)} %bitcast.8, ...), custom_call_target="tpu_custom_call" | custom-call | tf_op jit(solution)/shard_map/unpack/pallas_call | solution.py:529
  (9 shorter events, 0.1 us)
Async XLA Ops:
  3.1 14.6 %copy-start = (f32[64,16]{0,1:T(8,128)S(1)}, f32[64,16]{0,1:T(8,128)}, u32[]{:S(2)}) copy-start(f32[64,16]{0,1:T(8,128)} %param.15) | copy-start | bytes 12292
  3.1 45.8 %all-to-all-start = ((bf16[256,16,128]{2,1,0:T(8,128)(2,1)}), bf16[256,16,128]{2,1,0:T(8,128)(2,1)S(1)}, u32[]{:S(2)}, u32[]{:S(2)}) async-start(bf16[256,16,128]{2,1,0:T(8,128)(2,1)} %bitcast.13), calls=%async_computation | async-start | bytes 2097152 | tf_op jit(solution)/shard_map/all_to_all | solution.py:597
  17.7 0.7 copy-start.1
  22.5 1.3 %copy-start.2 = (s32[8]{0:T(128)S(1)}, s32[8]{0:T(128)}, u32[]{:S(2)}) copy-start(s32[8]{0:T(128)} %lens_ref.1) | copy-start | bytes 100
  22.5 1.3 %copy-start.3 = (s32[32]{0:T(128)S(1)}, s32[32]{0:T(128)}, u32[]{:S(2)}) copy-start(s32[32]{0:T(128)} %param.19) | copy-start | bytes 388
  54.3 38.4 %all-to-all-start.1 = ((bf16[256,16,128]{2,1,0:T(8,128)(2,1)}), bf16[256,16,128]{2,1,0:T(8,128)(2,1)S(1)}, u32[]{:S(2)}, u32[]{:S(2)}) async-start(bf16[256,16,128]{2,1,0:T(8,128)(2,1)} %get-tuple-element.18), calls=%async_computation.1 | async-start | bytes 2097152 | tf_op jit(solution)/shard_map/all_to_all | solution.py:597
  60.5 4.9 %collective-permute-start.2 = (f32[1,4,128]{2,1,0:T(4,128)S(1)}, f32[1,4,128]{2,1,0:T(4,128)S(1)}, u32[]{:S(2)}, u32[]{:S(2)}) collective-permute-start(f32[1,4,128]{2,1,0:T(4,128)S(1)} %bitcast.9), channel_id=1, source_target_pairs={{0,192},{8,200},{16,208},{24,216},{32,224},{40,232},{48,240},{56,2... | collective-permute-start | bytes 6152 | tf_op jit(solution)/shard_map/ppermute | solution.py:606
  63.3 5.1 %collective-permute-start.1 = (f32[1,4,128]{2,1,0:T(4,128)S(1)}, f32[1,4,128]{2,1,0:T(4,128)S(1)}, u32[]{:S(2)}, u32[]{:S(2)}) collective-permute-start(f32[1,4,128]{2,1,0:T(4,128)S(1)} %bitcast.10), channel_id=1, source_target_pairs={{0,128},{8,136},{16,144},{24,152},{32,160},{40,168},{48,176},{56,1... | collective-permute-start | bytes 6152 | tf_op jit(solution)/shard_map/ppermute | solution.py:606
  64.1 4.2 %collective-permute-start = (f32[1,4,128]{2,1,0:T(4,128)S(1)}, f32[1,4,128]{2,1,0:T(4,128)S(1)}, u32[]{:S(2)}, u32[]{:S(2)}) collective-permute-start(f32[1,4,128]{2,1,0:T(4,128)S(1)} %bitcast.11), channel_id=1, source_target_pairs={{0,64},{8,72},{16,80},{24,88},{32,96},{40,104},{48,112},{56,120},{... | collective-permute-start | bytes 6152 | tf_op jit(solution)/shard_map/ppermute | solution.py:606
  68.4 16.5 %collective-permute-start.5 = (f32[4,4,128]{2,1,0:T(4,128)S(1)}, f32[4,4,128]{2,1,0:T(4,128)S(1)}, u32[]{:S(2)}, u32[]{:S(2)}) collective-permute-start(f32[4,4,128]{2,1,0:T(4,128)S(1)} %pad_maximum_fusion), channel_id=1, source_target_pairs={{0,24},{8,16},{16,8},{24,0},{32,56},{40,48},{48,40},{56,32},{64,88... | collective-permute-start | bytes 24584 | tf_op jit(solution)/shard_map/ppermute | solution.py:606
  72.5 11.8 %collective-permute-start.4 = (f32[4,4,128]{2,1,0:T(4,128)S(1)}, f32[4,4,128]{2,1,0:T(4,128)S(1)}, u32[]{:S(2)}, u32[]{:S(2)}) collective-permute-start(f32[4,4,128]{2,1,0:T(4,128)S(1)} %pad_maximum_fusion), channel_id=1, source_target_pairs={{0,16},{8,24},{16,0},{24,8},{32,48},{40,56},{48,32},{56,40},{64,80... | collective-permute-start | bytes 24584 | tf_op jit(solution)/shard_map/ppermute | solution.py:606
  72.5 11.7 %collective-permute-start.3 = (f32[4,4,128]{2,1,0:T(4,128)S(1)}, f32[4,4,128]{2,1,0:T(4,128)S(1)}, u32[]{:S(2)}, u32[]{:S(2)}) collective-permute-start(f32[4,4,128]{2,1,0:T(4,128)S(1)} %pad_maximum_fusion), channel_id=1, source_target_pairs={{0,8},{8,0},{16,24},{24,16},{32,40},{40,32},{48,56},{56,48},{64,72... | collective-permute-start | bytes 24584 | tf_op jit(solution)/shard_map/ppermute | solution.py:606
  84.9 7.8 %collective-permute-start.6 = (f32[16,4,128]{2,1,0:T(4,128)S(1)}, f32[16,4,128]{2,1,0:T(4,128)S(1)}, u32[]{:S(2)}, u32[]{:S(2)}) collective-permute-start(f32[16,4,128]{2,1,0:T(4,128)S(1)} %get-tuple-element.26), channel_id=1, source_target_pairs={{0,32},{8,40},{16,48},{24,56},{32,0},{40,8},{48,16},{56,24},{64,96... | collective-permute-start | bytes 98312 | tf_op jit(solution)/shard_map/ppermute | solution.py:606
